TPU v7x, 256 devices: a whole 4x4x8 slice. The times are simulated.
256 devices in a mesh: prow: 8 (over y, core), pcol: 32 (over z, x).
Axes of the slice: x: 4, y: 4, z: 8, core: 2. Of those that a mesh axis runs over, the one named last changes fastest.
Arguments:
- matrix: float32 [16384, 16384], P('prow', 'pcol'), may hold values from -6 to 6
- pivots: int32 [2, 256], replicated, may hold values from 0 to 16383, as said below
- lower_inverse: float32 [2, 256, 256], replicated, as said below
- upper_inverse: float32 [2, 256, 256], replicated, as said below
Outputs:
- factored: float32 [16384, 16384], P('prow', 'pcol')
Inputs may be any that keep to these rules, and one draw needn't show every extreme that they name: For panel k and position r, pivots[k, r] is either k * 256 + r or a row at or after (k + 1) * 256; the rows of the second kind are distinct within a panel. `lower_inverse`: unit lower triangular. `upper_inverse`: upper triangular with a positive diagonal.
All inputs are finite; a program needn't handle non-finite values.
Results may differ from a plain program's by a relative error of at most 0.00012.
Values sent between devices are 32-bit elements; how exact they have to be, the bound alone decides.
No kernel may reach another device: no remote copies, remote signals or barrier semaphores. Data moves between devices by JAX's collectives and lax.ppermute only.
A program may use at most 64 MiB of HBM per device.

v0:
```python
import jax
import jax.numpy as jnp
from jax import lax
from jax.sharding import PartitionSpec as P


def spread(value, axis, source):
    kept = jnp.where(lax.axis_index(axis) == source, value, 0).astype(value.dtype)
    return lax.psum(kept, axis)


def exact_dot(left, right):
    return jnp.dot(left, right, precision=lax.Precision.HIGHEST, preferred_element_type=jnp.float32)


def global_index(count, block_size, axis_size, axis_place):
    place = jnp.arange(count, dtype=jnp.int32)
    return (place // block_size * axis_size + axis_place) * block_size + place % block_size


def swap_rows(columns, panel_index, pivots, block_size):
    axis_size = lax.axis_size("prow")
    my_row = lax.axis_index("prow")
    local_rows = columns.shape[0]
    chosen_rows = pivots[panel_index]
    owner_row = chosen_rows // block_size % axis_size
    where_local = chosen_rows // block_size // axis_size * block_size + chosen_rows % block_size
    is_mine = owner_row == my_row
    first_row = panel_index // axis_size * block_size
    is_root = my_row == panel_index % axis_size
    current_top = columns[first_row : first_row + block_size]
    picked_rows = jnp.where(is_mine[:, None], columns[where_local], 0.0)
    offered_rows = jnp.where(is_root, current_top, 0.0)
    new_top, old_top = lax.psum((picked_rows, offered_rows), "prow")
    targets = jnp.where(is_mine, where_local, local_rows)
    columns = columns.at[targets].set(old_top, mode="drop")
    kept_rows = columns[first_row : first_row + block_size]
    columns = columns.at[first_row : first_row + block_size].set(
        jnp.where(is_root, new_top, kept_rows)
    )
    return (columns, new_top)


def broadcast_panel(columns, panel_index, inverse_block, row_ids, block_size):
    axis_size = lax.axis_size("pcol")
    slab_start = panel_index // axis_size * block_size
    panel_piece = columns[:, slab_start : slab_start + block_size]
    arrived = spread(panel_piece, "pcol", panel_index % axis_size)
    lower_part = exact_dot(arrived, inverse_block)
    return jnp.where((row_ids >= (panel_index + 1) * block_size)[:, None], lower_part, 0.0)


def upper_rows(new_top, inverse_block, col_ids, panel_index, block_size):
    is_root = lax.axis_index("prow") == panel_index % lax.axis_size("prow")
    product_rows = lax.cond(
        is_root, lambda: exact_dot(inverse_block, new_top), lambda: jnp.zeros_like(new_top)
    )
    product_rows = spread(product_rows, "prow", panel_index % lax.axis_size("prow"))
    return jnp.where((col_ids >= (panel_index + 1) * block_size)[None, :], product_rows, 0.0)


def apply_update(columns, col_ids, row_ids, lower_part, upper_part, panel_index, block_size):
    axis_size = lax.axis_size("prow")
    columns = columns - exact_dot(lower_part, upper_part)
    first_row = panel_index // axis_size * block_size
    is_root = lax.axis_index("prow") == panel_index % axis_size
    top_rows = columns[first_row : first_row + block_size]
    keep_upper = jnp.logical_and(is_root, col_ids >= (panel_index + 1) * block_size)
    columns = columns.at[first_row : first_row + block_size].set(
        jnp.where(keep_upper[None, :], upper_part, top_rows)
    )
    in_panel = jnp.logical_and(
        col_ids >= panel_index * block_size, col_ids < (panel_index + 1) * block_size
    )
    spread_lower = jnp.tile(lower_part, (1, columns.shape[1] // block_size))
    below_panel = row_ids >= (panel_index + 1) * block_size
    return jnp.where(
        jnp.logical_and(below_panel[:, None], in_panel[None, :]), spread_lower, columns
    )


def on_device(matrix, pivots, lower_inverse, upper_inverse):
    block_size = lower_inverse.shape[1]
    panels = lower_inverse.shape[0]
    row_ids = global_index(
        matrix.shape[0], block_size, lax.axis_size("prow"), lax.axis_index("prow")
    )
    col_ids = global_index(
        matrix.shape[1], block_size, lax.axis_size("pcol"), lax.axis_index("pcol")
    )
    current, new_top = swap_rows(matrix, 0, pivots, block_size)
    lower_part = broadcast_panel(current, 0, upper_inverse[0], row_ids, block_size)
    for panel_index in range(panels):
        upper_part = upper_rows(
            new_top, lower_inverse[panel_index], col_ids, panel_index, block_size
        )
        if panel_index + 1 < panels:
            current = apply_update(
                current, col_ids, row_ids, lower_part, upper_part, panel_index, block_size
            )
            current, new_top = swap_rows(current, panel_index + 1, pivots, block_size)
            following = broadcast_panel(
                current, panel_index + 1, upper_inverse[panel_index + 1], row_ids, block_size
            )
            lower_part = following
        else:
            current = apply_update(
                current, col_ids, row_ids, lower_part, upper_part, panel_index, block_size
            )
    return current


def solution(mesh):
    in_specs = (P("prow", "pcol"), P(), P(), P())
    out_specs = P("prow", "pcol")
    return jax.shard_map(
        on_device, mesh=mesh, in_specs=in_specs, out_specs=out_specs, check_vma=False
    )
```

profile of v0, /device:TPU:1, one launch (start us, length us, event | category | flops | bytes accessed | tf_op | source)
XLA Modules:
  0.0 650.2 jit_solution(4542272793898555124)
XLA Ops:
  6.5 4.7 copy.26
  11.3 3.4 gather_fusion
  14.7 0.9 broadcast_select_fusion.3
  15.7 0.0 all-reduce.9.cloned.1.call-update
  15.7 0.0 all-reduce.19.cloned.1.call-start
  15.8 1.9 slice_select_fusion.7
  17.6 65.9 %all-reduce.9.cloned.1.call-done = f32[256,512]{1,0:T(8,128)} async-done(((f32[256,512]{1,0:T(8,128)}), f32[256,512]{1,0:T(8,128)}) %all-reduce.9.cloned.1.call-update) | async-done | bytes 524304 | tf_op jit(solution)/shard_map/psum | solution.py:34
  83.5 0.1 conditional.2
  83.6 0.9 broadcast_select_fusion.2
  84.4 0.0 all-reduce.19.cloned.1.call-update
  84.5 0.0 all-reduce.11.cloned.1.call-start
  84.5 68.6 %all-reduce.19.cloned.1.call-done = (f32[256,512]{1,0:T(8,128)}, f32[256,512]{1,0:T(8,128)}) async-done(((f32[256,512]{1,0:T(8,128)}, f32[256,512]{1,0:T(8,128)}), (f32[256,512]{1,0:T(8,128)}, f32[256,512]{1,0:T(8,128)})) %all-reduce.19.cloned.1.call-update) | async-done | bytes 1048592 | tf_op jit(solution)/shard_map/psum | solution.py:34
  153.1 6.1 scatter_fusion
  159.3 2.0 fusion.9
  161.2 3.0 slice_select_fusion.1
  164.3 0.0 all-reduce.11.cloned.1.call-update
  164.3 0.0 all-reduce.13.cloned.1.call-start
  164.4 151.2 %all-reduce.11.cloned.1.call-done = f32[2048,256]{1,0:T(8,128)} async-done(((f32[2048,256]{1,0:T(8,128)}), f32[2048,256]{1,0:T(8,128)}) %all-reduce.11.cloned.1.call-update) | async-done | bytes 2097168 | tf_op jit(solution)/shard_map/psum | solution.py:9
  315.6 3.2 convolution_select_fusion.1
  318.9 1.5 tile.8
  320.4 0.4 copy.5
  320.8 1.7 copy-done
  322.6 0.1 copy-done.2
  322.7 3.5 convolution_subtract_fusion.1
  326.2 0.1 fusion.8
  326.4 2.3 and_select_fusion
  328.7 3.4 gather_fusion.1
  332.1 0.9 broadcast_select_fusion.1
  333.0 0.0 all-reduce.17.cloned.1.call-start
  333.1 1.9 slice_select_fusion.4
  335.0 63.5 %all-reduce.13.cloned.1.call-done = f32[256,512]{1,0:T(8,128)} async-done(((f32[256,512]{1,0:T(8,128)}), f32[256,512]{1,0:T(8,128)}) %all-reduce.13.cloned.1.call-update) | async-done | bytes 524304 | tf_op jit(solution)/shard_map/psum | solution.py:34
  398.5 1.7 conditional.3
  398.5 1.6 fusion.3
  400.1 0.9 broadcast_select_fusion
  401.0 0.2 all-reduce.15.cloned.1.call-start
  401.3 66.6 %all-reduce.17.cloned.1.call-done = (f32[256,512]{1,0:T(8,128)}, f32[256,512]{1,0:T(8,128)}) async-done(((f32[256,512]{1,0:T(8,128)}, f32[256,512]{1,0:T(8,128)}), (f32[256,512]{1,0:T(8,128)}, f32[256,512]{1,0:T(8,128)})) %all-reduce.17.cloned.1.call-update) | async-done | bytes 1048592 | tf_op jit(solution)/shard_map/psum | solution.py:34
  467.9 6.1 scatter_fusion.1
  474.1 1.9 fusion.7
  476.0 3.0 slice_select_fusion
  479.1 151.3 %all-reduce.15.cloned.1.call-done = f32[2048,256]{1,0:T(8,128)} async-done(((f32[2048,256]{1,0:T(8,128)}), f32[2048,256]{1,0:T(8,128)}) %all-reduce.15.cloned.1.call-update) | async-done | bytes 2097168 | tf_op jit(solution)/shard_map/psum | solution.py:9
  630.3 3.2 convolution_select_fusion
  633.6 1.5 tile.20
  635.1 0.4 copy.6
  635.6 1.7 copy-done.1
  637.3 0.1 copy-done.5
  637.4 3.5 convolution_subtract_fusion
  640.9 0.1 fusion.6
  641.1 2.3 and_select_fusion.1
  (34 shorter events, 0.3 us)
Async XLA Ops:
  6.5 4.7 copy-start.8
  6.5 77.0 %all-reduce.9.cloned.1.call-start = ((), (), s32[]{:S(2)}) async-start(), calls=%async_computation | async-start | bytes 1048576 | tf_op jit(solution)/shard_map/psum | solution.py:34
  11.2 72.3 %copy-start.6 = (f32[2,256,256]{2,1,0:T(8,128)S(1)}, f32[2,256,256]{2,1,0:T(8,128)}, u32[]{:S(2)}) copy-start(f32[2,256,256]{2,1,0:T(8,128)} %param.18) | copy-start | bytes 1572868
  15.7 137.4 %all-reduce.19.cloned.1.call-start = ((), (), s32[]{:S(2)}) async-start(), calls=%async_computation.5 | async-start | bytes 2097152 | tf_op jit(solution)/shard_map/psum | solution.py:34
  84.5 231.1 %all-reduce.11.cloned.1.call-start = ((), (), s32[]{:S(2)}) async-start(), calls=%async_computation.1 | async-start | bytes 4194304 | tf_op jit(solution)/shard_map/psum | solution.py:9
  153.1 6.1 copy-start.3
  159.3 156.4 %copy-start.7 = (f32[2,256,256]{2,1,0:T(8,128)S(1)}, f32[2,256,256]{2,1,0:T(8,128)}, u32[]{:S(2)}) copy-start(f32[2,256,256]{2,1,0:T(8,128)} %param.19) | copy-start | bytes 1572868
  164.3 234.2 %all-reduce.13.cloned.1.call-start = ((), (), s32[]{:S(2)}) async-start(), calls=%async_computation.2 | async-start | bytes 1048576 | tf_op jit(solution)/shard_map/psum | solution.py:34
  320.4 2.2 copy-start
  320.4 2.3 copy-start.2
  333.0 134.9 %all-reduce.17.cloned.1.call-start = ((), (), s32[]{:S(2)}) async-start(), calls=%async_computation.4 | async-start | bytes 2097152 | tf_op jit(solution)/shard_map/psum | solution.py:34
  401.0 229.3 %all-reduce.15.cloned.1.call-start = ((), (), s32[]{:S(2)}) async-start(), calls=%async_computation.3 | async-start | bytes 4194304 | tf_op jit(solution)/shard_map/psum | solution.py:9
  467.9 6.1 copy-start.4
  635.1 2.2 copy-start.1
  635.1 2.3 copy-start.5
Sparse Core Ops, SparseCore 0:
  15.8 67.6 all-reduce.8
  86.1 66.9 all-reduce.18
  164.4 151.1 all-reduce.10
  333.1 65.3 all-reduce.12
  401.1 66.7 all-reduce.16
  479.2 151.1 all-reduce.14
where the time goes:
time: 655 us; the launch traced here: 650 us
  waiting for transfers between devices  567 us (87%)
  local copies, waits for them, and re-layouts  31.4 us (5%)
  other arithmetic  22.4 us (3%)
  matrix products  15.2 us (2%)
  between operations  13.7 us (2%)
    psum x2, waiting for transfers between devices, spread(): return lax.psum(kept, axis)  302 us
    psum x4, waiting for transfers between devices, swap_rows(): new_top, old_top = lax.psum((picked_rows, offered_rows), 'prow')  265 us
    dot_general x5, matrix products, exact_dot(): jnp.dot(left, right, precision=lax.Precision.HIGHEST, preferred_element_t...  15.2 us
  transfers between devices with their start and end apart: 6, of which 6 were waited for; matrix products, arithmetic and copies ran while one was open for 1% of the time, Pallas kernels for 0%

commit v1 on v0

v1 whole, which is shorter than its diff:
```python
import jax
import jax.numpy as jnp
from jax import lax
from jax.sharding import PartitionSpec as P

NZ, NX, NY, NCORE = 8, 4, 4, 2


def dot(left, right, precision=lax.Precision.HIGHEST):
    return jnp.dot(left, right, precision=precision, preferred_element_type=jnp.float32)


def at(z, x):
    return z % NZ * NX + x % NX


def along_y(step):
    return [
        (y * NCORE + c, (y + step) % NY * NCORE + c) for y in range(NY) for c in range(NCORE)
    ]


def other_core():
    return [(y * NCORE + c, y * NCORE + 1 - c) for y in range(NY) for c in range(NCORE)]


def pick(index, options):
    value = options[0]
    for place in range(1, len(options)):
        value = jnp.where(index == place, options[place], value)
    return value


def down_z(z, pieces):
    arrived = [pieces[0]]
    for k in range(1, NZ):
        arrived.append(lax.ppermute(pieces[k], "pcol", [(at(0, 0), at(k, 0)), (at(0, 1), at(k, 1))]))
    return pick(z, arrived)


def across_x(x, mine):
    zs = range(NZ)
    plus = lax.ppermute(
        mine, "pcol", [(at(z, 0), at(z, 1)) for z in zs] + [(at(z, 1), at(z, 2)) for z in zs]
    )
    minus = lax.ppermute(
        mine, "pcol", [(at(z, 0), at(z, 3)) for z in zs] + [(at(z, 1), at(z, 0)) for z in zs]
    )
    twice = lax.ppermute(
        mine, "pcol", [(at(z, 0), at(z, 2)) for z in zs] + [(at(z, 1), at(z, 3)) for z in zs]
    )
    first = pick(x, [mine, plus, twice, minus])
    second = pick(x, [minus, mine, plus, twice])
    return jnp.concatenate([first, second], axis=1)


def gather_prow(y, core, mine):
    held = jnp.zeros((NY,) + mine.shape, mine.dtype)
    held = lax.dynamic_update_index_in_dim(held, mine, y, 0)
    for step in range(1, NY):
        got = lax.ppermute(mine, "prow", along_y(step))
        held = lax.dynamic_update_index_in_dim(held, got, (y - step) % NY, 0)
    others = lax.ppermute(held, "prow", other_core())
    return jnp.stack([jnp.where(core == 0, held, others), jnp.where(core == 0, others, held)])


def on_device(matrix, pivots, lower_inverse, upper_inverse):
    nb = lower_inverse.shape[1]
    rows = matrix.shape[0]
    n_prow = lax.axis_size("prow")
    p, q = lax.axis_index("prow"), lax.axis_index("pcol")
    y, core = p // NCORE, p % NCORE
    z, x = q // NX, q % NX
    share = 2 * nb // n_prow

    with jax.named_scope("panel_scatter"):
        piece = down_z(z, [matrix[nb * k : nb * (k + 1), :nb] for k in range(NZ)])
    with jax.named_scope("panel_across"):
        piece = across_x(x, piece)

    pivot0, pivot1 = pivots[0], pivots[1]
    order = jnp.arange(nb, dtype=jnp.int32)

    def before0(wanted):
        hit = wanted[:, None] == pivot0[None, :]
        found = jnp.sum(jnp.where(hit, order[None, :] + 1, 0), axis=1)
        return jnp.where(found > 0, found - 1, wanted)

    sources = jnp.concatenate([pivot0, before0(pivot1)])
    second_top = before0(nb + order)
    place = jnp.arange(rows, dtype=jnp.int32)
    row_ids = (place // nb * n_prow + p) * nb + place % nb
    hit1 = row_ids[:, None] == pivot1[None, :]
    hit0 = row_ids[:, None] == pivot0[None, :]
    from1 = jnp.sum(jnp.where(hit1, second_top[None, :] + 1, 0), axis=1)
    from0 = jnp.sum(jnp.where(hit0, order[None, :] + 1, 0), axis=1)
    below = row_ids >= 2 * nb
    origin = jnp.where(below, jnp.where(from1 > 0, from1, from0), 0) - 1
    kept_row = jnp.logical_and(below, origin < 0)

    with jax.named_scope("top_exchange"):
        mine = sources // nb % n_prow == p
        local = sources // nb // n_prow * nb + sources % nb
        chosen = jnp.where(mine[:, None], matrix[local], 0.0)
        sent = lax.dynamic_slice_in_dim(chosen, (1 - core) * nb, nb, 0)
        kept = lax.dynamic_slice_in_dim(chosen, core * nb, nb, 0)
        half = kept + lax.ppermute(sent, "prow", other_core())
        total = lax.dynamic_slice_in_dim(half, y * share, share, 0)
        olds = [matrix[:share]]
        for step in range(1, NY):
            to = (y + step) % NY * share
            packed = jnp.concatenate(
                [
                    lax.dynamic_slice_in_dim(half, to, share, 0),
                    lax.dynamic_slice_in_dim(matrix, to, share, 0),
                ]
            )
            got = lax.ppermute(packed, "prow", along_y(step))
            total = total + got[:share]
            olds.append(got[share:])
        slab = jnp.concatenate([total, pick(y, olds)])
    with jax.named_scope("top_gather"):
        tops = gather_prow(y, core, slab)
    with jax.named_scope("fix_down"):
        fix = down_z(z, [slab[:, :nb]] * NZ)
    with jax.named_scope("fix_across"):
        fix = across_x(x, fix)
    with jax.named_scope("fix_gather"):
        fix = gather_prow(y, core, fix)
    width = matrix.shape[1]
    top = tops[:, :, :share].reshape(2 * nb, width)
    old = tops[:, :, share:].reshape(2 * nb, width)
    top_panel = fix[:, :, :share].reshape(2 * nb, 2 * nb)
    old_panel = fix[:, :, share:].reshape(2 * nb, 2 * nb)

    with jax.named_scope("upper"):
        column = jnp.arange(width, dtype=jnp.int32)[None, :]
        in_first = jnp.logical_and(q == 0, column < nb)
        in_second = jnp.logical_and(q == 1, column < nb)
        keep = jnp.logical_not(jnp.logical_or(in_first, in_second))
        minus_one = jnp.where(
            lax.broadcasted_iota(jnp.int32, (nb, width), 0)
            == lax.broadcasted_iota(jnp.int32, (nb, width), 1),
            -1.0,
            0.0,
        ).astype(jnp.float32)
        upper0 = dot(lower_inverse[0], top[:nb])
        lower_top = dot(top_panel[nb:, :nb], upper_inverse[0])
        cross = dot(lower_inverse[0], top_panel[:nb, nb:])
        swapped1 = top[nb:] - dot(lower_top, upper0)
        upper1 = dot(lower_inverse[1], swapped1)
        use0 = jnp.where(in_first, minus_one, jnp.where(in_second, 0.0, upper0))
        use1 = jnp.where(in_second, minus_one, jnp.where(in_first, 0.0, upper1))
        solved1 = dot(upper_inverse[1], use1)
        solved0 = dot(upper_inverse[0], use0 - dot(cross, solved1))
        factor = jnp.concatenate([solved0, solved1])
        lower_wide = jnp.concatenate([lower_top] * (width // nb), axis=1)
        top0 = jnp.where(in_first, top[:nb], upper0)
        top1 = jnp.where(in_first, lower_wide, jnp.where(in_second, swapped1, upper1))

    with jax.named_scope("base"):
        moved = jnp.where(keep, old, 0.0) - dot(old_panel, factor)
        select = (origin[:, None] == jnp.arange(2 * nb, dtype=jnp.int32)[None, :]).astype(jnp.float32)
        base = jnp.where(jnp.logical_and(keep, kept_row[:, None]), matrix, 0.0) + dot(select, moved)
        head = jnp.where(p == 0, top0, jnp.where(p == 1, top1, base[:nb]))
        base = base.at[:nb].set(head)

    with jax.named_scope("panel_gather"):
        panel = lax.all_gather(
            piece,
            "pcol",
            axis_index_groups=[[at(k, j) for k in range(NZ)] for j in range(NX)],
            tiled=True,
        )
    with jax.named_scope("update"):
        product = dot(panel, factor, lax.Precision.HIGH)
        return base - jnp.where(kept_row[:, None], product, 0.0)


def solution(mesh):
    in_specs = (P("prow", "pcol"), P(), P(), P())
    out_specs = P("prow", "pcol")
    return jax.shard_map(
        on_device, mesh=mesh, in_specs=in_specs, out_specs=out_specs, check_vma=False
    )
```

time: 655 us -> 174 us (0.27)
  waiting for transfers between devices: 567 us -> 34.8 us
  starting transfers between devices: 0.39 us -> 66.4 us
  other arithmetic: 22.4 us -> 11.5 us
  matrix products: 15.2 us -> 22.8 us
  local copies, waits for them, and re-layouts: 31.4 us -> 24 us
    psum x6 -> x0, waiting for transfers between devices: 567 us -> none  [the longest x2 302 us: spread(): return lax.psum(kept, axis)]
    ppermute x0 -> x32, starting transfers between devices: none -> 66.4 us  [the longest x14 25.7 us: down_z(): lax.ppermute(pieces[k], 'pcol', [(at(0, 0), at(k, 0)), (at(0, 1), at(k, 1...]
    ppermute x0 -> x32, waiting for transfers between devices: none -> 34.8 us  [the longest x14 17.8 us: down_z(): lax.ppermute(pieces[k], 'pcol', [(at(0, 0), at(k, 0)), (at(0, 1), at(k, 1...]
    select_n x14 -> x8, other arithmetic: 18.1 us -> 1.56 us  [the longest x4 1.26 us: pick(): value = jnp.where(index == place, options[place], value)]
    scatter x2 -> x0, local copies, waits for them, and re-layouts: 12.3 us -> none  [swap_rows(): columns = columns.at[targets].set(old_top, mode='drop')]
    dot_general x5 -> x11, matrix products: 15.2 us -> 22.8 us  [dot(): jnp.dot(left, right, precision=precision, preferred_element_type=jnp.floa...]
  transfers between devices with their start and end apart: 6 -> 33, of which waited for: 6 -> 11; matrix products, arithmetic and copies ran while one was open for 1% -> 23% of each run, Pallas kernels for 0% -> 0%
where the time goes in v1:
time: 174 us
  starting transfers between devices  66.4 us (38%)
  waiting for transfers between devices  34.8 us (20%)
  local copies, waits for them, and re-layouts  24 us (14%)
  matrix products  22.8 us (13%)
  between operations  14.1 us (8%)
  other arithmetic  11.5 us (7%)
    ppermute x14, starting transfers between devices, down_z(): lax.ppermute(pieces[k], 'pcol', [(at(0, 0), at(k, 0)), (at(0, 1), at(k, 1...  25.7 us
    dot_general x11, matrix products, dot(): jnp.dot(left, right, precision=precision, preferred_element_type=jnp.floa...  22.8 us
    ppermute x14, waiting for transfers between devices, down_z(): lax.ppermute(pieces[k], 'pcol', [(at(0, 0), at(k, 0)), (at(0, 1), at(k, 1...  17.8 us
    ppermute x6, waiting for transfers between devices, gather_prow(): got = lax.ppermute(mine, 'prow', along_y(step))  13.3 us
    ppermute x2, starting transfers between devices, gather_prow(): others = lax.ppermute(held, 'prow', other_core())  10.9 us
    ppermute x6, starting transfers between devices, gather_prow(): got = lax.ppermute(mine, 'prow', along_y(step))  8.41 us
    ppermute x2, starting transfers between devices, across_x(): lax.ppermute(mine, 'pcol', [(at(z, 0), at(z, 1)) for z in zs] + [(at(z, 1...  7.79 us
    unnamed x9, local copies, waits for them, and re-layouts  5.36 us
  transfers between devices with their start and end apart: 33, of which 11 were waited for; matrix products, arithmetic and copies ran while one was open for 23% of the time, Pallas kernels for 0%

profile of v1, /device:TPU:1, one launch (start us, length us, event | category | flops | bytes accessed | tf_op | source)
XLA Modules:
  0.0 173.6 jit_solution(5214677627348664358)
XLA Ops:
  7.7 4.2 %gather_fusion = f32[512,512]{1,0:T(8,128)S(1)} fusion(f32[2048,512]{1,0:T(8,128)} %param.6, s32[1024]{0:T(1024)S(1)} %pad_clamp_fusion), kind=kCustom, calls=%fused_computation | custom fusion | bytes 2099200 | tf_op jit(solution)/shard_map/top_exchange/gather | solution.py:104
  12.1 3.3 %collective-permute-start = (f32[256,512]{1,0:T(8,128)S(1)}, f32[256,512]{1,0:T(8,128)S(1)}, u32[]{:S(2)}, u32[]{:S(2)}) collective-permute-start(f32[256,512]{1,0:T(8,128)S(1)} %constant_dynamic-slice_fusion.6), channel_id=1, source_target_pairs={{0,32},{32,0},{64,96},{96,64},{128,160},{160,128},{192,224},{224,1... | collective-permute-start | bytes 1572872 | tf_op jit(solution)/shard_map/top_exchange/ppermute | solution.py:107
  15.4 2.5 %fusion.58 = (f32[256,256]{1,0:T(8,128)S(1)}, f32[256,256]{1,0:T(8,128)S(1)}, f32[256,256]{1,0:T(8,128)S(1)}, f32[256,256]{1,0:T(8,128)S(1)}, f32[256,256]{1,0:T...) fusion(f32[2048,512]{1,0:T(8,128)} %param.6), kind=kLoop, calls=%fused_computation.156 | loop fusion | bytes 3670016 | tf_op jit(solution)/shard_map/panel_scatter/slice | solution.py:77
  17.9 6.4 %collective-permute-start.22 = (f32[256,256]{1,0:T(8,128)}, f32[256,256]{1,0:T(8,128)}, u32[]{:S(2)}, u32[]{:S(2)}) collective-permute-start(f32[256,256]{1,0:T(8,128)} %get-tuple-element.29), channel_id=1, source_target_pairs={{0,28},{1,29},{32,60},{33,61},{64,92},{65,93},{96,124},{97,125},{1... | collective-permute-start | bytes 786440 | tf_op jit(solution)/shard_map/panel_scatter/ppermute | solution.py:37
  24.3 2.0 %collective-permute-start.23 = (f32[256,256]{1,0:T(8,128)}, f32[256,256]{1,0:T(8,128)}, u32[]{:S(2)}, u32[]{:S(2)}) collective-permute-start(f32[256,256]{1,0:T(8,128)} %get-tuple-element.28), channel_id=1, source_target_pairs={{0,24},{1,25},{32,56},{33,57},{64,88},{65,89},{96,120},{97,121},{1... | collective-permute-start | bytes 786440 | tf_op jit(solution)/shard_map/panel_scatter/ppermute | solution.py:37
  26.3 2.0 %collective-permute-start.24 = (f32[256,256]{1,0:T(8,128)S(1)}, f32[256,256]{1,0:T(8,128)}, u32[]{:S(2)}, u32[]{:S(2)}) collective-permute-start(f32[256,256]{1,0:T(8,128)S(1)} %get-tuple-element.27), channel_id=1, source_target_pairs={{0,20},{1,21},{32,52},{33,53},{64,84},{65,85},{96,116},{97,117},{1... | collective-permute-start | bytes 786440 | tf_op jit(solution)/shard_map/panel_scatter/ppermute | solution.py:37
  28.3 2.0 %collective-permute-start.25 = (f32[256,256]{1,0:T(8,128)S(1)}, f32[256,256]{1,0:T(8,128)}, u32[]{:S(2)}, u32[]{:S(2)}) collective-permute-start(f32[256,256]{1,0:T(8,128)S(1)} %get-tuple-element.26), channel_id=1, source_target_pairs={{0,16},{1,17},{32,48},{33,49},{64,80},{65,81},{96,112},{97,113},{1... | collective-permute-start | bytes 786440 | tf_op jit(solution)/shard_map/panel_scatter/ppermute | solution.py:37
  32.4 1.3 collective-permute-start.26
  33.8 1.3 collective-permute-start.27
  35.2 1.3 collective-permute-start.28
  36.6 4.1 %collective-permute-done.24 = f32[256,256]{1,0:T(8,128)} collective-permute-done((f32[256,256]{1,0:T(8,128)S(1)}, f32[256,256]{1,0:T(8,128)}, u32[]{:S(2)}, u32[]{:S(2)}) %collective-permute-start.24) | collective-permute-done | bytes 262176 | tf_op jit(solution)/shard_map/panel_scatter/ppermute | solution.py:37
  40.8 2.7 %collective-permute-start.3 = (f32[128,512]{1,0:T(8,128)S(1)}, f32[128,512]{1,0:T(8,128)S(1)}, u32[]{:S(2)}, u32[]{:S(2)}) collective-permute-start(f32[128,512]{1,0:T(8,128)S(1)} %pad_maximum_fusion.9), channel_id=1, source_target_pairs={{0,192},{32,224},{64,0},{96,32},{128,64},{160,96},{192,128},{224,1... | collective-permute-start | bytes 786440 | tf_op jit(solution)/shard_map/top_exchange/ppermute | solution.py:118
  44.5 2.0 %collective-permute-done.27 = f32[256,256]{1,0:T(8,128)S(1)} collective-permute-done((f32[256,256]{1,0:T(8,128)S(1)}, f32[256,256]{1,0:T(8,128)S(1)}, u32[]{:S(2)}, u32[]{:S(2)}) %collective-permute-start.27) | collective-permute-done | bytes 262176 | tf_op jit(solution)/shard_map/panel_scatter/ppermute | solution.py:37
  46.5 5.6 %collective-permute-done.28 = f32[256,256]{1,0:T(8,128)S(1)} collective-permute-done((f32[256,256]{1,0:T(8,128)S(1)}, f32[256,256]{1,0:T(8,128)S(1)}, u32[]{:S(2)}, u32[]{:S(2)}) %collective-permute-start.28) | collective-permute-done | bytes 262176 | tf_op jit(solution)/shard_map/panel_scatter/ppermute | solution.py:37
  53.2 1.9 %collective-permute-start.29 = (f32[256,256]{1,0:T(8,128)S(1)}, f32[256,256]{1,0:T(8,128)S(1)}, u32[]{:S(2)}, u32[]{:S(2)}) collective-permute-start(f32[256,256]{1,0:T(8,128)S(1)} %select_select_fusion.5), channel_id=1, source_target_pairs={{0,3},{4,7},{8,11},{12,15},{16,19},{20,23},{24,27},{28,31},{1,0},{... | collective-permute-start | bytes 786440 | tf_op jit(solution)/shard_map/panel_across/ppermute | solution.py:46
  55.1 1.3 collective-permute-start.30
  56.5 3.4 %collective-permute-start.31 = (f32[256,256]{1,0:T(8,128)S(1)}, f32[256,256]{1,0:T(8,128)S(1)}, u32[]{:S(2)}, u32[]{:S(2)}) collective-permute-start(f32[256,256]{1,0:T(8,128)S(1)} %select_select_fusion.5), channel_id=1, source_target_pairs={{0,1},{4,5},{8,9},{12,13},{16,17},{20,21},{24,25},{28,29},{1,2},{5... | collective-permute-start | bytes 786440 | tf_op jit(solution)/shard_map/panel_across/ppermute | solution.py:43
  60.9 1.3 collective-permute-start.8
  62.2 1.3 collective-permute-start.9
  63.5 3.7 %collective-permute-done.31 = f32[256,256]{1,0:T(8,128)S(1)} collective-permute-done((f32[256,256]{1,0:T(8,128)S(1)}, f32[256,256]{1,0:T(8,128)S(1)}, u32[]{:S(2)}, u32[]{:S(2)}) %collective-permute-start.31) | collective-permute-done | bytes 262176 | tf_op jit(solution)/shard_map/panel_across/ppermute | solution.py:43
  68.2 1.3 collective-permute-start.10
  69.5 1.3 collective-permute-start.11
  70.8 1.3 collective-permute-start.12
  72.2 1.3 collective-permute-start.13
  73.5 1.6 collective-permute-start.14
  75.2 2.4 %collective-permute-done.13 = f32[128,256]{1,0:T(8,128)S(1)} collective-permute-done((f32[128,256]{1,0:T(8,128)S(1)}, f32[128,256]{1,0:T(8,128)S(1)}, u32[]{:S(2)}, u32[]{:S(2)}) %collective-permute-start.13) | collective-permute-done | bytes 131104 | tf_op jit(solution)/shard_map/fix_down/ppermute | solution.py:37
  77.6 3.6 %collective-permute-done.14 = f32[128,256]{1,0:T(8,128)S(1)} collective-permute-done((f32[128,256]{1,0:T(8,128)S(1)}, f32[128,256]{1,0:T(8,128)S(1)}, u32[]{:S(2)}, u32[]{:S(2)}) %collective-permute-start.14) | collective-permute-done | bytes 131104 | tf_op jit(solution)/shard_map/fix_down/ppermute | solution.py:37
  81.3 1.9 %collective-permute-start.15 = (f32[128,256]{1,0:T(8,128)S(1)}, f32[128,256]{1,0:T(8,128)S(1)}, u32[]{:S(2)}, u32[]{:S(2)}) collective-permute-start(f32[128,256]{1,0:T(8,128)S(1)} %select_select_fusion.8), channel_id=1, source_target_pairs={{0,3},{4,7},{8,11},{12,15},{16,19},{20,23},{24,27},{28,31},{1,0},{... | collective-permute-start | bytes 393224 | tf_op jit(solution)/shard_map/fix_across/ppermute | solution.py:46
  83.2 1.3 collective-permute-start.16
  84.5 4.4 %collective-permute-start.17 = (f32[128,256]{1,0:T(8,128)S(1)}, f32[128,256]{1,0:T(8,128)S(1)}, u32[]{:S(2)}, u32[]{:S(2)}) collective-permute-start(f32[128,256]{1,0:T(8,128)S(1)} %select_select_fusion.8), channel_id=1, source_target_pairs={{0,1},{4,5},{8,9},{12,13},{16,17},{20,21},{24,25},{28,29},{1,2},{5... | collective-permute-start | bytes 393224 | tf_op jit(solution)/shard_map/fix_across/ppermute | solution.py:43
  89.0 2.5 %collective-permute-start.4 = (f32[128,512]{1,0:T(8,128)S(1)}, f32[128,512]{1,0:T(8,128)S(1)}, u32[]{:S(2)}, u32[]{:S(2)}) collective-permute-start(f32[128,512]{1,0:T(8,128)S(1)} %pad_maximum_fusion.6), channel_id=1, source_target_pairs={{0,64},{32,96},{64,128},{96,160},{128,192},{160,224},{192,0},{224,... | collective-permute-start | bytes 786440 | tf_op jit(solution)/shard_map/top_gather/ppermute | solution.py:61
  91.4 1.8 %collective-permute-start.5 = (f32[128,512]{1,0:T(8,128)S(1)}, f32[128,512]{1,0:T(8,128)S(1)}, u32[]{:S(2)}, u32[]{:S(2)}) collective-permute-start(f32[128,512]{1,0:T(8,128)S(1)} %pad_maximum_fusion.6), channel_id=1, source_target_pairs={{0,128},{32,160},{64,192},{96,224},{128,0},{160,32},{192,64},{224,... | collective-permute-start | bytes 786440 | tf_op jit(solution)/shard_map/top_gather/ppermute | solution.py:61
  93.4 2.0 %collective-permute-start.6 = (f32[128,512]{1,0:T(8,128)S(1)}, f32[128,512]{1,0:T(8,128)S(1)}, u32[]{:S(2)}, u32[]{:S(2)}) collective-permute-start(f32[128,512]{1,0:T(8,128)S(1)} %pad_maximum_fusion.6), channel_id=1, source_target_pairs={{0,192},{32,224},{64,0},{96,32},{128,64},{160,96},{192,128},{224,1... | collective-permute-start | bytes 786440 | tf_op jit(solution)/shard_map/top_gather/ppermute | solution.py:61
  95.9 3.9 %collective-permute-done.5 = f32[128,512]{1,0:T(8,128)S(1)} collective-permute-done((f32[128,512]{1,0:T(8,128)S(1)}, f32[128,512]{1,0:T(8,128)S(1)}, u32[]{:S(2)}, u32[]{:S(2)}) %collective-permute-start.5) | collective-permute-done | bytes 262176 | tf_op jit(solution)/shard_map/top_gather/ppermute | solution.py:61
  99.8 10.1 %collective-permute-start.7 = (f32[4,128,512]{2,1,0:T(8,128)S(1)}, f32[4,128,512]{2,1,0:T(8,128)}, u32[]{:S(2)}, u32[]{:S(2)}) collective-permute-start(f32[4,128,512]{2,1,0:T(8,128)S(1)} %bitcast_dynamic-update-slice_fusion.4), channel_id=1, source_target_pairs={{0,32},{32,0},{64,96},{96,64},{128,160},{160,128},{192,224},{224,1... | collective-permute-start | bytes 3145736 | tf_op jit(solution)/shard_map/top_gather/ppermute | solution.py:63
  110.5 1.4 collective-permute-start.20
  111.9 1.1 broadcast.510.clone.1
  114.4 4.8 %collective-permute-done.19 = f32[128,512]{1,0:T(8,128)S(1)} collective-permute-done((f32[128,512]{1,0:T(8,128)S(1)}, f32[128,512]{1,0:T(8,128)S(1)}, u32[]{:S(2)}, u32[]{:S(2)}) %collective-permute-start.19) | collective-permute-done | bytes 262176 | tf_op jit(solution)/shard_map/fix_gather/ppermute | solution.py:61
  120.0 4.3 %collective-permute-done.20 = f32[128,512]{1,0:T(8,128)S(1)} collective-permute-done((f32[128,512]{1,0:T(8,128)S(1)}, f32[128,512]{1,0:T(8,128)S(1)}, u32[]{:S(2)}, u32[]{:S(2)}) %collective-permute-start.20) | collective-permute-done | bytes 262176 | tf_op jit(solution)/shard_map/fix_gather/ppermute | solution.py:61
  125.9 5.3 %copy.26 = f32[2048,512]{0,1:T(8,128)} copy(f32[2048,512]{1,0:T(8,128)} %param.6) | data formatting | bytes 8388608 | tf_op args[0]
  131.2 1.5 select_bitcast_fusion.3
  134.2 1.9 %fusion.16 = f32[512,256]{1,0:T(8,128)S(1)} fusion(f32[256,512]{1,0:T(8,128)S(1)} %bitcast.76, f32[2,256,256]{2,1,0:T(8,128)} %param.8), kind=kOutput, calls=%fused_computation.53 | convolution fusion | flops 402653184 | bytes 1310720 | tf_op jit(solution)/shard_map/upper/dot_general | solution.py:10
  136.3 1.9 %select_bitcast_fusion = (f32[1,4,128,512]{3,2,1,0:T(8,128)S(1)}, f32[1,4,128,512]{3,2,1,0:T(8,128)S(1)}) fusion(f32[4,128,512]{2,1,0:T(8,128)} %collective-permute-done.21, f32[4,128,512]{2,1,0:T(8,128)} %bitcast_dynamic-update-slice_fusion, pred[]{:T(512)S(6)} %eq.185), kind=kLoop, calls=%fused_computation.19 | loop fusion | flops 524288 | bytes 4194305 | tf_op jit(solution)/shard_map/fix_gather/stack | solution.py:64
  143.3 1.9 %convolution_subtract_fusion = f32[512,512]{1,0:T(8,128)S(1)} fusion(f32[512,512]{1,0:T(8,128)S(1)} %bitcast_select_fusion, f32[512,512]{1,0:T(8,128)S(1)} %bitcast.77, f32[256,512]{1,0:T(8,128)S(1)} %bitcast.73, f32[256,512]{1,0:T(8,128)S(1)} %convolution_bitcast_fusion), kind=kOutput, calls=%fused_computation.10 | convolution fusion | flops 1611137024 | bytes 4194304 | tf_op jit(solution)/shard_map/base/dot_general | solution.py:10
  145.2 6.1 %select_add_fusion = f32[2048,512]{0,1:T(8,128)} fusion(f32[2048,512]{0,1:T(8,128)S(1)} %copy-done, f32[512,512]{1,0:T(8,128)S(1)} %convolution_subtract_fusion, s32[2048]{0:T(1024)S(1)} %get-tuple-element.22, pred[2048]{0:T(1024)(128)(4,1)S(1)} %get-tuple-element.21, pred[512]{0:T(512)(128)(4,1)S(1)} %or_not_fusion), kind=kOutput, calls=%fused_computation.3 | convolution fusion | flops 6446645248 | bytes 9447936 | tf_op jit(solution)/shard_map/base/dot_general | solution.py:10
  151.3 2.1 %fusion.5 = f32[2048,512]{0,1:T(8,128)} fusion(f32[2048,512]{0,1:T(8,128)} %select_add_fusion, f32[256,256]{0,1:T(8,128)S(1)} %fusion.7, f32[256,512]{0,1:T(8,128)S(1)} %copy-done.1, f32[512,256]{1,0:T(8,128)S(1)} %fusion.16, f32[256,512]{0,1:T(8,128)S(1)} %convolution_bitcast_fusion.1, pred[512]{0:T(512)(128)(4,1)S(1)} %fusion.49, ...), kind=kLoop, calls=%fused_computation.28 | loop fusion | flops 917504 | bytes 3933186 | tf_op jit(solution)/shard_map/base/scatter | solution.py:166
  153.4 8.0 %select_subtract_fusion = f32[2048,512]{0,1:T(8,128)} fusion(f32[2048,512]{0,1:T(8,128)} %fusion.5, f32[2048,512]{1,0:T(8,128)} %all-gather.2.cloned.1.call-done, pred[2048]{0:T(1024)(128)(4,1)S(1)} %get-tuple-element.21, f32[256,512]{1,0:T(8,128)S(1)} %bitcast.74, f32[256,512]{1,0:T(8,128)S(1)} %convolution_bitcast_fusion), kind=kOutput, calls=%fused_computation.1 | convolution fusion | flops 3223584768 | bytes 13633536 | tf_op jit(solution)/shard_map/update/dot_general | solution.py:10
  161.4 5.3 %copy.33 = f32[2048,512]{1,0:T(8,128)} copy(f32[2048,512]{0,1:T(8,128)} %select_subtract_fusion) | data formatting | bytes 8388608 | tf_op jit(solution)/shard_map/update/sub | solution.py:177
  (93 shorter events, 19.5 us)
Async XLA Ops:
  6.5 146.9 %all-gather.2.cloned.1.call-start = ((), (), s32[]{:S(2)}) async-start(), calls=%async_computation | async-start | bytes 4718592 | tf_op jit(solution)/shard_map/panel_gather/all_gather | solution.py:169
  12.1 20.3 %collective-permute-start = (f32[256,512]{1,0:T(8,128)S(1)}, f32[256,512]{1,0:T(8,128)S(1)}, u32[]{:S(2)}, u32[]{:S(2)}) collective-permute-start(f32[256,512]{1,0:T(8,128)S(1)} %constant_dynamic-slice_fusion.6), channel_id=1, source_target_pairs={{0,32},{32,0},{64,96},{96,64},{128,160},{160,128},{192,224},{224,1... | collective-permute-start | bytes 1572872 | tf_op jit(solution)/shard_map/top_exchange/ppermute | solution.py:107
  17.9 15.9 %collective-permute-start.22 = (f32[256,256]{1,0:T(8,128)}, f32[256,256]{1,0:T(8,128)}, u32[]{:S(2)}, u32[]{:S(2)}) collective-permute-start(f32[256,256]{1,0:T(8,128)} %get-tuple-element.29), channel_id=1, source_target_pairs={{0,28},{1,29},{32,60},{33,61},{64,92},{65,93},{96,124},{97,125},{1... | collective-permute-start | bytes 786440 | tf_op jit(solution)/shard_map/panel_scatter/ppermute | solution.py:37
  24.3 10.9 %collective-permute-start.23 = (f32[256,256]{1,0:T(8,128)}, f32[256,256]{1,0:T(8,128)}, u32[]{:S(2)}, u32[]{:S(2)}) collective-permute-start(f32[256,256]{1,0:T(8,128)} %get-tuple-element.28), channel_id=1, source_target_pairs={{0,24},{1,25},{32,56},{33,57},{64,88},{65,89},{96,120},{97,121},{1... | collective-permute-start | bytes 786440 | tf_op jit(solution)/shard_map/panel_scatter/ppermute | solution.py:37
  26.3 14.5 %collective-permute-start.24 = (f32[256,256]{1,0:T(8,128)S(1)}, f32[256,256]{1,0:T(8,128)}, u32[]{:S(2)}, u32[]{:S(2)}) collective-permute-start(f32[256,256]{1,0:T(8,128)S(1)} %get-tuple-element.27), channel_id=1, source_target_pairs={{0,20},{1,21},{32,52},{33,53},{64,84},{65,85},{96,116},{97,117},{1... | collective-permute-start | bytes 786440 | tf_op jit(solution)/shard_map/panel_scatter/ppermute | solution.py:37
  28.3 15.2 %collective-permute-start.25 = (f32[256,256]{1,0:T(8,128)S(1)}, f32[256,256]{1,0:T(8,128)}, u32[]{:S(2)}, u32[]{:S(2)}) collective-permute-start(f32[256,256]{1,0:T(8,128)S(1)} %get-tuple-element.26), channel_id=1, source_target_pairs={{0,16},{1,17},{32,48},{33,49},{64,80},{65,81},{96,112},{97,113},{1... | collective-permute-start | bytes 786440 | tf_op jit(solution)/shard_map/panel_scatter/ppermute | solution.py:37
  32.4 11.5 %collective-permute-start.26 = (f32[256,256]{1,0:T(8,128)S(1)}, f32[256,256]{1,0:T(8,128)S(1)}, u32[]{:S(2)}, u32[]{:S(2)}) collective-permute-start(f32[256,256]{1,0:T(8,128)S(1)} %get-tuple-element.25), channel_id=1, source_target_pairs={{0,12},{1,13},{32,44},{33,45},{64,76},{65,77},{96,108},{97,109},{1... | collective-permute-start | bytes 786440 | tf_op jit(solution)/shard_map/panel_scatter/ppermute | solution.py:37
  33.8 12.7 %collective-permute-start.27 = (f32[256,256]{1,0:T(8,128)S(1)}, f32[256,256]{1,0:T(8,128)S(1)}, u32[]{:S(2)}, u32[]{:S(2)}) collective-permute-start(f32[256,256]{1,0:T(8,128)S(1)} %get-tuple-element.24), channel_id=1, source_target_pairs={{0,8},{1,9},{32,40},{33,41},{64,72},{65,73},{96,104},{97,105},{128... | collective-permute-start | bytes 786440 | tf_op jit(solution)/shard_map/panel_scatter/ppermute | solution.py:37
  35.2 16.9 %collective-permute-start.28 = (f32[256,256]{1,0:T(8,128)S(1)}, f32[256,256]{1,0:T(8,128)S(1)}, u32[]{:S(2)}, u32[]{:S(2)}) collective-permute-start(f32[256,256]{1,0:T(8,128)S(1)} %get-tuple-element.23), channel_id=1, source_target_pairs={{0,4},{1,5},{32,36},{33,37},{64,68},{65,69},{96,100},{97,101},{128... | collective-permute-start | bytes 786440 | tf_op jit(solution)/shard_map/panel_scatter/ppermute | solution.py:37
  40.8 15.7 %collective-permute-start.3 = (f32[128,512]{1,0:T(8,128)S(1)}, f32[128,512]{1,0:T(8,128)S(1)}, u32[]{:S(2)}, u32[]{:S(2)}) collective-permute-start(f32[128,512]{1,0:T(8,128)S(1)} %pad_maximum_fusion.9), channel_id=1, source_target_pairs={{0,192},{32,224},{64,0},{96,32},{128,64},{160,96},{192,128},{224,1... | collective-permute-start | bytes 786440 | tf_op jit(solution)/shard_map/top_exchange/ppermute | solution.py:118
  43.5 16.4 %collective-permute-start.2 = (f32[128,512]{1,0:T(8,128)S(1)}, f32[128,512]{1,0:T(8,128)S(1)}, u32[]{:S(2)}, u32[]{:S(2)}) collective-permute-start(f32[128,512]{1,0:T(8,128)S(1)} %pad_maximum_fusion.8), channel_id=1, source_target_pairs={{0,128},{32,160},{64,192},{96,224},{128,0},{160,32},{192,64},{224,... | collective-permute-start | bytes 786440 | tf_op jit(solution)/shard_map/top_exchange/ppermute | solution.py:118
  43.9 16.0 %collective-permute-start.1 = (f32[128,512]{1,0:T(8,128)S(1)}, f32[128,512]{1,0:T(8,128)S(1)}, u32[]{:S(2)}, u32[]{:S(2)}) collective-permute-start(f32[128,512]{1,0:T(8,128)S(1)} %pad_maximum_fusion.7), channel_id=1, source_target_pairs={{0,64},{32,96},{64,128},{96,160},{128,192},{160,224},{192,0},{224,... | collective-permute-start | bytes 786440 | tf_op jit(solution)/shard_map/top_exchange/ppermute | solution.py:118
  53.2 10.3 %collective-permute-start.29 = (f32[256,256]{1,0:T(8,128)S(1)}, f32[256,256]{1,0:T(8,128)S(1)}, u32[]{:S(2)}, u32[]{:S(2)}) collective-permute-start(f32[256,256]{1,0:T(8,128)S(1)} %select_select_fusion.5), channel_id=1, source_target_pairs={{0,3},{4,7},{8,11},{12,15},{16,19},{20,23},{24,27},{28,31},{1,0},{... | collective-permute-start | bytes 786440 | tf_op jit(solution)/shard_map/panel_across/ppermute | solution.py:46
  55.1 8.4 %collective-permute-start.30 = (f32[256,256]{1,0:T(8,128)S(1)}, f32[256,256]{1,0:T(8,128)S(1)}, u32[]{:S(2)}, u32[]{:S(2)}) collective-permute-start(f32[256,256]{1,0:T(8,128)S(1)} %select_select_fusion.5), channel_id=1, source_target_pairs={{0,2},{4,6},{8,10},{12,14},{16,18},{20,22},{24,26},{28,30},{1,3},{... | collective-permute-start | bytes 786440 | tf_op jit(solution)/shard_map/panel_across/ppermute | solution.py:49
  56.5 10.8 %collective-permute-start.31 = (f32[256,256]{1,0:T(8,128)S(1)}, f32[256,256]{1,0:T(8,128)S(1)}, u32[]{:S(2)}, u32[]{:S(2)}) collective-permute-start(f32[256,256]{1,0:T(8,128)S(1)} %select_select_fusion.5), channel_id=1, source_target_pairs={{0,1},{4,5},{8,9},{12,13},{16,17},{20,21},{24,25},{28,29},{1,2},{5... | collective-permute-start | bytes 786440 | tf_op jit(solution)/shard_map/panel_across/ppermute | solution.py:43
  60.9 11.3 %collective-permute-start.8 = (f32[128,256]{1,0:T(8,128)S(1)}, f32[128,256]{1,0:T(8,128)S(1)}, u32[]{:S(2)}, u32[]{:S(2)}) collective-permute-start(f32[128,256]{1,0:T(8,128)S(1)} %fusion.29), channel_id=1, source_target_pairs={{0,28},{1,29},{32,60},{33,61},{64,92},{65,93},{96,124},{97,125},{1... | collective-permute-start | bytes 393224 | tf_op jit(solution)/shard_map/fix_down/ppermute | solution.py:37
  62.2 11.3 %collective-permute-start.9 = (f32[128,256]{1,0:T(8,128)S(1)}, f32[128,256]{1,0:T(8,128)S(1)}, u32[]{:S(2)}, u32[]{:S(2)}) collective-permute-start(f32[128,256]{1,0:T(8,128)S(1)} %fusion.29), channel_id=1, source_target_pairs={{0,24},{1,25},{32,56},{33,57},{64,88},{65,89},{96,120},{97,121},{1... | collective-permute-start | bytes 393224 | tf_op jit(solution)/shard_map/fix_down/ppermute | solution.py:37
  68.2 7.0 %collective-permute-start.10 = (f32[128,256]{1,0:T(8,128)S(1)}, f32[128,256]{1,0:T(8,128)S(1)}, u32[]{:S(2)}, u32[]{:S(2)}) collective-permute-start(f32[128,256]{1,0:T(8,128)S(1)} %fusion.29), channel_id=1, source_target_pairs={{0,20},{1,21},{32,52},{33,53},{64,84},{65,85},{96,116},{97,117},{1... | collective-permute-start | bytes 393224 | tf_op jit(solution)/shard_map/fix_down/ppermute | solution.py:37
  69.5 5.7 %collective-permute-start.11 = (f32[128,256]{1,0:T(8,128)S(1)}, f32[128,256]{1,0:T(8,128)S(1)}, u32[]{:S(2)}, u32[]{:S(2)}) collective-permute-start(f32[128,256]{1,0:T(8,128)S(1)} %fusion.29), channel_id=1, source_target_pairs={{0,16},{1,17},{32,48},{33,49},{64,80},{65,81},{96,112},{97,113},{1... | collective-permute-start | bytes 393224 | tf_op jit(solution)/shard_map/fix_down/ppermute | solution.py:37
  70.8 4.4 %collective-permute-start.12 = (f32[128,256]{1,0:T(8,128)S(1)}, f32[128,256]{1,0:T(8,128)S(1)}, u32[]{:S(2)}, u32[]{:S(2)}) collective-permute-start(f32[128,256]{1,0:T(8,128)S(1)} %fusion.29), channel_id=1, source_target_pairs={{0,12},{1,13},{32,44},{33,45},{64,76},{65,77},{96,108},{97,109},{1... | collective-permute-start | bytes 393224 | tf_op jit(solution)/shard_map/fix_down/ppermute | solution.py:37
  72.2 5.5 %collective-permute-start.13 = (f32[128,256]{1,0:T(8,128)S(1)}, f32[128,256]{1,0:T(8,128)S(1)}, u32[]{:S(2)}, u32[]{:S(2)}) collective-permute-start(f32[128,256]{1,0:T(8,128)S(1)} %fusion.29), channel_id=1, source_target_pairs={{0,8},{1,9},{32,40},{33,41},{64,72},{65,73},{96,104},{97,105},{128... | collective-permute-start | bytes 393224 | tf_op jit(solution)/shard_map/fix_down/ppermute | solution.py:37
  73.5 7.7 %collective-permute-start.14 = (f32[128,256]{1,0:T(8,128)S(1)}, f32[128,256]{1,0:T(8,128)S(1)}, u32[]{:S(2)}, u32[]{:S(2)}) collective-permute-start(f32[128,256]{1,0:T(8,128)S(1)} %fusion.29), channel_id=1, source_target_pairs={{0,4},{1,5},{32,36},{33,37},{64,68},{65,69},{96,100},{97,101},{128... | collective-permute-start | bytes 393224 | tf_op jit(solution)/shard_map/fix_down/ppermute | solution.py:37
  81.3 12.1 %collective-permute-start.15 = (f32[128,256]{1,0:T(8,128)S(1)}, f32[128,256]{1,0:T(8,128)S(1)}, u32[]{:S(2)}, u32[]{:S(2)}) collective-permute-start(f32[128,256]{1,0:T(8,128)S(1)} %select_select_fusion.8), channel_id=1, source_target_pairs={{0,3},{4,7},{8,11},{12,15},{16,19},{20,23},{24,27},{28,31},{1,0},{... | collective-permute-start | bytes 393224 | tf_op jit(solution)/shard_map/fix_across/ppermute | solution.py:46
  83.2 12.2 %collective-permute-start.16 = (f32[128,256]{1,0:T(8,128)S(1)}, f32[128,256]{1,0:T(8,128)S(1)}, u32[]{:S(2)}, u32[]{:S(2)}) collective-permute-start(f32[128,256]{1,0:T(8,128)S(1)} %select_select_fusion.8), channel_id=1, source_target_pairs={{0,2},{4,6},{8,10},{12,14},{16,18},{20,22},{24,26},{28,30},{1,3},{... | collective-permute-start | bytes 393224 | tf_op jit(solution)/shard_map/fix_across/ppermute | solution.py:49
  84.5 10.9 %collective-permute-start.17 = (f32[128,256]{1,0:T(8,128)S(1)}, f32[128,256]{1,0:T(8,128)S(1)}, u32[]{:S(2)}, u32[]{:S(2)}) collective-permute-start(f32[128,256]{1,0:T(8,128)S(1)} %select_select_fusion.8), channel_id=1, source_target_pairs={{0,1},{4,5},{8,9},{12,13},{16,17},{20,21},{24,25},{28,29},{1,2},{5... | collective-permute-start | bytes 393224 | tf_op jit(solution)/shard_map/fix_across/ppermute | solution.py:43
  89.0 6.9 %collective-permute-start.4 = (f32[128,512]{1,0:T(8,128)S(1)}, f32[128,512]{1,0:T(8,128)S(1)}, u32[]{:S(2)}, u32[]{:S(2)}) collective-permute-start(f32[128,512]{1,0:T(8,128)S(1)} %pad_maximum_fusion.6), channel_id=1, source_target_pairs={{0,64},{32,96},{64,128},{96,160},{128,192},{160,224},{192,0},{224,... | collective-permute-start | bytes 786440 | tf_op jit(solution)/shard_map/top_gather/ppermute | solution.py:61
  91.4 8.3 %collective-permute-start.5 = (f32[128,512]{1,0:T(8,128)S(1)}, f32[128,512]{1,0:T(8,128)S(1)}, u32[]{:S(2)}, u32[]{:S(2)}) collective-permute-start(f32[128,512]{1,0:T(8,128)S(1)} %pad_maximum_fusion.6), channel_id=1, source_target_pairs={{0,128},{32,160},{64,192},{96,224},{128,0},{160,32},{192,64},{224,... | collective-permute-start | bytes 786440 | tf_op jit(solution)/shard_map/top_gather/ppermute | solution.py:61
  93.4 6.4 %collective-permute-start.6 = (f32[128,512]{1,0:T(8,128)S(1)}, f32[128,512]{1,0:T(8,128)S(1)}, u32[]{:S(2)}, u32[]{:S(2)}) collective-permute-start(f32[128,512]{1,0:T(8,128)S(1)} %pad_maximum_fusion.6), channel_id=1, source_target_pairs={{0,192},{32,224},{64,0},{96,32},{128,64},{160,96},{192,128},{224,1... | collective-permute-start | bytes 786440 | tf_op jit(solution)/shard_map/top_gather/ppermute | solution.py:61
  95.5 18.2 %collective-permute-start.18 = (f32[128,512]{1,0:T(8,128)S(1)}, f32[128,512]{1,0:T(8,128)S(1)}, u32[]{:S(2)}, u32[]{:S(2)}) collective-permute-start(f32[128,512]{1,0:T(8,128)S(1)} %pad_maximum_fusion.10), channel_id=1, source_target_pairs={{0,64},{32,96},{64,128},{96,160},{128,192},{160,224},{192,0},{224,... | collective-permute-start | bytes 786440 | tf_op jit(solution)/shard_map/fix_gather/ppermute | solution.py:61
  99.8 31.4 %collective-permute-start.7 = (f32[4,128,512]{2,1,0:T(8,128)S(1)}, f32[4,128,512]{2,1,0:T(8,128)}, u32[]{:S(2)}, u32[]{:S(2)}) collective-permute-start(f32[4,128,512]{2,1,0:T(8,128)S(1)} %bitcast_dynamic-update-slice_fusion.4), channel_id=1, source_target_pairs={{0,32},{32,0},{64,96},{96,64},{128,160},{160,128},{192,224},{224,1... | collective-permute-start | bytes 3145736 | tf_op jit(solution)/shard_map/top_gather/ppermute | solution.py:63
  109.9 9.4 %collective-permute-start.19 = (f32[128,512]{1,0:T(8,128)S(1)}, f32[128,512]{1,0:T(8,128)S(1)}, u32[]{:S(2)}, u32[]{:S(2)}) collective-permute-start(f32[128,512]{1,0:T(8,128)S(1)} %pad_maximum_fusion.10), channel_id=1, source_target_pairs={{0,128},{32,160},{64,192},{96,224},{128,0},{160,32},{192,64},{224,... | collective-permute-start | bytes 786440 | tf_op jit(solution)/shard_map/fix_gather/ppermute | solution.py:61
  110.5 13.8 %collective-permute-start.20 = (f32[128,512]{1,0:T(8,128)S(1)}, f32[128,512]{1,0:T(8,128)S(1)}, u32[]{:S(2)}, u32[]{:S(2)}) collective-permute-start(f32[128,512]{1,0:T(8,128)S(1)} %pad_maximum_fusion.10), channel_id=1, source_target_pairs={{0,192},{32,224},{64,0},{96,32},{128,64},{160,96},{192,128},{224,1... | collective-permute-start | bytes 786440 | tf_op jit(solution)/shard_map/fix_gather/ppermute | solution.py:61
  125.0 11.3 %collective-permute-start.21 = (f32[4,128,512]{2,1,0:T(8,128)}, f32[4,128,512]{2,1,0:T(8,128)}, u32[]{:S(2)}, u32[]{:S(2)}) collective-permute-start(f32[4,128,512]{2,1,0:T(8,128)} %bitcast_dynamic-update-slice_fusion), channel_id=1, source_target_pairs={{0,32},{32,0},{64,96},{96,64},{128,160},{160,128},{192,224},{224,1... | collective-permute-start | bytes 3145736 | tf_op jit(solution)/shard_map/fix_gather/ppermute | solution.py:63
  136.3 2.1 %copy-start.2 = (f32[2,256,256]{2,1,0:T(8,128)S(1)}, f32[2,256,256]{2,1,0:T(8,128)}, u32[]{:S(2)}) copy-start(f32[2,256,256]{2,1,0:T(8,128)} %param.8) | copy-start | bytes 1572868
  136.3 2.7 %copy-start.3 = (f32[2,256,256]{2,1,0:T(8,128)S(1)}, f32[2,256,256]{2,1,0:T(8,128)}, u32[]{:S(2)}) copy-start(f32[2,256,256]{2,1,0:T(8,128)} %param.9) | copy-start | bytes 1572868
  140.8 4.4 %copy-start = (f32[2048,512]{0,1:T(8,128)S(1)}, f32[2048,512]{0,1:T(8,128)}, u32[]{:S(2)}) copy-start(f32[2048,512]{0,1:T(8,128)} %copy.26) | copy-start | bytes 12582916
  145.2 6.1 %copy-start.1 = (f32[256,512]{0,1:T(8,128)S(1)}, f32[256,512]{0,1:T(8,128)}, u32[]{:S(2)}) copy-start(f32[256,512]{0,1:T(8,128)} %copy.31) | copy-start | bytes 1572868
Sparse Core Ops, SparseCore 0:
  68.4 54.6 all-gather.1

commit v2 on v1

v2 whole, which is shorter than its diff:
```python
import functools

import jax
import jax.numpy as jnp
from jax import lax
from jax.experimental import pallas as pl
from jax.experimental.pallas import tpu as pltpu
from jax.sharding import PartitionSpec as P

NZ, NX, NY, NCORE = 8, 4, 4, 2


def dot(left, right, precision=lax.Precision.HIGHEST):
    return jnp.dot(left, right, precision=precision, preferred_element_type=jnp.float32)


def at(z, x):
    return z % NZ * NX + x % NX


def along_z(step):
    return [(at(z, x), at(z + step, x)) for z in range(NZ) for x in range(NX)]


def along_y(step):
    return [
        (y * NCORE + c, (y + step) % NY * NCORE + c) for y in range(NY) for c in range(NCORE)
    ]


def other_core():
    return [(y * NCORE + c, y * NCORE + 1 - c) for y in range(NY) for c in range(NCORE)]


def pick(index, options):
    value = options[0]
    for place in range(1, len(options)):
        value = jnp.where(index == place, options[place], value)
    return value


def down_z(z, pieces):
    arrived = [pieces[0]]
    for k in range(1, NZ):
        arrived.append(lax.ppermute(pieces[k], "pcol", [(at(0, 0), at(k, 0)), (at(0, 1), at(k, 1))]))
    return pick(z, arrived)


def across_x(x, mine):
    zs = range(NZ)
    plus = lax.ppermute(
        mine, "pcol", [(at(z, 0), at(z, 1)) for z in zs] + [(at(z, 1), at(z, 2)) for z in zs]
    )
    minus = lax.ppermute(
        mine, "pcol", [(at(z, 0), at(z, 3)) for z in zs] + [(at(z, 1), at(z, 0)) for z in zs]
    )
    twice = lax.ppermute(
        mine, "pcol", [(at(z, 0), at(z, 2)) for z in zs] + [(at(z, 1), at(z, 3)) for z in zs]
    )
    first = pick(x, [mine, plus, twice, minus])
    second = pick(x, [minus, mine, plus, twice])
    return jnp.concatenate([first, second], axis=1)


def gather_y(mine):
    return jnp.stack([mine] + [lax.ppermute(mine, "prow", along_y(k)) for k in range(1, NY)])


def split(value):
    high = value.astype(jnp.bfloat16)
    return high, (value - high.astype(jnp.float32)).astype(jnp.bfloat16)


def factor_kernel(
    ids, top_mine, top_other, fix_mine, fix_other, lower_inverse, upper_inverse,
    factor_high, factor_low, moved_high, moved_low, head,
):
    p, q, y, core = ids[0], ids[1], ids[2], ids[3]
    nb = lower_inverse.shape[1]
    share = top_mine.shape[1] // 2
    width = top_mine.shape[2]

    def rows(mine, other, which, part):
        held = []
        for owner in range(NY):
            back = lax.rem(y - owner + NY, NY)
            held.append(
                jnp.where(
                    core == which,
                    mine[back, part * share : (part + 1) * share, :],
                    other[back, part * share : (part + 1) * share, :],
                )
            )
        return jnp.concatenate(held, axis=0)

    first, second = rows(top_mine, top_other, 0, 0), rows(top_mine, top_other, 1, 0)
    cross_rows = rows(fix_mine, fix_other, 0, 0)[:, nb:]
    panel_rows = rows(fix_mine, fix_other, 1, 0)[:, :nb]
    row = lax.broadcasted_iota(jnp.int32, (nb, width), 0)
    column = lax.broadcasted_iota(jnp.int32, (nb, width), 1)
    in_first = jnp.logical_and(q == 0, column < nb)
    in_second = jnp.logical_and(q == 1, column < nb)
    minus_one = jnp.where(row == column, -1.0, 0.0).astype(jnp.float32)
    upper0 = dot(lower_inverse[0], first)
    lower_top = dot(panel_rows, upper_inverse[0])
    cross = dot(lower_inverse[0], cross_rows)
    swapped1 = second - dot(lower_top, upper0)
    upper1 = dot(lower_inverse[1], swapped1)
    use0 = jnp.where(in_first, minus_one, jnp.where(in_second, 0.0, upper0))
    use1 = jnp.where(in_second, minus_one, jnp.where(in_first, 0.0, upper1))
    solved1 = dot(upper_inverse[1], use1)
    solved0 = dot(upper_inverse[0], use0 - dot(cross, solved1))
    high0, low0 = split(solved0)
    high1, low1 = split(solved1)
    factor_high[:nb], factor_high[nb:] = high0, high1
    factor_low[:nb], factor_low[nb:] = low0, low1
    lower_wide = jnp.concatenate([lower_top] * (width // nb), axis=1)
    top0 = jnp.where(in_first, first, upper0)
    top1 = jnp.where(in_first, lower_wide, jnp.where(in_second, swapped1, upper1))
    head[...] = jnp.where(p == 0, top0, top1)
    drop = jnp.logical_or(in_first, in_second)
    for which in range(NCORE):
        old = jnp.where(drop, 0.0, rows(top_mine, top_other, which, 1))
        panel_part = rows(fix_mine, fix_other, which, 1)
        moved = old - dot(panel_part[:, :nb], solved0) - dot(panel_part[:, nb:], solved1)
        high, low = split(moved)
        moved_high[which * nb : (which + 1) * nb] = high
        moved_low[which * nb : (which + 1) * nb] = low


def update_kernel(
    ids, origin, factor_high, factor_low, moved_high, moved_low, head, *rest
):
    pieces = rest[: NZ + 1]
    matrix, out, matrix_block, out_block, matrix_sem, out_sem = rest[NZ + 1 :]
    p, q = ids[0], ids[1]
    z = lax.div(q, NX)
    nb, width = head.shape
    one = functools.partial(jnp.dot, preferred_element_type=jnp.float32)
    column = lax.broadcasted_iota(jnp.int32, (nb, width), 1)
    drop = jnp.logical_and(q < 2, column < nb)
    owners = [lax.rem(z + step + NZ, NZ) for step in (0, -1, 1, -2, 2, -3, 3, NZ // 2)]

    def place(i):
        return pl.ds(pl.multiple_of(owners[i] * nb, nb), nb)

    def matrix_copy(i):
        return pltpu.make_async_copy(matrix.at[place(i)], matrix_block.at[i % 2], matrix_sem.at[i % 2])

    def out_copy(i):
        return pltpu.make_async_copy(out_block.at[i % 2], out.at[place(i)], out_sem.at[i % 2])

    for i in range(2):
        matrix_copy(i).start()
    for i in range(NZ):
        matrix_copy(i).wait()
        if i >= 2:
            out_copy(i - 2).wait()
        if i < NZ - 1:
            panel = pieces[i][...]
        else:
            panel = jnp.concatenate([pieces[i][...], pieces[i + 1][...]], axis=0)
        high, low = split(panel)
        product = (
            one(high, factor_high[...]) + one(high, factor_low[...]) + one(low, factor_high[...])
        )
        source = origin[place(i), :]
        places = lax.broadcasted_iota(jnp.int32, (nb, 2 * nb), 1)
        chosen = jnp.where(source == places, 1.0, 0.0).astype(jnp.bfloat16)
        moved = one(chosen, moved_high[...]) + one(chosen, moved_low[...])
        kept = jnp.where(drop, 0.0, matrix_block[i % 2]) - product
        value = jnp.where(source >= 0, moved, kept)
        is_head = jnp.logical_and(owners[i] == 0, p < 2)
        out_block[i % 2] = jnp.where(is_head, head[...], value)
        out_copy(i).start()
        if i + 2 < NZ:
            matrix_copy(i + 2).start()
    for i in (NZ - 2, NZ - 1):
        out_copy(i).wait()


def on_device(matrix, pivots, lower_inverse, upper_inverse):
    nb = lower_inverse.shape[1]
    rows = matrix.shape[0]
    n_prow = lax.axis_size("prow")
    p, q = lax.axis_index("prow"), lax.axis_index("pcol")
    y, core = p // NCORE, p % NCORE
    z, x = q // NX, q % NX
    share = 2 * nb // n_prow

    with jax.named_scope("panel_scatter"):
        piece = down_z(z, [matrix[nb * k : nb * (k + 1), :nb] for k in range(NZ)])

    pivot0, pivot1 = pivots[0], pivots[1]
    order = jnp.arange(nb, dtype=jnp.int32)

    def before0(wanted):
        hit = wanted[:, None] == pivot0[None, :]
        found = jnp.sum(jnp.where(hit, order[None, :] + 1, 0), axis=1)
        return jnp.where(found > 0, found - 1, wanted)

    sources = jnp.concatenate([pivot0, before0(pivot1)])
    second_top = before0(nb + order)
    place = lax.broadcasted_iota(jnp.int32, (rows, 1), 0)
    row_ids = (place // nb * n_prow + p) * nb + place % nb
    hit1 = row_ids == pivot1[None, :]
    hit0 = row_ids == pivot0[None, :]
    from1 = jnp.sum(jnp.where(hit1, second_top[None, :] + 1, 0), axis=1, keepdims=True)
    from0 = jnp.sum(jnp.where(hit0, order[None, :] + 1, 0), axis=1, keepdims=True)
    origin = jnp.where(row_ids >= 2 * nb, jnp.where(from1 > 0, from1, from0), 0) - 1

    with jax.named_scope("top_exchange"):
        mine = sources // nb % n_prow == p
        local = sources // nb // n_prow * nb + sources % nb
        chosen = jnp.where(mine[:, None], matrix[local], 0.0)
        sent = lax.dynamic_slice_in_dim(chosen, (1 - core) * nb, nb, 0)
        kept = lax.dynamic_slice_in_dim(chosen, core * nb, nb, 0)
        half = kept + lax.ppermute(sent, "prow", other_core())
        piece, half = lax.optimization_barrier((piece, half))
        total = lax.dynamic_slice_in_dim(half, y * share, share, 0)
        olds = [matrix[:share]]
        for step in range(1, NY):
            to = (y + step) % NY * share
            packed = jnp.concatenate(
                [
                    lax.dynamic_slice_in_dim(half, to, share, 0),
                    lax.dynamic_slice_in_dim(matrix, to, share, 0),
                ]
            )
            got = lax.ppermute(packed, "prow", along_y(step))
            total = total + got[:share]
            olds.append(got[share:])
        slab = jnp.concatenate([total, pick(y, olds)])
    with jax.named_scope("panel_across"):
        piece = across_x(x, piece)
    piece, slab = lax.optimization_barrier((piece, slab))

    def ring(up, down):
        with jax.named_scope("panel_ring"):
            return (
                lax.ppermute(up, "pcol", along_z(1)),
                lax.ppermute(down, "pcol", along_z(-1)),
            )

    up1, down1 = ring(piece, piece)
    with jax.named_scope("fix_down"):
        fix = down_z(z, [slab[:, :nb]] * NZ)
    up1, down1, fix, origin = lax.optimization_barrier((up1, down1, fix, origin))
    up2, down2 = ring(up1, down1)
    with jax.named_scope("fix_across"):
        fix = across_x(x, fix)
    with jax.named_scope("top_gather"):
        top_mine = gather_y(slab)
    up2, down2, fix, top_mine = lax.optimization_barrier((up2, down2, fix, top_mine))
    up3, down3 = ring(up2, down2)
    with jax.named_scope("fix_gather"):
        fix_mine = gather_y(fix)
    up3, down3, fix_mine = lax.optimization_barrier((up3, down3, fix_mine))
    up4, down4 = ring(up3[: nb // 2], down3[nb // 2 :])
    with jax.named_scope("core_gather"):
        top_other = lax.ppermute(top_mine, "prow", other_core())
        fix_other = lax.ppermute(fix_mine, "prow", other_core())

    width = matrix.shape[1]
    ids = jnp.stack([p, q, y, core]).astype(jnp.int32)
    vmem = pl.BlockSpec(memory_space=pltpu.VMEM)
    smem = pl.BlockSpec(memory_space=pltpu.SMEM)
    hbm = pl.BlockSpec(memory_space=pltpu.HBM)
    small = jax.ShapeDtypeStruct((2 * nb, width), jnp.bfloat16)
    with jax.named_scope("factor"):
        parts = pl.pallas_call(
            factor_kernel,
            out_shape=[small] * 4 + [jax.ShapeDtypeStruct((nb, width), jnp.float32)],
            in_specs=[smem] + [vmem] * 6,
            out_specs=[vmem] * 5,
            compiler_params=pltpu.CompilerParams(vmem_limit_bytes=24 * 1024 * 1024),
            cost_estimate=pl.CostEstimate(
                flops=3 * 10**9, bytes_accessed=8 * 2**20, transcendentals=0
            ),
        )(ids, top_mine, top_other, fix_mine, fix_other, lower_inverse, upper_inverse)
    blocks = pltpu.VMEM((2, nb, width), jnp.float32)
    with jax.named_scope("update"):
        return pl.pallas_call(
            update_kernel,
            out_shape=jax.ShapeDtypeStruct((rows, width), jnp.float32),
            in_specs=[smem] + [vmem] * (6 + NZ + 1) + [hbm],
            out_specs=hbm,
            scratch_shapes=[blocks] * 2 + [pltpu.SemaphoreType.DMA((2,))] * 2,
            compiler_params=pltpu.CompilerParams(vmem_limit_bytes=24 * 1024 * 1024),
            cost_estimate=pl.CostEstimate(
                flops=6 * 10**9, bytes_accessed=14 * 2**20, transcendentals=0
            ),
        )(
            ids, origin, *parts, piece, up1, down1, up2, down2, up3, down3, up4, down4,
            pltpu.with_memory_space_constraint(matrix, pltpu.HBM),
        )


def solution(mesh):
    in_specs = (P("prow", "pcol"), P(), P(), P())
    out_specs = P("prow", "pcol")
    return jax.shard_map(
        on_device, mesh=mesh, in_specs=in_specs, out_specs=out_specs, check_vma=False
    )
```

time: 174 us -> 138 us (0.79)
  matrix products: 22.8 us -> 0 us
  Pallas kernels: 0 us -> 16.4 us
  local copies, waits for them, and re-layouts: 24 us -> 8.91 us
  between operations: 14.1 us -> 0.74 us
  starting transfers between devices: 66.4 us -> 75.1 us
  other arithmetic: 11.5 us -> 5.2 us
  waiting for transfers between devices: 34.8 us -> 31 us
    dot_general x11 -> x0, matrix products: 22.8 us -> none  [dot(): jnp.dot(left, right, precision=precision, preferred_element_type=jnp.floa...]
    pallas_call x0 -> x2, Pallas kernels: none -> 16.4 us  [the longest x1 9.73 us: on_device(): pl.pallas_call(update_kernel, out_shape=jax.ShapeDtypeStruct((rows, width...]
    ppermute x14, waiting for transfers between devices: 17.8 us -> 7.33 us  [down_z(): lax.ppermute(pieces[k], 'pcol', [(at(0, 0), at(k, 0)), (at(0, 1), at(k, 1...]
    ppermute x8 -> x16, starting transfers between devices: 19.3 us -> 24.7 us  [the longest x4 8.02 us: ring(): lax.ppermute(down, 'pcol', along_z(-1))]
    sub x1 -> x0, local copies, waits for them, and re-layouts: 5.34 us -> none  [on_device(): return base - jnp.where(kept_row[:, None], product, 0.0)]
    unnamed x9 -> x12, local copies, waits for them, and re-layouts: 5.36 us -> 0.33 us
    ppermute x14, starting transfers between devices: 25.7 us -> 30.1 us  [down_z(): lax.ppermute(pieces[k], 'pcol', [(at(0, 0), at(k, 0)), (at(0, 1), at(k, 1...]
    another operation x4 -> x3, other arithmetic: 3.67 us -> 0.22 us  [the longest x2 0.14 us: gather_y(): jnp.stack([mine] + [lax.ppermute(mine, 'prow', along_y(k)) for k in range...]
  transfers between devices with their start and end apart: 33 -> 40, of which waited for: 11 -> 8; matrix products, arithmetic and copies ran while one was open for 23% -> 8% of each run, Pallas kernels for 0% -> 5%
where the time goes in v2:
time: 138 us; the launch traced here: 137 us
  starting transfers between devices  75.1 us (54%)
  waiting for transfers between devices  31 us (22%)
  Pallas kernels  16.4 us (12%)
  local copies, waits for them, and re-layouts  8.91 us (6%)
  other arithmetic  5.2 us (4%)
    ppermute x14, starting transfers between devices, down_z(): lax.ppermute(pieces[k], 'pcol', [(at(0, 0), at(k, 0)), (at(0, 1), at(k, 1...  30.1 us
    pallas_call x1, Pallas kernels, on_device(): pl.pallas_call(update_kernel, out_shape=jax.ShapeDtypeStruct((rows, width...  9.73 us
    ppermute x4, waiting for transfers between devices, ring(): lax.ppermute(up, 'pcol', along_z(1))  9.09 us
    ppermute x4, starting transfers between devices, ring(): lax.ppermute(down, 'pcol', along_z(-1))  8.02 us
    ppermute x2, starting transfers between devices, across_x(): lax.ppermute(mine, 'pcol', [(at(z, 0), at(z, 1)) for z in zs] + [(at(z, 1...  7.66 us
    ppermute x14, waiting for transfers between devices, down_z(): lax.ppermute(pieces[k], 'pcol', [(at(0, 0), at(k, 0)), (at(0, 1), at(k, 1...  7.33 us
    pallas_call x1, Pallas kernels, on_device(): pl.pallas_call(factor_kernel, out_shape=[small] * 4 + [jax.ShapeDtypeStru...  6.63 us
    ppermute x6, waiting for transfers between devices, gather_y(): lax.ppermute(mine, 'prow', along_y(k))  6.44 us
  transfers between devices with their start and end apart: 40, of which 8 were waited for; matrix products, arithmetic and copies ran while one was open for 8% of the time, Pallas kernels for 5%

profile of v2, /device:TPU:1, one launch (start us, length us, event | category | flops | bytes accessed | tf_op | source)
XLA Modules:
  0.0 137.4 jit_solution(5101664890970132973)
XLA Ops:
  0.0 2.4 %fusion.33 = (f32[256,256]{1,0:T(8,128)S(1)}, f32[256,256]{1,0:T(8,128)S(1)}, f32[256,256]{1,0:T(8,128)S(1)}, f32[256,256]{1,0:T(8,128)S(1)}, f32[256,256]{1,0:T...) fusion(f32[2048,512]{1,0:T(8,128)} %rest_9_.1), kind=kLoop, calls=%fused_computation.101 | loop fusion | bytes 3670016 | tf_op jit(solution)/shard_map/panel_scatter/slice | solution.py:192
  2.4 9.0 %collective-permute-start = (f32[256,256]{1,0:T(8,128)}, f32[256,256]{1,0:T(8,128)}, u32[]{:S(2)}, u32[]{:S(2)}) collective-permute-start(f32[256,256]{1,0:T(8,128)} %get-tuple-element.58), channel_id=1, source_target_pairs={{0,28},{1,29},{32,60},{33,61},{64,92},{65,93},{96,124},{97,125},{1... | collective-permute-start | bytes 786440 | tf_op jit(solution)/shard_map/panel_scatter/ppermute | solution.py:45
  11.5 2.0 %collective-permute-start.1 = (f32[256,256]{1,0:T(8,128)}, f32[256,256]{1,0:T(8,128)}, u32[]{:S(2)}, u32[]{:S(2)}) collective-permute-start(f32[256,256]{1,0:T(8,128)} %get-tuple-element.57), channel_id=1, source_target_pairs={{0,24},{1,25},{32,56},{33,57},{64,88},{65,89},{96,120},{97,121},{1... | collective-permute-start | bytes 786440 | tf_op jit(solution)/shard_map/panel_scatter/ppermute | solution.py:45
  13.5 2.0 %collective-permute-start.2 = (f32[256,256]{1,0:T(8,128)S(1)}, f32[256,256]{1,0:T(8,128)}, u32[]{:S(2)}, u32[]{:S(2)}) collective-permute-start(f32[256,256]{1,0:T(8,128)S(1)} %get-tuple-element.56), channel_id=1, source_target_pairs={{0,20},{1,21},{32,52},{33,53},{64,84},{65,85},{96,116},{97,117},{1... | collective-permute-start | bytes 786440 | tf_op jit(solution)/shard_map/panel_scatter/ppermute | solution.py:45
  15.5 2.0 %collective-permute-start.3 = (f32[256,256]{1,0:T(8,128)S(1)}, f32[256,256]{1,0:T(8,128)}, u32[]{:S(2)}, u32[]{:S(2)}) collective-permute-start(f32[256,256]{1,0:T(8,128)S(1)} %get-tuple-element.55), channel_id=1, source_target_pairs={{0,16},{1,17},{32,48},{33,49},{64,80},{65,81},{96,112},{97,113},{1... | collective-permute-start | bytes 786440 | tf_op jit(solution)/shard_map/panel_scatter/ppermute | solution.py:45
  17.4 2.0 %collective-permute-start.4 = (f32[256,256]{1,0:T(8,128)S(1)}, f32[256,256]{1,0:T(8,128)}, u32[]{:S(2)}, u32[]{:S(2)}) collective-permute-start(f32[256,256]{1,0:T(8,128)S(1)} %get-tuple-element.54), channel_id=1, source_target_pairs={{0,12},{1,13},{32,44},{33,45},{64,76},{65,77},{96,108},{97,109},{1... | collective-permute-start | bytes 786440 | tf_op jit(solution)/shard_map/panel_scatter/ppermute | solution.py:45
  20.7 4.2 %gather_fusion = f32[512,512]{1,0:T(8,128)S(1)} fusion(f32[2048,512]{1,0:T(8,128)} %rest_9_.1, s32[1024]{0:T(1024)S(1)} %pad_clamp_fusion), kind=kCustom, calls=%fused_computation | custom fusion | bytes 2099200 | tf_op jit(solution)/shard_map/top_exchange/gather | solution.py:215
  25.1 2.0 %collective-permute-start.5 = (f32[256,256]{1,0:T(8,128)S(1)}, f32[256,256]{1,0:T(8,128)}, u32[]{:S(2)}, u32[]{:S(2)}) collective-permute-start(f32[256,256]{1,0:T(8,128)S(1)} %get-tuple-element.53), channel_id=1, source_target_pairs={{0,8},{1,9},{32,40},{33,41},{64,72},{65,73},{96,104},{97,105},{128... | collective-permute-start | bytes 786440 | tf_op jit(solution)/shard_map/panel_scatter/ppermute | solution.py:45
  27.1 2.0 %collective-permute-start.6 = (f32[256,256]{1,0:T(8,128)S(1)}, f32[256,256]{1,0:T(8,128)}, u32[]{:S(2)}, u32[]{:S(2)}) collective-permute-start(f32[256,256]{1,0:T(8,128)S(1)} %get-tuple-element.52), channel_id=1, source_target_pairs={{0,4},{1,5},{32,36},{33,37},{64,68},{65,69},{96,100},{97,101},{128... | collective-permute-start | bytes 786440 | tf_op jit(solution)/shard_map/panel_scatter/ppermute | solution.py:45
  29.1 1.0 collective-permute-start.7
  30.2 1.1 constant_dynamic-slice_fusion
  31.3 1.7 %collective-permute-done.5 = f32[256,256]{1,0:T(8,128)} collective-permute-done((f32[256,256]{1,0:T(8,128)S(1)}, f32[256,256]{1,0:T(8,128)}, u32[]{:S(2)}, u32[]{:S(2)}) %collective-permute-start.5) | collective-permute-done | bytes 262176 | tf_op jit(solution)/shard_map/panel_scatter/ppermute | solution.py:45
  32.9 5.6 %collective-permute-done.6 = f32[256,256]{1,0:T(8,128)} collective-permute-done((f32[256,256]{1,0:T(8,128)S(1)}, f32[256,256]{1,0:T(8,128)}, u32[]{:S(2)}, u32[]{:S(2)}) %collective-permute-start.6) | collective-permute-done | bytes 262176 | tf_op jit(solution)/shard_map/panel_scatter/ppermute | solution.py:45
  38.6 1.1 select_select_fusion.2
  39.8 1.4 %collective-permute-start.11 = (f32[128,512]{1,0:T(8,128)S(1)}, f32[128,512]{1,0:T(8,128)S(1)}, u32[]{:S(2)}, u32[]{:S(2)}) collective-permute-start(f32[128,512]{1,0:T(8,128)S(1)} %pad_maximum_fusion.3), channel_id=1, source_target_pairs={{0,64},{32,96},{64,128},{96,160},{128,192},{160,224},{192,0},{224,... | collective-permute-start | bytes 786440 | tf_op jit(solution)/shard_map/top_exchange/ppermute | solution.py:230
  41.2 2.7 %collective-permute-start.12 = (f32[128,512]{1,0:T(8,128)S(1)}, f32[128,512]{1,0:T(8,128)S(1)}, u32[]{:S(2)}, u32[]{:S(2)}) collective-permute-start(f32[128,512]{1,0:T(8,128)S(1)} %pad_maximum_fusion.4), channel_id=1, source_target_pairs={{0,128},{32,160},{64,192},{96,224},{128,0},{160,32},{192,64},{224,... | collective-permute-start | bytes 786440 | tf_op jit(solution)/shard_map/top_exchange/ppermute | solution.py:230
  44.0 1.1 collective-permute-start.13
  45.1 3.1 %collective-permute-start.10 = (f32[256,256]{1,0:T(8,128)S(1)}, f32[256,256]{1,0:T(8,128)S(1)}, u32[]{:S(2)}, u32[]{:S(2)}) collective-permute-start(f32[256,256]{1,0:T(8,128)S(1)} %select_select_fusion.2), channel_id=1, source_target_pairs={{0,1},{4,5},{8,9},{12,13},{16,17},{20,21},{24,25},{28,29},{1,2},{5... | collective-permute-start | bytes 786440 | tf_op jit(solution)/shard_map/panel_across/ppermute | solution.py:51
  48.3 1.9 %collective-permute-start.8 = (f32[256,256]{1,0:T(8,128)S(1)}, f32[256,256]{1,0:T(8,128)S(1)}, u32[]{:S(2)}, u32[]{:S(2)}) collective-permute-start(f32[256,256]{1,0:T(8,128)S(1)} %select_select_fusion.2), channel_id=1, source_target_pairs={{0,3},{4,7},{8,11},{12,15},{16,19},{20,23},{24,27},{28,31},{1,0},{... | collective-permute-start | bytes 786440 | tf_op jit(solution)/shard_map/panel_across/ppermute | solution.py:54
  50.2 1.3 collective-permute-start.9
  51.5 2.7 %collective-permute-done.12 = f32[128,512]{1,0:T(8,128)S(1)} collective-permute-done((f32[128,512]{1,0:T(8,128)S(1)}, f32[128,512]{1,0:T(8,128)S(1)}, u32[]{:S(2)}, u32[]{:S(2)}) %collective-permute-start.12) | collective-permute-done | bytes 262176 | tf_op jit(solution)/shard_map/top_exchange/ppermute | solution.py:230
  54.2 1.0 slice_add_fusion
  55.7 1.8 %collective-permute-done.9 = f32[256,256]{1,0:T(8,128)S(1)} collective-permute-done((f32[256,256]{1,0:T(8,128)S(1)}, f32[256,256]{1,0:T(8,128)S(1)}, u32[]{:S(2)}, u32[]{:S(2)}) %collective-permute-start.9) | collective-permute-done | bytes 262176 | tf_op jit(solution)/shard_map/panel_across/ppermute | solution.py:57
  57.7 1.3 collective-permute-start.16
  59.0 1.3 collective-permute-start.17
  60.3 1.3 collective-permute-start.18
  61.6 1.3 collective-permute-start.19
  62.9 1.0 select_reduce_fusion
  64.7 1.3 collective-permute-start.20
  66.0 1.3 collective-permute-start.21
  67.3 1.3 collective-permute-start.22
  68.7 2.7 %collective-permute-start.15 = (f32[256,512]{1,0:T(8,128)S(1)}, f32[256,512]{1,0:T(8,128)S(1)}, u32[]{:S(2)}, u32[]{:S(2)}) collective-permute-start(f32[256,512]{1,0:T(8,128)S(1)} %pad_maximum_fusion.2.rest_0_), channel_id=1, source_target_pairs={{0,28},{1,29},{2,30},{3,31},{4,0},{5,1},{6,2},{7,3},{8,4},{9,5},{1... | collective-permute-start | bytes 1572872 | tf_op jit(solution)/shard_map/panel_ring/ppermute | solution.py:242
  72.3 1.9 %collective-permute-start.29 = (f32[128,512]{1,0:T(8,128)S(1)}, f32[128,512]{1,0:T(8,128)S(1)}, u32[]{:S(2)}, u32[]{:S(2)}) collective-permute-start(f32[128,512]{1,0:T(8,128)S(1)} %pad_maximum_fusion.6), channel_id=1, source_target_pairs={{0,128},{32,160},{64,192},{96,224},{128,0},{160,32},{192,64},{224,... | collective-permute-start | bytes 786440 | tf_op jit(solution)/shard_map/top_gather/ppermute | solution.py:66
  74.2 1.3 collective-permute-start.30
  75.5 9.1 %collective-permute-done.14.rest_1_ = f32[256,512]{1,0:T(8,128)S(1)} collective-permute-done((f32[256,512]{1,0:T(8,128)S(1)}, f32[256,512]{1,0:T(8,128)S(1)}, u32[]{:S(2)}, u32[]{:S(2)}) %collective-permute-start.14) | collective-permute-done | bytes 524320 | tf_op jit(solution)/shard_map/panel_ring/ppermute | solution.py:241
  84.6 2.2 %collective-permute-start.23 = (f32[256,512]{1,0:T(8,128)S(1)}, f32[256,512]{1,0:T(8,128)S(1)}, u32[]{:S(2)}, u32[]{:S(2)}) collective-permute-start(f32[256,512]{1,0:T(8,128)S(1)} %collective-permute-done.14.rest_1_), channel_id=1, source_target_pairs={{0,4},{1,5},{2,6},{3,7},{4,8},{5,9},{6,10},{7,11},{8,12},{9,13},{1... | collective-permute-start | bytes 1572872 | tf_op jit(solution)/shard_map/panel_ring/ppermute | solution.py:241
  87.3 1.9 %collective-permute-start.25 = (f32[128,256]{1,0:T(8,128)S(1)}, f32[128,256]{1,0:T(8,128)S(1)}, u32[]{:S(2)}, u32[]{:S(2)}) collective-permute-start(f32[128,256]{1,0:T(8,128)S(1)} %select_select_fusion.5), channel_id=1, source_target_pairs={{0,3},{4,7},{8,11},{12,15},{16,19},{20,23},{24,27},{28,31},{1,0},{... | collective-permute-start | bytes 393224 | tf_op jit(solution)/shard_map/fix_across/ppermute | solution.py:54
  89.2 1.3 collective-permute-start.26
  90.5 4.5 %collective-permute-start.27 = (f32[128,256]{1,0:T(8,128)S(1)}, f32[128,256]{1,0:T(8,128)S(1)}, u32[]{:S(2)}, u32[]{:S(2)}) collective-permute-start(f32[128,256]{1,0:T(8,128)S(1)} %select_select_fusion.5), channel_id=1, source_target_pairs={{0,1},{4,5},{8,9},{12,13},{16,17},{20,21},{24,25},{28,29},{1,2},{5... | collective-permute-start | bytes 393224 | tf_op jit(solution)/shard_map/fix_across/ppermute | solution.py:51
  95.2 3.2 %collective-permute-done.27 = f32[128,256]{1,0:T(8,128)S(1)} collective-permute-done((f32[128,256]{1,0:T(8,128)S(1)}, f32[128,256]{1,0:T(8,128)S(1)}, u32[]{:S(2)}, u32[]{:S(2)}) %collective-permute-start.27) | collective-permute-done | bytes 131104 | tf_op jit(solution)/shard_map/fix_across/ppermute | solution.py:51
  98.4 0.8 collective-permute-start.32
  99.3 1.9 %collective-permute-start.33 = (f32[256,512]{1,0:T(8,128)S(1)}, f32[256,512]{1,0:T(8,128)S(1)}, u32[]{:S(2)}, u32[]{:S(2)}) collective-permute-start(f32[256,512]{1,0:T(8,128)S(1)} %collective-permute-done.24.rest_4_), channel_id=1, source_target_pairs={{0,28},{1,29},{2,30},{3,31},{4,0},{5,1},{6,2},{7,3},{8,4},{9,5},{1... | collective-permute-start | bytes 1572872 | tf_op jit(solution)/shard_map/panel_ring/ppermute | solution.py:242
  101.6 1.9 %collective-permute-start.35 = (f32[128,512]{1,0:T(8,128)S(1)}, f32[128,512]{1,0:T(8,128)S(1)}, u32[]{:S(2)}, u32[]{:S(2)}) collective-permute-start(f32[128,512]{1,0:T(8,128)S(1)} %pad_maximum_fusion.7), channel_id=1, source_target_pairs={{0,128},{32,160},{64,192},{96,224},{128,0},{160,32},{192,64},{224,... | collective-permute-start | bytes 786440 | tf_op jit(solution)/shard_map/fix_gather/ppermute | solution.py:66
  104.0 6.4 %collective-permute-done.34 = f32[128,512]{1,0:T(8,128)S(1)} collective-permute-done((f32[128,512]{1,0:T(8,128)S(1)}, f32[128,512]{1,0:T(8,128)S(1)}, u32[]{:S(2)}, u32[]{:S(2)}) %collective-permute-start.34) | collective-permute-done | bytes 262176 | tf_op jit(solution)/shard_map/fix_gather/ppermute | solution.py:66
  110.4 6.3 %collective-permute-start.31 = (f32[4,128,512]{2,1,0:T(8,128)S(1)}, f32[4,128,512]{2,1,0:T(8,128)S(1)}, u32[]{:S(2)}, u32[]{:S(2)}) collective-permute-start(f32[4,128,512]{2,1,0:T(8,128)S(1)} %pad_maximum_fusion.top_mine), channel_id=1, source_target_pairs={{0,32},{32,0},{64,96},{96,64},{128,160},{160,128},{192,224},{224,1... | collective-permute-start | bytes 3145736 | tf_op jit(solution)/shard_map/core_gather/ppermute | solution.py:261
  117.8 3.0 %collective-permute-start.39 = (f32[128,512]{1,0:T(8,128)S(1)}, f32[128,512]{1,0:T(8,128)S(1)}, u32[]{:S(2)}, u32[]{:S(2)}) collective-permute-start(f32[128,512]{1,0:T(8,128)S(1)} %slice.79), channel_id=1, source_target_pairs={{0,28},{1,29},{2,30},{3,31},{4,0},{5,1},{6,2},{7,3},{8,4},{9,5},{1... | collective-permute-start | bytes 786440 | tf_op jit(solution)/shard_map/panel_ring/ppermute | solution.py:242
  120.8 6.6 %factor.1 = (bf16[512,512]{1,0:T(8,128)(2,1)S(1)}, bf16[512,512]{1,0:T(8,128)(2,1)S(1)}, bf16[512,512]{1,0:T(8,128)(2,1)S(1)}, bf16[512,512]{1,0:T(8,128)(2,1)S(1)}, f32[256,512]{1,0:T(8,128)S(1)}) custom-call(s32[4]{0:T(128)S(1)} %pad_add_fusion.2.ids, f32[4,128,512]{2,1,0:T(8,128)S(1)} %pad_maximum_fusion.top_mine, ...), custom_call_target="tpu_custom_call" | custom-call | flops 3000000000 | bytes 8388608 | tf_op jit(solution)/shard_map/factor/pallas_call | solution.py:271
  127.5 9.7 %update.1 = f32[2048,512]{1,0:T(8,128)} custom-call(s32[4]{0:T(128)S(1)} %pad_add_fusion.2.ids, s32[2048,1]{1,0:T(8,128)S(1)} %fusion.13.origin, bf16[512,512]{1,0:T(8,128)(2,1)S(1)} %get-tuple-element.38.factor_high, bf16[512,512]{1,0:T(8,128)(2,1)S(1)} %get-tuple-element.39.factor_low, bf16[512,512]{1,0:T(8,128)(2,1)S(1)} %get-tuple-element.40.moved_high, ...), custom_call_target="tpu_custom_call" | custom-call | flops 6000000000 | bytes 14680064 | tf_op jit(solution)/shard_map/update/pallas_call | solution.py:283
  (83 shorter events, 6.5 us)
Async XLA Ops:
  0.0 19.5 %copy-start.5 = (s32[2,256]{1,0:T(2,128)S(1)}, s32[2,256]{1,0:T(2,128)}, u32[]{:S(2)}) copy-start(s32[2,256]{1,0:T(2,128)} %param.5) | copy-start | bytes 6148
  2.4 22.6 %collective-permute-start = (f32[256,256]{1,0:T(8,128)}, f32[256,256]{1,0:T(8,128)}, u32[]{:S(2)}, u32[]{:S(2)}) collective-permute-start(f32[256,256]{1,0:T(8,128)} %get-tuple-element.58), channel_id=1, source_target_pairs={{0,28},{1,29},{32,60},{33,61},{64,92},{65,93},{96,124},{97,125},{1... | collective-permute-start | bytes 786440 | tf_op jit(solution)/shard_map/panel_scatter/ppermute | solution.py:45
  11.5 15.7 %collective-permute-start.1 = (f32[256,256]{1,0:T(8,128)}, f32[256,256]{1,0:T(8,128)}, u32[]{:S(2)}, u32[]{:S(2)}) collective-permute-start(f32[256,256]{1,0:T(8,128)} %get-tuple-element.57), channel_id=1, source_target_pairs={{0,24},{1,25},{32,56},{33,57},{64,88},{65,89},{96,120},{97,121},{1... | collective-permute-start | bytes 786440 | tf_op jit(solution)/shard_map/panel_scatter/ppermute | solution.py:45
  13.5 15.7 %collective-permute-start.2 = (f32[256,256]{1,0:T(8,128)S(1)}, f32[256,256]{1,0:T(8,128)}, u32[]{:S(2)}, u32[]{:S(2)}) collective-permute-start(f32[256,256]{1,0:T(8,128)S(1)} %get-tuple-element.56), channel_id=1, source_target_pairs={{0,20},{1,21},{32,52},{33,53},{64,84},{65,85},{96,116},{97,117},{1... | collective-permute-start | bytes 786440 | tf_op jit(solution)/shard_map/panel_scatter/ppermute | solution.py:45
  15.5 15.8 %collective-permute-start.3 = (f32[256,256]{1,0:T(8,128)S(1)}, f32[256,256]{1,0:T(8,128)}, u32[]{:S(2)}, u32[]{:S(2)}) collective-permute-start(f32[256,256]{1,0:T(8,128)S(1)} %get-tuple-element.55), channel_id=1, source_target_pairs={{0,16},{1,17},{32,48},{33,49},{64,80},{65,81},{96,112},{97,113},{1... | collective-permute-start | bytes 786440 | tf_op jit(solution)/shard_map/panel_scatter/ppermute | solution.py:45
  17.4 13.8 %collective-permute-start.4 = (f32[256,256]{1,0:T(8,128)S(1)}, f32[256,256]{1,0:T(8,128)}, u32[]{:S(2)}, u32[]{:S(2)}) collective-permute-start(f32[256,256]{1,0:T(8,128)S(1)} %get-tuple-element.54), channel_id=1, source_target_pairs={{0,12},{1,13},{32,44},{33,45},{64,76},{65,77},{96,108},{97,109},{1... | collective-permute-start | bytes 786440 | tf_op jit(solution)/shard_map/panel_scatter/ppermute | solution.py:45
  19.4 0.6 copy-start.3
  25.1 7.9 %collective-permute-start.5 = (f32[256,256]{1,0:T(8,128)S(1)}, f32[256,256]{1,0:T(8,128)}, u32[]{:S(2)}, u32[]{:S(2)}) collective-permute-start(f32[256,256]{1,0:T(8,128)S(1)} %get-tuple-element.53), channel_id=1, source_target_pairs={{0,8},{1,9},{32,40},{33,41},{64,72},{65,73},{96,104},{97,105},{128... | collective-permute-start | bytes 786440 | tf_op jit(solution)/shard_map/panel_scatter/ppermute | solution.py:45
  27.1 11.4 %collective-permute-start.6 = (f32[256,256]{1,0:T(8,128)S(1)}, f32[256,256]{1,0:T(8,128)}, u32[]{:S(2)}, u32[]{:S(2)}) collective-permute-start(f32[256,256]{1,0:T(8,128)S(1)} %get-tuple-element.52), channel_id=1, source_target_pairs={{0,4},{1,5},{32,36},{33,37},{64,68},{65,69},{96,100},{97,101},{128... | collective-permute-start | bytes 786440 | tf_op jit(solution)/shard_map/panel_scatter/ppermute | solution.py:45
  29.1 10.5 %collective-permute-start.7 = (f32[256,512]{1,0:T(8,128)S(1)}, f32[256,512]{1,0:T(8,128)S(1)}, u32[]{:S(2)}, u32[]{:S(2)}) collective-permute-start(f32[256,512]{1,0:T(8,128)S(1)} %constant_dynamic-slice_fusion.6), channel_id=1, source_target_pairs={{0,32},{32,0},{64,96},{96,64},{128,160},{160,128},{192,224},{224,1... | collective-permute-start | bytes 1572872 | tf_op jit(solution)/shard_map/top_exchange/ppermute | solution.py:218
  39.8 10.4 %collective-permute-start.11 = (f32[128,512]{1,0:T(8,128)S(1)}, f32[128,512]{1,0:T(8,128)S(1)}, u32[]{:S(2)}, u32[]{:S(2)}) collective-permute-start(f32[128,512]{1,0:T(8,128)S(1)} %pad_maximum_fusion.3), channel_id=1, source_target_pairs={{0,64},{32,96},{64,128},{96,160},{128,192},{160,224},{192,0},{224,... | collective-permute-start | bytes 786440 | tf_op jit(solution)/shard_map/top_exchange/ppermute | solution.py:230
  41.2 13.0 %collective-permute-start.12 = (f32[128,512]{1,0:T(8,128)S(1)}, f32[128,512]{1,0:T(8,128)S(1)}, u32[]{:S(2)}, u32[]{:S(2)}) collective-permute-start(f32[128,512]{1,0:T(8,128)S(1)} %pad_maximum_fusion.4), channel_id=1, source_target_pairs={{0,128},{32,160},{64,192},{96,224},{128,0},{160,32},{192,64},{224,... | collective-permute-start | bytes 786440 | tf_op jit(solution)/shard_map/top_exchange/ppermute | solution.py:230
  44.0 10.3 %collective-permute-start.13 = (f32[128,512]{1,0:T(8,128)S(1)}, f32[128,512]{1,0:T(8,128)S(1)}, u32[]{:S(2)}, u32[]{:S(2)}) collective-permute-start(f32[128,512]{1,0:T(8,128)S(1)} %pad_maximum_fusion.5), channel_id=1, source_target_pairs={{0,192},{32,224},{64,0},{96,32},{128,64},{160,96},{192,128},{224,1... | collective-permute-start | bytes 786440 | tf_op jit(solution)/shard_map/top_exchange/ppermute | solution.py:230
  45.1 17.8 %copy-start.2 = (s32[256]{0:T(256)S(1)}, s32[256]{0:T(256)}, u32[]{:S(2)}) copy-start(s32[256]{0:T(256)} %get-tuple-element.72) | copy-start | bytes 3076
  45.1 17.8 %copy-start.4 = (s32[256]{0:T(256)S(1)}, s32[256]{0:T(256)}, u32[]{:S(2)}) copy-start(s32[256]{0:T(256)} %copy-done.3) | copy-start | bytes 3076
  45.1 10.1 %collective-permute-start.10 = (f32[256,256]{1,0:T(8,128)S(1)}, f32[256,256]{1,0:T(8,128)S(1)}, u32[]{:S(2)}, u32[]{:S(2)}) collective-permute-start(f32[256,256]{1,0:T(8,128)S(1)} %select_select_fusion.2), channel_id=1, source_target_pairs={{0,1},{4,5},{8,9},{12,13},{16,17},{20,21},{24,25},{28,29},{1,2},{5... | collective-permute-start | bytes 786440 | tf_op jit(solution)/shard_map/panel_across/ppermute | solution.py:51
  48.3 7.4 %collective-permute-start.8 = (f32[256,256]{1,0:T(8,128)S(1)}, f32[256,256]{1,0:T(8,128)S(1)}, u32[]{:S(2)}, u32[]{:S(2)}) collective-permute-start(f32[256,256]{1,0:T(8,128)S(1)} %select_select_fusion.2), channel_id=1, source_target_pairs={{0,3},{4,7},{8,11},{12,15},{16,19},{20,23},{24,27},{28,31},{1,0},{... | collective-permute-start | bytes 786440 | tf_op jit(solution)/shard_map/panel_across/ppermute | solution.py:54
  50.2 7.3 %collective-permute-start.9 = (f32[256,256]{1,0:T(8,128)S(1)}, f32[256,256]{1,0:T(8,128)S(1)}, u32[]{:S(2)}, u32[]{:S(2)}) collective-permute-start(f32[256,256]{1,0:T(8,128)S(1)} %select_select_fusion.2), channel_id=1, source_target_pairs={{0,2},{4,6},{8,10},{12,14},{16,18},{20,22},{24,26},{28,30},{1,3},{... | collective-permute-start | bytes 786440 | tf_op jit(solution)/shard_map/panel_across/ppermute | solution.py:57
  57.7 8.3 %collective-permute-start.16 = (f32[128,256]{1,0:T(8,128)S(1)}, f32[128,256]{1,0:T(8,128)S(1)}, u32[]{:S(2)}, u32[]{:S(2)}) collective-permute-start(f32[128,256]{1,0:T(8,128)S(1)} %slice.77), channel_id=1, source_target_pairs={{0,28},{1,29},{32,60},{33,61},{64,92},{65,93},{96,124},{97,125},{1... | collective-permute-start | bytes 393224 | tf_op jit(solution)/shard_map/fix_down/ppermute | solution.py:45
  59.0 8.3 %collective-permute-start.17 = (f32[128,256]{1,0:T(8,128)S(1)}, f32[128,256]{1,0:T(8,128)S(1)}, u32[]{:S(2)}, u32[]{:S(2)}) collective-permute-start(f32[128,256]{1,0:T(8,128)S(1)} %slice.77), channel_id=1, source_target_pairs={{0,24},{1,25},{32,56},{33,57},{64,88},{65,89},{96,120},{97,121},{1... | collective-permute-start | bytes 393224 | tf_op jit(solution)/shard_map/fix_down/ppermute | solution.py:45
  60.3 8.3 %collective-permute-start.18 = (f32[128,256]{1,0:T(8,128)S(1)}, f32[128,256]{1,0:T(8,128)S(1)}, u32[]{:S(2)}, u32[]{:S(2)}) collective-permute-start(f32[128,256]{1,0:T(8,128)S(1)} %slice.77), channel_id=1, source_target_pairs={{0,20},{1,21},{32,52},{33,53},{64,84},{65,85},{96,116},{97,117},{1... | collective-permute-start | bytes 393224 | tf_op jit(solution)/shard_map/fix_down/ppermute | solution.py:45
  61.6 7.1 %collective-permute-start.19 = (f32[128,256]{1,0:T(8,128)S(1)}, f32[128,256]{1,0:T(8,128)S(1)}, u32[]{:S(2)}, u32[]{:S(2)}) collective-permute-start(f32[128,256]{1,0:T(8,128)S(1)} %slice.77), channel_id=1, source_target_pairs={{0,16},{1,17},{32,48},{33,49},{64,80},{65,81},{96,112},{97,113},{1... | collective-permute-start | bytes 393224 | tf_op jit(solution)/shard_map/fix_down/ppermute | solution.py:45
  64.7 7.1 %collective-permute-start.20 = (f32[128,256]{1,0:T(8,128)S(1)}, f32[128,256]{1,0:T(8,128)S(1)}, u32[]{:S(2)}, u32[]{:S(2)}) collective-permute-start(f32[128,256]{1,0:T(8,128)S(1)} %slice.77), channel_id=1, source_target_pairs={{0,12},{1,13},{32,44},{33,45},{64,76},{65,77},{96,108},{97,109},{1... | collective-permute-start | bytes 393224 | tf_op jit(solution)/shard_map/fix_down/ppermute | solution.py:45
  66.0 6.3 %collective-permute-start.21 = (f32[128,256]{1,0:T(8,128)S(1)}, f32[128,256]{1,0:T(8,128)S(1)}, u32[]{:S(2)}, u32[]{:S(2)}) collective-permute-start(f32[128,256]{1,0:T(8,128)S(1)} %slice.77), channel_id=1, source_target_pairs={{0,8},{1,9},{32,40},{33,41},{64,72},{65,73},{96,104},{97,105},{128... | collective-permute-start | bytes 393224 | tf_op jit(solution)/shard_map/fix_down/ppermute | solution.py:45
  67.3 6.8 %collective-permute-start.22 = (f32[128,256]{1,0:T(8,128)S(1)}, f32[128,256]{1,0:T(8,128)S(1)}, u32[]{:S(2)}, u32[]{:S(2)}) collective-permute-start(f32[128,256]{1,0:T(8,128)S(1)} %slice.77), channel_id=1, source_target_pairs={{0,4},{1,5},{32,36},{33,37},{64,68},{65,69},{96,100},{97,101},{128... | collective-permute-start | bytes 393224 | tf_op jit(solution)/shard_map/fix_down/ppermute | solution.py:45
  68.6 16.0 %collective-permute-start.14 = (f32[256,512]{1,0:T(8,128)S(1)}, f32[256,512]{1,0:T(8,128)S(1)}, u32[]{:S(2)}, u32[]{:S(2)}) collective-permute-start(f32[256,512]{1,0:T(8,128)S(1)} %pad_maximum_fusion.2.rest_0_), channel_id=1, source_target_pairs={{0,4},{1,5},{2,6},{3,7},{4,8},{5,9},{6,10},{7,11},{8,12},{9,13},{1... | collective-permute-start | bytes 1572872 | tf_op jit(solution)/shard_map/panel_ring/ppermute | solution.py:241
  68.7 15.9 %collective-permute-start.15 = (f32[256,512]{1,0:T(8,128)S(1)}, f32[256,512]{1,0:T(8,128)S(1)}, u32[]{:S(2)}, u32[]{:S(2)}) collective-permute-start(f32[256,512]{1,0:T(8,128)S(1)} %pad_maximum_fusion.2.rest_0_), channel_id=1, source_target_pairs={{0,28},{1,29},{2,30},{3,31},{4,0},{5,1},{6,2},{7,3},{8,4},{9,5},{1... | collective-permute-start | bytes 1572872 | tf_op jit(solution)/shard_map/panel_ring/ppermute | solution.py:242
  71.8 15.5 %collective-permute-start.28 = (f32[128,512]{1,0:T(8,128)S(1)}, f32[128,512]{1,0:T(8,128)S(1)}, u32[]{:S(2)}, u32[]{:S(2)}) collective-permute-start(f32[128,512]{1,0:T(8,128)S(1)} %pad_maximum_fusion.6), channel_id=1, source_target_pairs={{0,64},{32,96},{64,128},{96,160},{128,192},{160,224},{192,0},{224,... | collective-permute-start | bytes 786440 | tf_op jit(solution)/shard_map/top_gather/ppermute | solution.py:66
  72.3 16.9 %collective-permute-start.29 = (f32[128,512]{1,0:T(8,128)S(1)}, f32[128,512]{1,0:T(8,128)S(1)}, u32[]{:S(2)}, u32[]{:S(2)}) collective-permute-start(f32[128,512]{1,0:T(8,128)S(1)} %pad_maximum_fusion.6), channel_id=1, source_target_pairs={{0,128},{32,160},{64,192},{96,224},{128,0},{160,32},{192,64},{224,... | collective-permute-start | bytes 786440 | tf_op jit(solution)/shard_map/top_gather/ppermute | solution.py:66
  74.2 16.4 %collective-permute-start.30 = (f32[128,512]{1,0:T(8,128)S(1)}, f32[128,512]{1,0:T(8,128)S(1)}, u32[]{:S(2)}, u32[]{:S(2)}) collective-permute-start(f32[128,512]{1,0:T(8,128)S(1)} %pad_maximum_fusion.6), channel_id=1, source_target_pairs={{0,192},{32,224},{64,0},{96,32},{128,64},{160,96},{192,128},{224,1... | collective-permute-start | bytes 786440 | tf_op jit(solution)/shard_map/top_gather/ppermute | solution.py:66
  84.6 13.8 %collective-permute-start.23 = (f32[256,512]{1,0:T(8,128)S(1)}, f32[256,512]{1,0:T(8,128)S(1)}, u32[]{:S(2)}, u32[]{:S(2)}) collective-permute-start(f32[256,512]{1,0:T(8,128)S(1)} %collective-permute-done.14.rest_1_), channel_id=1, source_target_pairs={{0,4},{1,5},{2,6},{3,7},{4,8},{5,9},{6,10},{7,11},{8,12},{9,13},{1... | collective-permute-start | bytes 1572872 | tf_op jit(solution)/shard_map/panel_ring/ppermute | solution.py:241
  86.8 11.6 %collective-permute-start.24 = (f32[256,512]{1,0:T(8,128)S(1)}, f32[256,512]{1,0:T(8,128)S(1)}, u32[]{:S(2)}, u32[]{:S(2)}) collective-permute-start(f32[256,512]{1,0:T(8,128)S(1)} %collective-permute-done.15.rest_2_), channel_id=1, source_target_pairs={{0,28},{1,29},{2,30},{3,31},{4,0},{5,1},{6,2},{7,3},{8,4},{9,5},{1... | collective-permute-start | bytes 1572872 | tf_op jit(solution)/shard_map/panel_ring/ppermute | solution.py:242
  87.3 7.9 %collective-permute-start.25 = (f32[128,256]{1,0:T(8,128)S(1)}, f32[128,256]{1,0:T(8,128)S(1)}, u32[]{:S(2)}, u32[]{:S(2)}) collective-permute-start(f32[128,256]{1,0:T(8,128)S(1)} %select_select_fusion.5), channel_id=1, source_target_pairs={{0,3},{4,7},{8,11},{12,15},{16,19},{20,23},{24,27},{28,31},{1,0},{... | collective-permute-start | bytes 393224 | tf_op jit(solution)/shard_map/fix_across/ppermute | solution.py:54
  89.2 6.0 %collective-permute-start.26 = (f32[128,256]{1,0:T(8,128)S(1)}, f32[128,256]{1,0:T(8,128)S(1)}, u32[]{:S(2)}, u32[]{:S(2)}) collective-permute-start(f32[128,256]{1,0:T(8,128)S(1)} %select_select_fusion.5), channel_id=1, source_target_pairs={{0,2},{4,6},{8,10},{12,14},{16,18},{20,22},{24,26},{28,30},{1,3},{... | collective-permute-start | bytes 393224 | tf_op jit(solution)/shard_map/fix_across/ppermute | solution.py:57
  90.5 7.8 %collective-permute-start.27 = (f32[128,256]{1,0:T(8,128)S(1)}, f32[128,256]{1,0:T(8,128)S(1)}, u32[]{:S(2)}, u32[]{:S(2)}) collective-permute-start(f32[128,256]{1,0:T(8,128)S(1)} %select_select_fusion.5), channel_id=1, source_target_pairs={{0,1},{4,5},{8,9},{12,13},{16,17},{20,21},{24,25},{28,29},{1,2},{5... | collective-permute-start | bytes 393224 | tf_op jit(solution)/shard_map/fix_across/ppermute | solution.py:51
  95.1 25.6 %copy-start = (f32[2,256,256]{2,1,0:T(8,128)S(1)}, f32[2,256,256]{2,1,0:T(8,128)}, u32[]{:S(2)}) copy-start(f32[2,256,256]{2,1,0:T(8,128)} %lower_inverse.1) | copy-start | bytes 1572868
  95.2 25.6 %copy-start.1 = (f32[2,256,256]{2,1,0:T(8,128)S(1)}, f32[2,256,256]{2,1,0:T(8,128)}, u32[]{:S(2)}) copy-start(f32[2,256,256]{2,1,0:T(8,128)} %upper_inverse.1) | copy-start | bytes 1572868
  98.4 18.4 %collective-permute-start.32 = (f32[256,512]{1,0:T(8,128)S(1)}, f32[256,512]{1,0:T(8,128)S(1)}, u32[]{:S(2)}, u32[]{:S(2)}) collective-permute-start(f32[256,512]{1,0:T(8,128)S(1)} %collective-permute-done.23.rest_3_), channel_id=1, source_target_pairs={{0,4},{1,5},{2,6},{3,7},{4,8},{5,9},{6,10},{7,11},{8,12},{9,13},{1... | collective-permute-start | bytes 1572872 | tf_op jit(solution)/shard_map/panel_ring/ppermute | solution.py:241
  99.3 17.6 %collective-permute-start.33 = (f32[256,512]{1,0:T(8,128)S(1)}, f32[256,512]{1,0:T(8,128)S(1)}, u32[]{:S(2)}, u32[]{:S(2)}) collective-permute-start(f32[256,512]{1,0:T(8,128)S(1)} %collective-permute-done.24.rest_4_), channel_id=1, source_target_pairs={{0,28},{1,29},{2,30},{3,31},{4,0},{5,1},{6,2},{7,3},{8,4},{9,5},{1... | collective-permute-start | bytes 1572872 | tf_op jit(solution)/shard_map/panel_ring/ppermute | solution.py:242
  101.2 9.2 %collective-permute-start.34 = (f32[128,512]{1,0:T(8,128)S(1)}, f32[128,512]{1,0:T(8,128)S(1)}, u32[]{:S(2)}, u32[]{:S(2)}) collective-permute-start(f32[128,512]{1,0:T(8,128)S(1)} %pad_maximum_fusion.7), channel_id=1, source_target_pairs={{0,64},{32,96},{64,128},{96,160},{128,192},{160,224},{192,0},{224,... | collective-permute-start | bytes 786440 | tf_op jit(solution)/shard_map/fix_gather/ppermute | solution.py:66
  101.6 15.2 %collective-permute-start.35 = (f32[128,512]{1,0:T(8,128)S(1)}, f32[128,512]{1,0:T(8,128)S(1)}, u32[]{:S(2)}, u32[]{:S(2)}) collective-permute-start(f32[128,512]{1,0:T(8,128)S(1)} %pad_maximum_fusion.7), channel_id=1, source_target_pairs={{0,128},{32,160},{64,192},{96,224},{128,0},{160,32},{192,64},{224,... | collective-permute-start | bytes 786440 | tf_op jit(solution)/shard_map/fix_gather/ppermute | solution.py:66
  103.5 13.2 %collective-permute-start.36 = (f32[128,512]{1,0:T(8,128)S(1)}, f32[128,512]{1,0:T(8,128)S(1)}, u32[]{:S(2)}, u32[]{:S(2)}) collective-permute-start(f32[128,512]{1,0:T(8,128)S(1)} %pad_maximum_fusion.7), channel_id=1, source_target_pairs={{0,192},{32,224},{64,0},{96,32},{128,64},{160,96},{192,128},{224,1... | collective-permute-start | bytes 786440 | tf_op jit(solution)/shard_map/fix_gather/ppermute | solution.py:66
  110.4 10.4 %collective-permute-start.31 = (f32[4,128,512]{2,1,0:T(8,128)S(1)}, f32[4,128,512]{2,1,0:T(8,128)S(1)}, u32[]{:S(2)}, u32[]{:S(2)}) collective-permute-start(f32[4,128,512]{2,1,0:T(8,128)S(1)} %pad_maximum_fusion.top_mine), channel_id=1, source_target_pairs={{0,32},{32,0},{64,96},{96,64},{128,160},{160,128},{192,224},{224,1... | collective-permute-start | bytes 3145736 | tf_op jit(solution)/shard_map/core_gather/ppermute | solution.py:261
  116.9 3.9 %collective-permute-start.37 = (f32[4,128,512]{2,1,0:T(8,128)S(1)}, f32[4,128,512]{2,1,0:T(8,128)S(1)}, u32[]{:S(2)}, u32[]{:S(2)}) collective-permute-start(f32[4,128,512]{2,1,0:T(8,128)S(1)} %pad_maximum_fusion.1.fix_mine), channel_id=1, source_target_pairs={{0,32},{32,0},{64,96},{96,64},{128,160},{160,128},{192,224},{224,1... | collective-permute-start | bytes 3145736 | tf_op jit(solution)/shard_map/core_gather/ppermute | solution.py:262
  117.7 9.7 %collective-permute-start.38 = (f32[128,512]{1,0:T(8,128)S(1)}, f32[128,512]{1,0:T(8,128)S(1)}, u32[]{:S(2)}, u32[]{:S(2)}) collective-permute-start(f32[128,512]{1,0:T(8,128)S(1)} %slice.78), channel_id=1, source_target_pairs={{0,4},{1,5},{2,6},{3,7},{4,8},{5,9},{6,10},{7,11},{8,12},{9,13},{1... | collective-permute-start | bytes 786440 | tf_op jit(solution)/shard_map/panel_ring/ppermute | solution.py:241
  117.8 9.6 %collective-permute-start.39 = (f32[128,512]{1,0:T(8,128)S(1)}, f32[128,512]{1,0:T(8,128)S(1)}, u32[]{:S(2)}, u32[]{:S(2)}) collective-permute-start(f32[128,512]{1,0:T(8,128)S(1)} %slice.79), channel_id=1, source_target_pairs={{0,28},{1,29},{2,30},{3,31},{4,0},{5,1},{6,2},{7,3},{8,4},{9,5},{1... | collective-permute-start | bytes 786440 | tf_op jit(solution)/shard_map/panel_ring/ppermute | solution.py:242

commit v3 on v2

--- a/solution.py
+++ b/solution.py
@@ -1,5 +1,3 @@
-import functools
-
 import jax
 import jax.numpy as jnp
 from jax import lax
@@ -10,8 +8,18 @@
 NZ, NX, NY, NCORE = 8, 4, 4, 2
 
 
-def dot(left, right, precision=lax.Precision.HIGHEST):
-    return jnp.dot(left, right, precision=precision, preferred_element_type=jnp.float32)
+def one(left, right):
+    return jnp.dot(left, right, preferred_element_type=jnp.float32)
+
+
+def split(value):
+    high = value.astype(jnp.bfloat16)
+    return high, (value - high.astype(jnp.float32)).astype(jnp.bfloat16)
+
+
+def dot(left, right):
+    (left_high, left_low), (right_high, right_low) = split(left), split(right)
+    return one(left_high, right_high) + one(left_high, right_low) + one(left_low, right_high)
 
 
 def at(z, x):
@@ -34,29 +42,40 @@
 
 def pick(index, options):
     value = options[0]
-    for place in range(1, len(options)):
+    for place in reversed(range(1, len(options))):
         value = jnp.where(index == place, options[place], value)
     return value
 
 
-def down_z(z, pieces):
+def scatter_z(z, pieces):
     arrived = [pieces[0]]
     for k in range(1, NZ):
-        arrived.append(lax.ppermute(pieces[k], "pcol", [(at(0, 0), at(k, 0)), (at(0, 1), at(k, 1))]))
-    return pick(z, arrived)
+        pairs = [(at(0, x), at(k, x)) for x in (0, 1)]
+        arrived.append(lax.ppermute(pieces[k], "pcol", pairs))
+    return arrived
+
+
+def send_z(value, pairs):
+    return lax.ppermute(value, "pcol", [(at(a, x), at(b, x)) for a, b in pairs for x in (0, 1)])
+
+
+def spread_z(z, mine):
+    mine = jnp.where(z == 4, send_z(mine, [(0, 4)]), mine)
+    above = send_z(mine, [(0, 1), (4, 3)])
+    below = send_z(mine, [(0, 7), (4, 5)])
+    between = send_z(mine, [(0, 2), (4, 6)])
+    return pick(z, [mine, above, between, above, mine, below, between, below])
 
 
 def across_x(x, mine):
-    zs = range(NZ)
-    plus = lax.ppermute(
-        mine, "pcol", [(at(z, 0), at(z, 1)) for z in zs] + [(at(z, 1), at(z, 2)) for z in zs]
-    )
-    minus = lax.ppermute(
-        mine, "pcol", [(at(z, 0), at(z, 3)) for z in zs] + [(at(z, 1), at(z, 0)) for z in zs]
-    )
-    twice = lax.ppermute(
-        mine, "pcol", [(at(z, 0), at(z, 2)) for z in zs] + [(at(z, 1), at(z, 3)) for z in zs]
-    )
+    def both(to_first, to_second):
+        return [(at(z, 0), at(z, to_first)) for z in range(NZ)] + [
+            (at(z, 1), at(z, to_second)) for z in range(NZ)
+        ]
+
+    plus = lax.ppermute(mine, "pcol", both(1, 2))
+    minus = lax.ppermute(mine, "pcol", both(3, 0))
+    twice = lax.ppermute(mine, "pcol", both(2, 3))
     first = pick(x, [mine, plus, twice, minus])
     second = pick(x, [minus, mine, plus, twice])
     return jnp.concatenate([first, second], axis=1)
@@ -64,11 +83,6 @@
 
 def gather_y(mine):
     return jnp.stack([mine] + [lax.ppermute(mine, "prow", along_y(k)) for k in range(1, NY)])
-
-
-def split(value):
-    high = value.astype(jnp.bfloat16)
-    return high, (value - high.astype(jnp.float32)).astype(jnp.bfloat16)
 
 
 def factor_kernel(
@@ -136,7 +150,6 @@
     p, q = ids[0], ids[1]
     z = lax.div(q, NX)
     nb, width = head.shape
-    one = functools.partial(jnp.dot, preferred_element_type=jnp.float32)
     column = lax.broadcasted_iota(jnp.int32, (nb, width), 1)
     drop = jnp.logical_and(q < 2, column < nb)
     owners = [lax.rem(z + step + NZ, NZ) for step in (0, -1, 1, -2, 2, -3, 3, NZ // 2)]
@@ -144,38 +157,44 @@
     def place(i):
         return pl.ds(pl.multiple_of(owners[i] * nb, nb), nb)
 
+    def part(i):
+        return pl.ds(i % 4 * nb, nb)
+
     def matrix_copy(i):
-        return pltpu.make_async_copy(matrix.at[place(i)], matrix_block.at[i % 2], matrix_sem.at[i % 2])
+        return pltpu.make_async_copy(
+            matrix.at[place(i)], matrix_block.at[part(i)], matrix_sem.at[i % 4]
+        )
 
     def out_copy(i):
-        return pltpu.make_async_copy(out_block.at[i % 2], out.at[place(i)], out_sem.at[i % 2])
-
-    for i in range(2):
+        return pltpu.make_async_copy(out_block.at[part(i)], out.at[place(i)], out_sem.at[i % 4])
+
+    for i in range(4):
         matrix_copy(i).start()
-    for i in range(NZ):
-        matrix_copy(i).wait()
-        if i >= 2:
-            out_copy(i - 2).wait()
-        if i < NZ - 1:
-            panel = pieces[i][...]
-        else:
-            panel = jnp.concatenate([pieces[i][...], pieces[i + 1][...]], axis=0)
-        high, low = split(panel)
+    for i in range(0, NZ, 2):
+        held = [pieces[i][...], pieces[i + 1][...]]
+        if i + 2 == NZ:
+            held.append(pieces[i + 2][...])
+        high, low = split(jnp.concatenate(held, axis=0))
         product = (
             one(high, factor_high[...]) + one(high, factor_low[...]) + one(low, factor_high[...])
         )
-        source = origin[place(i), :]
-        places = lax.broadcasted_iota(jnp.int32, (nb, 2 * nb), 1)
+        source = jnp.concatenate([origin[place(i), :], origin[place(i + 1), :]], axis=0)
+        places = lax.broadcasted_iota(jnp.int32, (2 * nb, 2 * nb), 1)
         chosen = jnp.where(source == places, 1.0, 0.0).astype(jnp.bfloat16)
         moved = one(chosen, moved_high[...]) + one(chosen, moved_low[...])
-        kept = jnp.where(drop, 0.0, matrix_block[i % 2]) - product
-        value = jnp.where(source >= 0, moved, kept)
-        is_head = jnp.logical_and(owners[i] == 0, p < 2)
-        out_block[i % 2] = jnp.where(is_head, head[...], value)
-        out_copy(i).start()
-        if i + 2 < NZ:
-            matrix_copy(i + 2).start()
-    for i in (NZ - 2, NZ - 1):
+        for j in (i, i + 1):
+            here = slice((j - i) * nb, (j - i + 1) * nb)
+            matrix_copy(j).wait()
+            if j >= 4:
+                out_copy(j - 4).wait()
+            kept = jnp.where(drop, 0.0, matrix_block[part(j)]) - product[here]
+            value = jnp.where(source[here] >= 0, moved[here], kept)
+            is_head = jnp.logical_and(owners[j] == 0, p < 2)
+            out_block[part(j)] = jnp.where(is_head, head[...], value)
+            out_copy(j).start()
+            if j + 4 < NZ:
+                matrix_copy(j + 4).start()
+    for i in range(NZ - 4, NZ):
         out_copy(i).wait()
 
 
@@ -189,25 +208,26 @@
     share = 2 * nb // n_prow
 
     with jax.named_scope("panel_scatter"):
-        piece = down_z(z, [matrix[nb * k : nb * (k + 1), :nb] for k in range(NZ)])
-
-    pivot0, pivot1 = pivots[0], pivots[1]
+        arrived = scatter_z(z, [matrix[nb * k : nb * (k + 1), :nb] for k in range(NZ)])
+
     order = jnp.arange(nb, dtype=jnp.int32)
 
-    def before0(wanted):
+    def before0(pivot0, wanted):
         hit = wanted[:, None] == pivot0[None, :]
         found = jnp.sum(jnp.where(hit, order[None, :] + 1, 0), axis=1)
         return jnp.where(found > 0, found - 1, wanted)
 
-    sources = jnp.concatenate([pivot0, before0(pivot1)])
-    second_top = before0(nb + order)
-    place = lax.broadcasted_iota(jnp.int32, (rows, 1), 0)
-    row_ids = (place // nb * n_prow + p) * nb + place % nb
-    hit1 = row_ids == pivot1[None, :]
-    hit0 = row_ids == pivot0[None, :]
-    from1 = jnp.sum(jnp.where(hit1, second_top[None, :] + 1, 0), axis=1, keepdims=True)
-    from0 = jnp.sum(jnp.where(hit0, order[None, :] + 1, 0), axis=1, keepdims=True)
-    origin = jnp.where(row_ids >= 2 * nb, jnp.where(from1 > 0, from1, from0), 0) - 1
+    def origin_of(pivots):
+        second_top = before0(pivots[0], nb + order)
+        place = lax.broadcasted_iota(jnp.int32, (rows, 1), 0)
+        row_ids = (place // nb * n_prow + p) * nb + place % nb
+        hit1 = row_ids == pivots[1][None, :]
+        hit0 = row_ids == pivots[0][None, :]
+        from1 = jnp.sum(jnp.where(hit1, second_top[None, :] + 1, 0), axis=1, keepdims=True)
+        from0 = jnp.sum(jnp.where(hit0, order[None, :] + 1, 0), axis=1, keepdims=True)
+        return jnp.where(row_ids >= 2 * nb, jnp.where(from1 > 0, from1, from0), 0) - 1
+
+    sources = jnp.concatenate([pivots[0], before0(pivots[0], pivots[1])])
 
     with jax.named_scope("top_exchange"):
         mine = sources // nb % n_prow == p
@@ -216,7 +236,7 @@
         sent = lax.dynamic_slice_in_dim(chosen, (1 - core) * nb, nb, 0)
         kept = lax.dynamic_slice_in_dim(chosen, core * nb, nb, 0)
         half = kept + lax.ppermute(sent, "prow", other_core())
-        piece, half = lax.optimization_barrier((piece, half))
+        piece, half = lax.optimization_barrier((pick(z, arrived), half))
         total = lax.dynamic_slice_in_dim(half, y * share, share, 0)
         olds = [matrix[:share]]
         for step in range(1, NY):
@@ -231,9 +251,6 @@
             total = total + got[:share]
             olds.append(got[share:])
         slab = jnp.concatenate([total, pick(y, olds)])
-    with jax.named_scope("panel_across"):
-        piece = across_x(x, piece)
-    piece, slab = lax.optimization_barrier((piece, slab))
 
     def ring(up, down):
         with jax.named_scope("panel_ring"):
@@ -242,16 +259,20 @@
                 lax.ppermute(down, "pcol", along_z(-1)),
             )
 
+    with jax.named_scope("panel_across"):
+        piece = across_x(x, piece)
+    piece, slab, pivots = lax.optimization_barrier((piece, slab, pivots))
     up1, down1 = ring(piece, piece)
     with jax.named_scope("fix_down"):
-        fix = down_z(z, [slab[:, :nb]] * NZ)
-    up1, down1, fix, origin = lax.optimization_barrier((up1, down1, fix, origin))
+        fix = spread_z(z, slab[:, :nb])
+    origin = origin_of(pivots)
+    fix, origin, _ = lax.optimization_barrier((fix, origin, up1))
     up2, down2 = ring(up1, down1)
     with jax.named_scope("fix_across"):
         fix = across_x(x, fix)
     with jax.named_scope("top_gather"):
         top_mine = gather_y(slab)
-    up2, down2, fix, top_mine = lax.optimization_barrier((up2, down2, fix, top_mine))
+    fix, top_mine, _ = lax.optimization_barrier((fix, top_mine, up2))
     up3, down3 = ring(up2, down2)
     with jax.named_scope("fix_gather"):
         fix_mine = gather_y(fix)
@@ -278,14 +299,14 @@
                 flops=3 * 10**9, bytes_accessed=8 * 2**20, transcendentals=0
             ),
         )(ids, top_mine, top_other, fix_mine, fix_other, lower_inverse, upper_inverse)
-    blocks = pltpu.VMEM((2, nb, width), jnp.float32)
+    blocks = pltpu.VMEM((4 * nb, width), jnp.float32)
     with jax.named_scope("update"):
         return pl.pallas_call(
             update_kernel,
             out_shape=jax.ShapeDtypeStruct((rows, width), jnp.float32),
             in_specs=[smem] + [vmem] * (6 + NZ + 1) + [hbm],
             out_specs=hbm,
-            scratch_shapes=[blocks] * 2 + [pltpu.SemaphoreType.DMA((2,))] * 2,
+            scratch_shapes=[blocks] * 2 + [pltpu.SemaphoreType.DMA((4,))] * 2,
             compiler_params=pltpu.CompilerParams(vmem_limit_bytes=24 * 1024 * 1024),
             cost_estimate=pl.CostEstimate(
                 flops=6 * 10**9, bytes_accessed=14 * 2**20, transcendentals=0

time: 138 us -> 134 us (0.971)
  Pallas kernels: 16.4 us -> 13.2 us
  waiting for transfers between devices: 31 us -> 28.8 us
    ppermute x20 -> x17, starting transfers between devices: 44.2 us -> 36.6 us  [the longest x7 20.3 us: scatter_z(): arrived.append(lax.ppermute(pieces[k], 'pcol', pairs))]
    ppermute x4, waiting for transfers between devices: 9.09 us -> 2.07 us  [ring(): lax.ppermute(up, 'pcol', along_z(1))]
    ppermute x1, starting transfers between devices: 6.33 us -> 12.9 us  [on_device(): top_other = lax.ppermute(top_mine, 'prow', other_core())]
    ppermute x4, starting transfers between devices: 8.02 us -> 12 us  [ring(): lax.ppermute(down, 'pcol', along_z(-1))]
    ppermute x20 -> x17, waiting for transfers between devices: 12.7 us -> 16.1 us  [the longest x7 5.73 us: scatter_z(): arrived.append(lax.ppermute(pieces[k], 'pcol', pairs))]
    ppermute x4, starting transfers between devices: 3.19 us -> 0.25 us  [ring(): lax.ppermute(up, 'pcol', along_z(1))]
    pallas_call x1, Pallas kernels: 6.63 us -> 4.05 us  [on_device(): pl.pallas_call(factor_kernel, out_shape=[small] * 4 + [jax.ShapeDtypeStru...]
    ppermute x6, waiting for transfers between devices: 6.44 us -> 8.07 us  [gather_y(): lax.ppermute(mine, 'prow', along_y(k))]
  transfers between devices with their start and end apart: 40 -> 37, of which waited for: 8 -> 9; matrix products, arithmetic and copies ran while one was open for 8% -> 10% of each run, Pallas kernels for 5% -> 3%
where the time goes in v3:
time: 134 us; the launch traced here: 133 us
  starting transfers between devices  75.1 us (56%)
  waiting for transfers between devices  28.8 us (21%)
  Pallas kernels  13.2 us (10%)
  local copies, waits for them, and re-layouts  9.55 us (7%)
  other arithmetic  5.94 us (4%)
    ppermute x7, starting transfers between devices, scatter_z(): arrived.append(lax.ppermute(pieces[k], 'pcol', pairs))  20.3 us
    ppermute x1, starting transfers between devices, on_device(): top_other = lax.ppermute(top_mine, 'prow', other_core())  12.9 us
    ppermute x4, starting transfers between devices, ring(): lax.ppermute(down, 'pcol', along_z(-1))  12 us
    pallas_call x1, Pallas kernels, on_device(): pl.pallas_call(update_kernel, out_shape=jax.ShapeDtypeStruct((rows, width...  9.11 us
    ppermute x6, waiting for transfers between devices, gather_y(): lax.ppermute(mine, 'prow', along_y(k))  8.07 us
    ppermute x6, starting transfers between devices, gather_y(): lax.ppermute(mine, 'prow', along_y(k))  6.12 us
    ppermute x7, waiting for transfers between devices, scatter_z(): arrived.append(lax.ppermute(pieces[k], 'pcol', pairs))  5.73 us
    ppermute x4, waiting for transfers between devices, send_z(): lax.ppermute(value, 'pcol', [(at(a, x), at(b, x)) for a, b in pairs for x...  5.53 us
  transfers between devices with their start and end apart: 37, of which 9 were waited for; matrix products, arithmetic and copies ran while one was open for 10% of the time, Pallas kernels for 3%

profile of v3, /device:TPU:1, one launch (start us, length us, event | category | flops | bytes accessed | tf_op | source)
XLA Modules:
  0.0 133.2 jit_solution(15523963382839133272)
XLA Ops:
  0.0 2.4 %fusion.33 = (f32[256,256]{1,0:T(8,128)S(1)}, f32[256,256]{1,0:T(8,128)S(1)}, f32[256,256]{1,0:T(8,128)S(1)}, f32[256,256]{1,0:T(8,128)S(1)}, f32[256,256]{1,0:T...) fusion(f32[2048,512]{1,0:T(8,128)} %rest_9_.1), kind=kLoop, calls=%fused_computation.102 | loop fusion | bytes 3670016 | tf_op jit(solution)/shard_map/panel_scatter/slice | solution.py:211
  2.4 5.1 %collective-permute-start = (f32[256,256]{1,0:T(8,128)}, f32[256,256]{1,0:T(8,128)}, u32[]{:S(2)}, u32[]{:S(2)}) collective-permute-start(f32[256,256]{1,0:T(8,128)} %get-tuple-element.50), channel_id=1, source_target_pairs={{0,4},{1,5},{32,36},{33,37},{64,68},{65,69},{96,100},{97,101},{128... | collective-permute-start | bytes 786440 | tf_op jit(solution)/shard_map/panel_scatter/ppermute | solution.py:54
  7.5 2.7 %collective-permute-start.1 = (f32[256,256]{1,0:T(8,128)}, f32[256,256]{1,0:T(8,128)}, u32[]{:S(2)}, u32[]{:S(2)}) collective-permute-start(f32[256,256]{1,0:T(8,128)} %get-tuple-element.49), channel_id=1, source_target_pairs={{0,8},{1,9},{32,40},{33,41},{64,72},{65,73},{96,104},{97,105},{128... | collective-permute-start | bytes 786440 | tf_op jit(solution)/shard_map/panel_scatter/ppermute | solution.py:54
  10.2 2.7 %collective-permute-start.2 = (f32[256,256]{1,0:T(8,128)S(1)}, f32[256,256]{1,0:T(8,128)}, u32[]{:S(2)}, u32[]{:S(2)}) collective-permute-start(f32[256,256]{1,0:T(8,128)S(1)} %get-tuple-element.48), channel_id=1, source_target_pairs={{0,12},{1,13},{32,44},{33,45},{64,76},{65,77},{96,108},{97,109},{1... | collective-permute-start | bytes 786440 | tf_op jit(solution)/shard_map/panel_scatter/ppermute | solution.py:54
  12.9 3.9 %collective-permute-start.3 = (f32[256,256]{1,0:T(8,128)S(1)}, f32[256,256]{1,0:T(8,128)}, u32[]{:S(2)}, u32[]{:S(2)}) collective-permute-start(f32[256,256]{1,0:T(8,128)S(1)} %get-tuple-element.47), channel_id=1, source_target_pairs={{0,16},{1,17},{32,48},{33,49},{64,80},{65,81},{96,112},{97,113},{1... | collective-permute-start | bytes 786440 | tf_op jit(solution)/shard_map/panel_scatter/ppermute | solution.py:54
  16.8 2.0 %collective-permute-start.4 = (f32[256,256]{1,0:T(8,128)S(1)}, f32[256,256]{1,0:T(8,128)}, u32[]{:S(2)}, u32[]{:S(2)}) collective-permute-start(f32[256,256]{1,0:T(8,128)S(1)} %get-tuple-element.46), channel_id=1, source_target_pairs={{0,20},{1,21},{32,52},{33,53},{64,84},{65,85},{96,116},{97,117},{1... | collective-permute-start | bytes 786440 | tf_op jit(solution)/shard_map/panel_scatter/ppermute | solution.py:54
  19.1 4.2 %gather_fusion = f32[512,512]{1,0:T(8,128)S(1)} fusion(f32[2048,512]{1,0:T(8,128)} %rest_9_.1, s32[1024]{0:T(1024)S(1)} %pad_clamp_fusion), kind=kCustom, calls=%fused_computation | custom fusion | bytes 2099200 | tf_op jit(solution)/shard_map/top_exchange/gather | solution.py:235
  23.5 2.0 %collective-permute-start.5 = (f32[256,256]{1,0:T(8,128)S(1)}, f32[256,256]{1,0:T(8,128)}, u32[]{:S(2)}, u32[]{:S(2)}) collective-permute-start(f32[256,256]{1,0:T(8,128)S(1)} %get-tuple-element.45), channel_id=1, source_target_pairs={{0,24},{1,25},{32,56},{33,57},{64,88},{65,89},{96,120},{97,121},{1... | collective-permute-start | bytes 786440 | tf_op jit(solution)/shard_map/panel_scatter/ppermute | solution.py:54
  25.5 2.0 %collective-permute-start.6 = (f32[256,256]{1,0:T(8,128)S(1)}, f32[256,256]{1,0:T(8,128)}, u32[]{:S(2)}, u32[]{:S(2)}) collective-permute-start(f32[256,256]{1,0:T(8,128)S(1)} %get-tuple-element.44), channel_id=1, source_target_pairs={{0,28},{1,29},{32,60},{33,61},{64,92},{65,93},{96,124},{97,125},{1... | collective-permute-start | bytes 786440 | tf_op jit(solution)/shard_map/panel_scatter/ppermute | solution.py:54
  27.5 1.0 collective-permute-start.7
  28.6 1.1 constant_dynamic-slice_fusion.4
  29.7 5.6 %collective-permute-done.6 = f32[256,256]{1,0:T(8,128)} collective-permute-done((f32[256,256]{1,0:T(8,128)S(1)}, f32[256,256]{1,0:T(8,128)}, u32[]{:S(2)}, u32[]{:S(2)}) %collective-permute-start.6) | collective-permute-done | bytes 262176 | tf_op jit(solution)/shard_map/panel_scatter/ppermute | solution.py:54
  35.4 1.1 select_select_fusion.2
  36.6 1.4 %collective-permute-start.11 = (f32[128,512]{1,0:T(8,128)S(1)}, f32[128,512]{1,0:T(8,128)S(1)}, u32[]{:S(2)}, u32[]{:S(2)}) collective-permute-start(f32[128,512]{1,0:T(8,128)S(1)} %pad_maximum_fusion.3), channel_id=1, source_target_pairs={{0,64},{32,96},{64,128},{96,160},{128,192},{160,224},{192,0},{224,... | collective-permute-start | bytes 786440 | tf_op jit(solution)/shard_map/top_exchange/ppermute | solution.py:250
  38.0 2.7 %collective-permute-start.12 = (f32[128,512]{1,0:T(8,128)S(1)}, f32[128,512]{1,0:T(8,128)S(1)}, u32[]{:S(2)}, u32[]{:S(2)}) collective-permute-start(f32[128,512]{1,0:T(8,128)S(1)} %pad_maximum_fusion.4), channel_id=1, source_target_pairs={{0,128},{32,160},{64,192},{96,224},{128,0},{160,32},{192,64},{224,... | collective-permute-start | bytes 786440 | tf_op jit(solution)/shard_map/top_exchange/ppermute | solution.py:250
  40.8 1.1 collective-permute-start.13
  41.9 1.9 %collective-permute-start.10 = (f32[256,256]{1,0:T(8,128)S(1)}, f32[256,256]{1,0:T(8,128)S(1)}, u32[]{:S(2)}, u32[]{:S(2)}) collective-permute-start(f32[256,256]{1,0:T(8,128)S(1)} %select_select_fusion.2), channel_id=1, source_target_pairs={{0,3},{4,7},{8,11},{12,15},{16,19},{20,23},{24,27},{28,31},{1,0},{... | collective-permute-start | bytes 786440 | tf_op jit(solution)/shard_map/panel_across/ppermute | solution.py:77
  43.8 3.4 %collective-permute-start.8 = (f32[256,256]{1,0:T(8,128)S(1)}, f32[256,256]{1,0:T(8,128)S(1)}, u32[]{:S(2)}, u32[]{:S(2)}) collective-permute-start(f32[256,256]{1,0:T(8,128)S(1)} %select_select_fusion.2), channel_id=1, source_target_pairs={{0,1},{4,5},{8,9},{12,13},{16,17},{20,21},{24,25},{28,29},{1,2},{5... | collective-permute-start | bytes 786440 | tf_op jit(solution)/shard_map/panel_across/ppermute | solution.py:76
  47.2 1.3 collective-permute-start.9
  48.5 2.5 %collective-permute-done.12 = f32[128,512]{1,0:T(8,128)S(1)} collective-permute-done((f32[128,512]{1,0:T(8,128)S(1)}, f32[128,512]{1,0:T(8,128)S(1)}, u32[]{:S(2)}, u32[]{:S(2)}) %collective-permute-start.12) | collective-permute-done | bytes 262176 | tf_op jit(solution)/shard_map/top_exchange/ppermute | solution.py:250
  51.0 1.0 slice_add_fusion
  52.1 3.7 %collective-permute-done.9 = f32[256,256]{1,0:T(8,128)S(1)} collective-permute-done((f32[256,256]{1,0:T(8,128)S(1)}, f32[256,256]{1,0:T(8,128)S(1)}, u32[]{:S(2)}, u32[]{:S(2)}) %collective-permute-start.9) | collective-permute-done | bytes 262176 | tf_op jit(solution)/shard_map/panel_across/ppermute | solution.py:78
  56.0 3.7 %collective-permute-start.28 = (f32[256,512]{1,0:T(8,128)S(1)}, f32[256,512]{1,0:T(8,128)S(1)}, u32[]{:S(2)}, u32[]{:S(2)}) collective-permute-start(f32[256,512]{1,0:T(8,128)S(1)} %pad_maximum_fusion.2.rest_0_), channel_id=1, source_target_pairs={{0,28},{1,29},{2,30},{3,31},{4,0},{5,1},{6,2},{7,3},{8,4},{9,5},{1... | collective-permute-start | bytes 1572872 | tf_op jit(solution)/shard_map/panel_ring/ppermute | solution.py:259
  59.7 1.3 collective-permute-start.14
  61.1 5.5 %collective-permute-done.14 = f32[128,256]{1,0:T(8,128)S(1)} collective-permute-done((f32[128,256]{1,0:T(8,128)S(1)}, f32[128,256]{1,0:T(8,128)S(1)}, u32[]{:S(2)}, u32[]{:S(2)}) %collective-permute-start.14) | collective-permute-done | bytes 131104 | tf_op jit(solution)/shard_map/fix_down/ppermute | solution.py:59
  66.7 1.3 collective-permute-start.15
  68.0 1.3 collective-permute-start.16
  69.3 1.3 collective-permute-start.17
  70.6 1.0 select_reduce_fusion
  72.0 1.4 %copy.8 = s32[2048,1]{1,0:T(8,128)} copy(s32[2048,1]{0,1:T(1,128)S(1)} %bitcast.30) | data formatting | bytes 16384 | tf_op jit(solution)/shard_map/reduce_sum | solution.py:226
  73.8 1.4 %collective-permute-start.23 = (f32[128,512]{1,0:T(8,128)S(1)}, f32[128,512]{1,0:T(8,128)S(1)}, u32[]{:S(2)}, u32[]{:S(2)}) collective-permute-start(f32[128,512]{1,0:T(8,128)S(1)} %pad_maximum_fusion.6), channel_id=1, source_target_pairs={{0,128},{32,160},{64,192},{96,224},{128,0},{160,32},{192,64},{224,... | collective-permute-start | bytes 786440 | tf_op jit(solution)/shard_map/top_gather/ppermute | solution.py:85
  75.2 1.1 collective-permute-start.24
  76.3 2.7 %collective-permute-start.29 = (f32[256,512]{1,0:T(8,128)S(1)}, f32[256,512]{1,0:T(8,128)S(1)}, u32[]{:S(2)}, u32[]{:S(2)}) collective-permute-start(f32[256,512]{1,0:T(8,128)S(1)} %collective-permute-done.28.rest_2_), channel_id=1, source_target_pairs={{0,28},{1,29},{2,30},{3,31},{4,0},{5,1},{6,2},{7,3},{8,4},{9,5},{1... | collective-permute-start | bytes 1572872 | tf_op jit(solution)/shard_map/panel_ring/ppermute | solution.py:259
  78.9 1.6 %fusion.13.origin = s32[2048,1]{1,0:T(8,128)S(1)} fusion(s32[2048,1]{1,0:T(8,128)} %copy.8, s32[2048,1]{1,0:T(8,128)S(1)} %copy.10, s32[]{:T(128)} %axis_index.23), kind=kLoop, calls=%fused_computation.21 | loop fusion | flops 43008 | bytes 24580 | tf_op jit(solution)/shard_map/sub | solution.py:228
  80.6 2.0 %collective-permute-done.22 = f32[128,512]{1,0:T(8,128)S(1)} collective-permute-done((f32[128,512]{1,0:T(8,128)S(1)}, f32[128,512]{1,0:T(8,128)S(1)}, u32[]{:S(2)}, u32[]{:S(2)}) %collective-permute-start.22) | collective-permute-done | bytes 262176 | tf_op jit(solution)/shard_map/top_gather/ppermute | solution.py:85
  82.6 1.3 collective-permute-start.19
  83.9 1.3 collective-permute-start.20
  85.2 1.9 %collective-permute-start.21 = (f32[128,256]{1,0:T(8,128)S(1)}, f32[128,256]{1,0:T(8,128)S(1)}, u32[]{:S(2)}, u32[]{:S(2)}) collective-permute-start(f32[128,256]{1,0:T(8,128)S(1)} %select_select_fusion.5), channel_id=1, source_target_pairs={{0,3},{4,7},{8,11},{12,15},{16,19},{20,23},{24,27},{28,31},{1,0},{... | collective-permute-start | bytes 393224 | tf_op jit(solution)/shard_map/fix_across/ppermute | solution.py:77
  87.4 2.7 %collective-permute-start.30 = (f32[256,512]{1,0:T(8,128)S(1)}, f32[256,512]{1,0:T(8,128)S(1)}, u32[]{:S(2)}, u32[]{:S(2)}) collective-permute-start(f32[256,512]{1,0:T(8,128)S(1)} %collective-permute-done.29.rest_4_), channel_id=1, source_target_pairs={{0,28},{1,29},{2,30},{3,31},{4,0},{5,1},{6,2},{7,3},{8,4},{9,5},{1... | collective-permute-start | bytes 1572872 | tf_op jit(solution)/shard_map/panel_ring/ppermute | solution.py:259
  90.0 1.2 collective-permute-done.21
  92.8 1.7 %collective-permute-start.33 = (f32[128,512]{1,0:T(8,128)S(1)}, f32[128,512]{1,0:T(8,128)S(1)}, u32[]{:S(2)}, u32[]{:S(2)}) collective-permute-start(f32[128,512]{1,0:T(8,128)S(1)} %pad_maximum_fusion.7), channel_id=1, source_target_pairs={{0,192},{32,224},{64,0},{96,32},{128,64},{160,96},{192,128},{224,1... | collective-permute-start | bytes 786440 | tf_op jit(solution)/shard_map/fix_gather/ppermute | solution.py:85
  94.5 6.1 %collective-permute-done.31 = f32[128,512]{1,0:T(8,128)S(1)} collective-permute-done((f32[128,512]{1,0:T(8,128)S(1)}, f32[128,512]{1,0:T(8,128)S(1)}, u32[]{:S(2)}, u32[]{:S(2)}) %collective-permute-start.31) | collective-permute-done | bytes 262176 | tf_op jit(solution)/shard_map/fix_gather/ppermute | solution.py:85
  100.6 12.9 %collective-permute-start.26 = (f32[4,128,512]{2,1,0:T(8,128)S(1)}, f32[4,128,512]{2,1,0:T(8,128)S(1)}, u32[]{:S(2)}, u32[]{:S(2)}) collective-permute-start(f32[4,128,512]{2,1,0:T(8,128)S(1)} %pad_maximum_fusion.top_mine), channel_id=1, source_target_pairs={{0,32},{32,0},{64,96},{96,64},{128,160},{160,128},{192,224},{224,1... | collective-permute-start | bytes 3145736 | tf_op jit(solution)/shard_map/core_gather/ppermute | solution.py:282
  113.6 1.0 collective-permute-start.34
  114.8 3.0 %collective-permute-start.36 = (f32[128,512]{1,0:T(8,128)S(1)}, f32[128,512]{1,0:T(8,128)S(1)}, u32[]{:S(2)}, u32[]{:S(2)}) collective-permute-start(f32[128,512]{1,0:T(8,128)S(1)} %slice.89), channel_id=1, source_target_pairs={{0,28},{1,29},{2,30},{3,31},{4,0},{5,1},{6,2},{7,3},{8,4},{9,5},{1... | collective-permute-start | bytes 786440 | tf_op jit(solution)/shard_map/panel_ring/ppermute | solution.py:259
  117.8 4.1 %factor.1 = (bf16[512,512]{1,0:T(8,128)(2,1)S(1)}, bf16[512,512]{1,0:T(8,128)(2,1)S(1)}, bf16[512,512]{1,0:T(8,128)(2,1)S(1)}, bf16[512,512]{1,0:T(8,128)(2,1)S(1)}, f32[256,512]{1,0:T(8,128)S(1)}) custom-call(s32[4]{0:T(128)S(1)} %pad_add_fusion.2.ids, f32[4,128,512]{2,1,0:T(8,128)S(1)} %pad_maximum_fusion.top_mine, ...), custom_call_target="tpu_custom_call" | custom-call | flops 3000000000 | bytes 8388608 | tf_op jit(solution)/shard_map/factor/pallas_call | solution.py:292
  121.8 2.1 %collective-permute-done.35.rest_7_ = f32[128,512]{1,0:T(8,128)S(1)} collective-permute-done((f32[128,512]{1,0:T(8,128)S(1)}, f32[128,512]{1,0:T(8,128)S(1)}, u32[]{:S(2)}, u32[]{:S(2)}) %collective-permute-start.35) | collective-permute-done | bytes 262176 | tf_op jit(solution)/shard_map/panel_ring/ppermute | solution.py:258
  123.9 9.1 %update.1 = f32[2048,512]{1,0:T(8,128)} custom-call(s32[4]{0:T(128)S(1)} %pad_add_fusion.2.ids, s32[2048,1]{1,0:T(8,128)S(1)} %fusion.13.origin, bf16[512,512]{1,0:T(8,128)(2,1)S(1)} %get-tuple-element.32.factor_high, bf16[512,512]{1,0:T(8,128)(2,1)S(1)} %get-tuple-element.33.factor_low, bf16[512,512]{1,0:T(8,128)(2,1)S(1)} %get-tuple-element.34.moved_high, ...), custom_call_target="tpu_custom_call" | custom-call | flops 6000000000 | bytes 14680064 | tf_op jit(solution)/shard_map/update/pallas_call | solution.py:304
  (74 shorter events, 4.1 us)
Async XLA Ops:
  0.0 18.8 %copy-start.2 = (s32[2,256]{1,0:T(2,128)S(1)}, s32[2,256]{1,0:T(2,128)}, u32[]{:S(2)}) copy-start(s32[2,256]{1,0:T(2,128)} %param.5) | copy-start | bytes 6148
  2.4 21.1 %collective-permute-start = (f32[256,256]{1,0:T(8,128)}, f32[256,256]{1,0:T(8,128)}, u32[]{:S(2)}, u32[]{:S(2)}) collective-permute-start(f32[256,256]{1,0:T(8,128)} %get-tuple-element.50), channel_id=1, source_target_pairs={{0,4},{1,5},{32,36},{33,37},{64,68},{65,69},{96,100},{97,101},{128... | collective-permute-start | bytes 786440 | tf_op jit(solution)/shard_map/panel_scatter/ppermute | solution.py:54
  7.5 18.0 %collective-permute-start.1 = (f32[256,256]{1,0:T(8,128)}, f32[256,256]{1,0:T(8,128)}, u32[]{:S(2)}, u32[]{:S(2)}) collective-permute-start(f32[256,256]{1,0:T(8,128)} %get-tuple-element.49), channel_id=1, source_target_pairs={{0,8},{1,9},{32,40},{33,41},{64,72},{65,73},{96,104},{97,105},{128... | collective-permute-start | bytes 786440 | tf_op jit(solution)/shard_map/panel_scatter/ppermute | solution.py:54
  10.2 17.3 %collective-permute-start.2 = (f32[256,256]{1,0:T(8,128)S(1)}, f32[256,256]{1,0:T(8,128)}, u32[]{:S(2)}, u32[]{:S(2)}) collective-permute-start(f32[256,256]{1,0:T(8,128)S(1)} %get-tuple-element.48), channel_id=1, source_target_pairs={{0,12},{1,13},{32,44},{33,45},{64,76},{65,77},{96,108},{97,109},{1... | collective-permute-start | bytes 786440 | tf_op jit(solution)/shard_map/panel_scatter/ppermute | solution.py:54
  12.9 16.7 %collective-permute-start.3 = (f32[256,256]{1,0:T(8,128)S(1)}, f32[256,256]{1,0:T(8,128)}, u32[]{:S(2)}, u32[]{:S(2)}) collective-permute-start(f32[256,256]{1,0:T(8,128)S(1)} %get-tuple-element.47), channel_id=1, source_target_pairs={{0,16},{1,17},{32,48},{33,49},{64,80},{65,81},{96,112},{97,113},{1... | collective-permute-start | bytes 786440 | tf_op jit(solution)/shard_map/panel_scatter/ppermute | solution.py:54
  16.8 12.8 %collective-permute-start.4 = (f32[256,256]{1,0:T(8,128)S(1)}, f32[256,256]{1,0:T(8,128)}, u32[]{:S(2)}, u32[]{:S(2)}) collective-permute-start(f32[256,256]{1,0:T(8,128)S(1)} %get-tuple-element.46), channel_id=1, source_target_pairs={{0,20},{1,21},{32,52},{33,53},{64,84},{65,85},{96,116},{97,117},{1... | collective-permute-start | bytes 786440 | tf_op jit(solution)/shard_map/panel_scatter/ppermute | solution.py:54
  23.5 6.3 %collective-permute-start.5 = (f32[256,256]{1,0:T(8,128)S(1)}, f32[256,256]{1,0:T(8,128)}, u32[]{:S(2)}, u32[]{:S(2)}) collective-permute-start(f32[256,256]{1,0:T(8,128)S(1)} %get-tuple-element.45), channel_id=1, source_target_pairs={{0,24},{1,25},{32,56},{33,57},{64,88},{65,89},{96,120},{97,121},{1... | collective-permute-start | bytes 786440 | tf_op jit(solution)/shard_map/panel_scatter/ppermute | solution.py:54
  25.5 9.9 %collective-permute-start.6 = (f32[256,256]{1,0:T(8,128)S(1)}, f32[256,256]{1,0:T(8,128)}, u32[]{:S(2)}, u32[]{:S(2)}) collective-permute-start(f32[256,256]{1,0:T(8,128)S(1)} %get-tuple-element.44), channel_id=1, source_target_pairs={{0,28},{1,29},{32,60},{33,61},{64,92},{65,93},{96,124},{97,125},{1... | collective-permute-start | bytes 786440 | tf_op jit(solution)/shard_map/panel_scatter/ppermute | solution.py:54
  27.5 8.9 %collective-permute-start.7 = (f32[256,512]{1,0:T(8,128)S(1)}, f32[256,512]{1,0:T(8,128)S(1)}, u32[]{:S(2)}, u32[]{:S(2)}) collective-permute-start(f32[256,512]{1,0:T(8,128)S(1)} %constant_dynamic-slice_fusion.6), channel_id=1, source_target_pairs={{0,32},{32,0},{64,96},{96,64},{128,160},{160,128},{192,224},{224,1... | collective-permute-start | bytes 1572872 | tf_op jit(solution)/shard_map/top_exchange/ppermute | solution.py:238
  36.6 10.6 %collective-permute-start.11 = (f32[128,512]{1,0:T(8,128)S(1)}, f32[128,512]{1,0:T(8,128)S(1)}, u32[]{:S(2)}, u32[]{:S(2)}) collective-permute-start(f32[128,512]{1,0:T(8,128)S(1)} %pad_maximum_fusion.3), channel_id=1, source_target_pairs={{0,64},{32,96},{64,128},{96,160},{128,192},{160,224},{192,0},{224,... | collective-permute-start | bytes 786440 | tf_op jit(solution)/shard_map/top_exchange/ppermute | solution.py:250
  38.0 13.0 %collective-permute-start.12 = (f32[128,512]{1,0:T(8,128)S(1)}, f32[128,512]{1,0:T(8,128)S(1)}, u32[]{:S(2)}, u32[]{:S(2)}) collective-permute-start(f32[128,512]{1,0:T(8,128)S(1)} %pad_maximum_fusion.4), channel_id=1, source_target_pairs={{0,128},{32,160},{64,192},{96,224},{128,0},{160,32},{192,64},{224,... | collective-permute-start | bytes 786440 | tf_op jit(solution)/shard_map/top_exchange/ppermute | solution.py:250
  40.8 10.3 %collective-permute-start.13 = (f32[128,512]{1,0:T(8,128)S(1)}, f32[128,512]{1,0:T(8,128)S(1)}, u32[]{:S(2)}, u32[]{:S(2)}) collective-permute-start(f32[128,512]{1,0:T(8,128)S(1)} %pad_maximum_fusion.5), channel_id=1, source_target_pairs={{0,192},{32,224},{64,0},{96,32},{128,64},{160,96},{192,128},{224,1... | collective-permute-start | bytes 786440 | tf_op jit(solution)/shard_map/top_exchange/ppermute | solution.py:250
  41.9 10.1 %collective-permute-start.10 = (f32[256,256]{1,0:T(8,128)S(1)}, f32[256,256]{1,0:T(8,128)S(1)}, u32[]{:S(2)}, u32[]{:S(2)}) collective-permute-start(f32[256,256]{1,0:T(8,128)S(1)} %select_select_fusion.2), channel_id=1, source_target_pairs={{0,3},{4,7},{8,11},{12,15},{16,19},{20,23},{24,27},{28,31},{1,0},{... | collective-permute-start | bytes 786440 | tf_op jit(solution)/shard_map/panel_across/ppermute | solution.py:77
  43.8 8.2 %collective-permute-start.8 = (f32[256,256]{1,0:T(8,128)S(1)}, f32[256,256]{1,0:T(8,128)S(1)}, u32[]{:S(2)}, u32[]{:S(2)}) collective-permute-start(f32[256,256]{1,0:T(8,128)S(1)} %select_select_fusion.2), channel_id=1, source_target_pairs={{0,1},{4,5},{8,9},{12,13},{16,17},{20,21},{24,25},{28,29},{1,2},{5... | collective-permute-start | bytes 786440 | tf_op jit(solution)/shard_map/panel_across/ppermute | solution.py:76
  47.2 8.5 %collective-permute-start.9 = (f32[256,256]{1,0:T(8,128)S(1)}, f32[256,256]{1,0:T(8,128)S(1)}, u32[]{:S(2)}, u32[]{:S(2)}) collective-permute-start(f32[256,256]{1,0:T(8,128)S(1)} %select_select_fusion.2), channel_id=1, source_target_pairs={{0,2},{4,6},{8,10},{12,14},{16,18},{20,22},{24,26},{28,30},{1,3},{... | collective-permute-start | bytes 786440 | tf_op jit(solution)/shard_map/panel_across/ppermute | solution.py:78
  55.9 20.4 %collective-permute-start.18 = (f32[256,512]{1,0:T(8,128)S(1)}, f32[256,512]{1,0:T(8,128)S(1)}, u32[]{:S(2)}, u32[]{:S(2)}) collective-permute-start(f32[256,512]{1,0:T(8,128)S(1)} %pad_maximum_fusion.2.rest_0_), channel_id=1, source_target_pairs={{0,4},{1,5},{2,6},{3,7},{4,8},{5,9},{6,10},{7,11},{8,12},{9,13},{1... | collective-permute-start | bytes 1572872 | tf_op jit(solution)/shard_map/panel_ring/ppermute | solution.py:258
  56.0 20.3 %collective-permute-start.28 = (f32[256,512]{1,0:T(8,128)S(1)}, f32[256,512]{1,0:T(8,128)S(1)}, u32[]{:S(2)}, u32[]{:S(2)}) collective-permute-start(f32[256,512]{1,0:T(8,128)S(1)} %pad_maximum_fusion.2.rest_0_), channel_id=1, source_target_pairs={{0,28},{1,29},{2,30},{3,31},{4,0},{5,1},{6,2},{7,3},{8,4},{9,5},{1... | collective-permute-start | bytes 1572872 | tf_op jit(solution)/shard_map/panel_ring/ppermute | solution.py:259
  59.7 7.0 %collective-permute-start.14 = (f32[128,256]{1,0:T(8,128)S(1)}, f32[128,256]{1,0:T(8,128)S(1)}, u32[]{:S(2)}, u32[]{:S(2)}) collective-permute-start(f32[128,256]{1,0:T(8,128)S(1)} %slice.85), channel_id=1, source_target_pairs={{0,16},{1,17},{32,48},{33,49},{64,80},{65,81},{96,112},{97,113},{1... | collective-permute-start | bytes 393224 | tf_op jit(solution)/shard_map/fix_down/ppermute | solution.py:59
  66.7 6.7 %collective-permute-start.15 = (f32[128,256]{1,0:T(8,128)S(1)}, f32[128,256]{1,0:T(8,128)S(1)}, u32[]{:S(2)}, u32[]{:S(2)}) collective-permute-start(f32[128,256]{1,0:T(8,128)S(1)} %broadcast_select_fusion.1), channel_id=1, source_target_pairs={{0,4},{1,5},{16,12},{17,13},{32,36},{33,37},{48,44},{49,45},{64,68... | collective-permute-start | bytes 393224 | tf_op jit(solution)/shard_map/fix_down/ppermute | solution.py:59
  68.0 5.8 %collective-permute-start.16 = (f32[128,256]{1,0:T(8,128)S(1)}, f32[128,256]{1,0:T(8,128)S(1)}, u32[]{:S(2)}, u32[]{:S(2)}) collective-permute-start(f32[128,256]{1,0:T(8,128)S(1)} %broadcast_select_fusion.1), channel_id=1, source_target_pairs={{0,8},{1,9},{16,24},{17,25},{32,40},{33,41},{48,56},{49,57},{64,72... | collective-permute-start | bytes 393224 | tf_op jit(solution)/shard_map/fix_down/ppermute | solution.py:59
  69.3 5.9 %collective-permute-start.17 = (f32[128,256]{1,0:T(8,128)S(1)}, f32[128,256]{1,0:T(8,128)S(1)}, u32[]{:S(2)}, u32[]{:S(2)}) collective-permute-start(f32[128,256]{1,0:T(8,128)S(1)} %broadcast_select_fusion.1), channel_id=1, source_target_pairs={{0,28},{1,29},{16,20},{17,21},{32,60},{33,61},{48,52},{49,53},{64,... | collective-permute-start | bytes 393224 | tf_op jit(solution)/shard_map/fix_down/ppermute | solution.py:59
  73.4 9.2 %collective-permute-start.22 = (f32[128,512]{1,0:T(8,128)S(1)}, f32[128,512]{1,0:T(8,128)S(1)}, u32[]{:S(2)}, u32[]{:S(2)}) collective-permute-start(f32[128,512]{1,0:T(8,128)S(1)} %pad_maximum_fusion.6), channel_id=1, source_target_pairs={{0,64},{32,96},{64,128},{96,160},{128,192},{160,224},{192,0},{224,... | collective-permute-start | bytes 786440 | tf_op jit(solution)/shard_map/top_gather/ppermute | solution.py:85
  73.8 10.1 %collective-permute-start.23 = (f32[128,512]{1,0:T(8,128)S(1)}, f32[128,512]{1,0:T(8,128)S(1)}, u32[]{:S(2)}, u32[]{:S(2)}) collective-permute-start(f32[128,512]{1,0:T(8,128)S(1)} %pad_maximum_fusion.6), channel_id=1, source_target_pairs={{0,128},{32,160},{64,192},{96,224},{128,0},{160,32},{192,64},{224,... | collective-permute-start | bytes 786440 | tf_op jit(solution)/shard_map/top_gather/ppermute | solution.py:85
  75.2 10.0 %collective-permute-start.24 = (f32[128,512]{1,0:T(8,128)S(1)}, f32[128,512]{1,0:T(8,128)S(1)}, u32[]{:S(2)}, u32[]{:S(2)}) collective-permute-start(f32[128,512]{1,0:T(8,128)S(1)} %pad_maximum_fusion.6), channel_id=1, source_target_pairs={{0,192},{32,224},{64,0},{96,32},{128,64},{160,96},{192,128},{224,1... | collective-permute-start | bytes 786440 | tf_op jit(solution)/shard_map/top_gather/ppermute | solution.py:85
  76.2 11.0 %collective-permute-start.25 = (f32[256,512]{1,0:T(8,128)S(1)}, f32[256,512]{1,0:T(8,128)S(1)}, u32[]{:S(2)}, u32[]{:S(2)}) collective-permute-start(f32[256,512]{1,0:T(8,128)S(1)} %collective-permute-done.18.rest_1_), channel_id=1, source_target_pairs={{0,4},{1,5},{2,6},{3,7},{4,8},{5,9},{6,10},{7,11},{8,12},{9,13},{1... | collective-permute-start | bytes 1572872 | tf_op jit(solution)/shard_map/panel_ring/ppermute | solution.py:258
  76.3 11.1 %collective-permute-start.29 = (f32[256,512]{1,0:T(8,128)S(1)}, f32[256,512]{1,0:T(8,128)S(1)}, u32[]{:S(2)}, u32[]{:S(2)}) collective-permute-start(f32[256,512]{1,0:T(8,128)S(1)} %collective-permute-done.28.rest_2_), channel_id=1, source_target_pairs={{0,28},{1,29},{2,30},{3,31},{4,0},{5,1},{6,2},{7,3},{8,4},{9,5},{1... | collective-permute-start | bytes 1572872 | tf_op jit(solution)/shard_map/panel_ring/ppermute | solution.py:259
  82.6 7.4 %collective-permute-start.19 = (f32[128,256]{1,0:T(8,128)S(1)}, f32[128,256]{1,0:T(8,128)S(1)}, u32[]{:S(2)}, u32[]{:S(2)}) collective-permute-start(f32[128,256]{1,0:T(8,128)S(1)} %select_select_fusion.5), channel_id=1, source_target_pairs={{0,1},{4,5},{8,9},{12,13},{16,17},{20,21},{24,25},{28,29},{1,2},{5... | collective-permute-start | bytes 393224 | tf_op jit(solution)/shard_map/fix_across/ppermute | solution.py:76
  83.9 6.1 %collective-permute-start.20 = (f32[128,256]{1,0:T(8,128)S(1)}, f32[128,256]{1,0:T(8,128)S(1)}, u32[]{:S(2)}, u32[]{:S(2)}) collective-permute-start(f32[128,256]{1,0:T(8,128)S(1)} %select_select_fusion.5), channel_id=1, source_target_pairs={{0,2},{4,6},{8,10},{12,14},{16,18},{20,22},{24,26},{28,30},{1,3},{... | collective-permute-start | bytes 393224 | tf_op jit(solution)/shard_map/fix_across/ppermute | solution.py:78
  85.2 6.0 %collective-permute-start.21 = (f32[128,256]{1,0:T(8,128)S(1)}, f32[128,256]{1,0:T(8,128)S(1)}, u32[]{:S(2)}, u32[]{:S(2)}) collective-permute-start(f32[128,256]{1,0:T(8,128)S(1)} %select_select_fusion.5), channel_id=1, source_target_pairs={{0,3},{4,7},{8,11},{12,15},{16,19},{20,23},{24,27},{28,31},{1,0},{... | collective-permute-start | bytes 393224 | tf_op jit(solution)/shard_map/fix_across/ppermute | solution.py:77
  87.2 30.5 %copy-start = (f32[2,256,256]{2,1,0:T(8,128)S(1)}, f32[2,256,256]{2,1,0:T(8,128)}, u32[]{:S(2)}) copy-start(f32[2,256,256]{2,1,0:T(8,128)} %lower_inverse.1) | copy-start | bytes 1572868
  87.2 30.5 %copy-start.1 = (f32[2,256,256]{2,1,0:T(8,128)S(1)}, f32[2,256,256]{2,1,0:T(8,128)}, u32[]{:S(2)}) copy-start(f32[2,256,256]{2,1,0:T(8,128)} %upper_inverse.1) | copy-start | bytes 1572868
  87.3 26.3 %collective-permute-start.27 = (f32[256,512]{1,0:T(8,128)S(1)}, f32[256,512]{1,0:T(8,128)S(1)}, u32[]{:S(2)}, u32[]{:S(2)}) collective-permute-start(f32[256,512]{1,0:T(8,128)S(1)} %collective-permute-done.25.rest_3_), channel_id=1, source_target_pairs={{0,4},{1,5},{2,6},{3,7},{4,8},{5,9},{6,10},{7,11},{8,12},{9,13},{1... | collective-permute-start | bytes 1572872 | tf_op jit(solution)/shard_map/panel_ring/ppermute | solution.py:258
  87.4 26.2 %collective-permute-start.30 = (f32[256,512]{1,0:T(8,128)S(1)}, f32[256,512]{1,0:T(8,128)S(1)}, u32[]{:S(2)}, u32[]{:S(2)}) collective-permute-start(f32[256,512]{1,0:T(8,128)S(1)} %collective-permute-done.29.rest_4_), channel_id=1, source_target_pairs={{0,28},{1,29},{2,30},{3,31},{4,0},{5,1},{6,2},{7,3},{8,4},{9,5},{1... | collective-permute-start | bytes 1572872 | tf_op jit(solution)/shard_map/panel_ring/ppermute | solution.py:259
  91.3 9.3 %collective-permute-start.31 = (f32[128,512]{1,0:T(8,128)S(1)}, f32[128,512]{1,0:T(8,128)S(1)}, u32[]{:S(2)}, u32[]{:S(2)}) collective-permute-start(f32[128,512]{1,0:T(8,128)S(1)} %pad_maximum_fusion.7), channel_id=1, source_target_pairs={{0,64},{32,96},{64,128},{96,160},{128,192},{160,224},{192,0},{224,... | collective-permute-start | bytes 786440 | tf_op jit(solution)/shard_map/fix_gather/ppermute | solution.py:85
  92.0 21.5 %collective-permute-start.32 = (f32[128,512]{1,0:T(8,128)S(1)}, f32[128,512]{1,0:T(8,128)S(1)}, u32[]{:S(2)}, u32[]{:S(2)}) collective-permute-start(f32[128,512]{1,0:T(8,128)S(1)} %pad_maximum_fusion.7), channel_id=1, source_target_pairs={{0,128},{32,160},{64,192},{96,224},{128,0},{160,32},{192,64},{224,... | collective-permute-start | bytes 786440 | tf_op jit(solution)/shard_map/fix_gather/ppermute | solution.py:85
  92.8 20.7 %collective-permute-start.33 = (f32[128,512]{1,0:T(8,128)S(1)}, f32[128,512]{1,0:T(8,128)S(1)}, u32[]{:S(2)}, u32[]{:S(2)}) collective-permute-start(f32[128,512]{1,0:T(8,128)S(1)} %pad_maximum_fusion.7), channel_id=1, source_target_pairs={{0,192},{32,224},{64,0},{96,32},{128,64},{160,96},{192,128},{224,1... | collective-permute-start | bytes 786440 | tf_op jit(solution)/shard_map/fix_gather/ppermute | solution.py:85
  100.6 17.1 %collective-permute-start.26 = (f32[4,128,512]{2,1,0:T(8,128)S(1)}, f32[4,128,512]{2,1,0:T(8,128)S(1)}, u32[]{:S(2)}, u32[]{:S(2)}) collective-permute-start(f32[4,128,512]{2,1,0:T(8,128)S(1)} %pad_maximum_fusion.top_mine), channel_id=1, source_target_pairs={{0,32},{32,0},{64,96},{96,64},{128,160},{160,128},{192,224},{224,1... | collective-permute-start | bytes 3145736 | tf_op jit(solution)/shard_map/core_gather/ppermute | solution.py:282
  113.6 4.2 %collective-permute-start.34 = (f32[4,128,512]{2,1,0:T(8,128)S(1)}, f32[4,128,512]{2,1,0:T(8,128)S(1)}, u32[]{:S(2)}, u32[]{:S(2)}) collective-permute-start(f32[4,128,512]{2,1,0:T(8,128)S(1)} %pad_maximum_fusion.1.fix_mine), channel_id=1, source_target_pairs={{0,32},{32,0},{64,96},{96,64},{128,160},{160,128},{192,224},{224,1... | collective-permute-start | bytes 3145736 | tf_op jit(solution)/shard_map/core_gather/ppermute | solution.py:283
  114.7 9.2 %collective-permute-start.35 = (f32[128,512]{1,0:T(8,128)S(1)}, f32[128,512]{1,0:T(8,128)S(1)}, u32[]{:S(2)}, u32[]{:S(2)}) collective-permute-start(f32[128,512]{1,0:T(8,128)S(1)} %slice.88), channel_id=1, source_target_pairs={{0,4},{1,5},{2,6},{3,7},{4,8},{5,9},{6,10},{7,11},{8,12},{9,13},{1... | collective-permute-start | bytes 786440 | tf_op jit(solution)/shard_map/panel_ring/ppermute | solution.py:258
  114.8 9.1 %collective-permute-start.36 = (f32[128,512]{1,0:T(8,128)S(1)}, f32[128,512]{1,0:T(8,128)S(1)}, u32[]{:S(2)}, u32[]{:S(2)}) collective-permute-start(f32[128,512]{1,0:T(8,128)S(1)} %slice.89), channel_id=1, source_target_pairs={{0,28},{1,29},{2,30},{3,31},{4,0},{5,1},{6,2},{7,3},{8,4},{9,5},{1... | collective-permute-start | bytes 786440 | tf_op jit(solution)/shard_map/panel_ring/ppermute | solution.py:259

commit v4 on v3

--- a/solution.py
+++ b/solution.py
@@ -59,8 +59,11 @@
     return lax.ppermute(value, "pcol", [(at(a, x), at(b, x)) for a, b in pairs for x in (0, 1)])
 
 
-def spread_z(z, mine):
-    mine = jnp.where(z == 4, send_z(mine, [(0, 4)]), mine)
+def half_way_z(z, mine):
+    return jnp.where(z == 4, send_z(mine, [(0, 4)]), mine)
+
+
+def rest_of_z(z, mine):
     above = send_z(mine, [(0, 1), (4, 3)])
     below = send_z(mine, [(0, 7), (4, 5)])
     between = send_z(mine, [(0, 2), (4, 6)])
@@ -146,7 +149,7 @@
     ids, origin, factor_high, factor_low, moved_high, moved_low, head, *rest
 ):
     pieces = rest[: NZ + 1]
-    matrix, out, matrix_block, out_block, matrix_sem, out_sem = rest[NZ + 1 :]
+    matrix, out, out_block, out_sem = rest[NZ + 1 :]
     p, q = ids[0], ids[1]
     z = lax.div(q, NX)
     nb, width = head.shape
@@ -160,16 +163,9 @@
     def part(i):
         return pl.ds(i % 4 * nb, nb)
 
-    def matrix_copy(i):
-        return pltpu.make_async_copy(
-            matrix.at[place(i)], matrix_block.at[part(i)], matrix_sem.at[i % 4]
-        )
-
     def out_copy(i):
         return pltpu.make_async_copy(out_block.at[part(i)], out.at[place(i)], out_sem.at[i % 4])
 
-    for i in range(4):
-        matrix_copy(i).start()
     for i in range(0, NZ, 2):
         held = [pieces[i][...], pieces[i + 1][...]]
         if i + 2 == NZ:
@@ -184,16 +180,13 @@
         moved = one(chosen, moved_high[...]) + one(chosen, moved_low[...])
         for j in (i, i + 1):
             here = slice((j - i) * nb, (j - i + 1) * nb)
-            matrix_copy(j).wait()
             if j >= 4:
                 out_copy(j - 4).wait()
-            kept = jnp.where(drop, 0.0, matrix_block[part(j)]) - product[here]
+            kept = jnp.where(drop, 0.0, matrix[place(j), :]) - product[here]
             value = jnp.where(source[here] >= 0, moved[here], kept)
             is_head = jnp.logical_and(owners[j] == 0, p < 2)
             out_block[part(j)] = jnp.where(is_head, head[...], value)
             out_copy(j).start()
-            if j + 4 < NZ:
-                matrix_copy(j + 4).start()
     for i in range(NZ - 4, NZ):
         out_copy(i).wait()
 
@@ -261,10 +254,12 @@
 
     with jax.named_scope("panel_across"):
         piece = across_x(x, piece)
-    piece, slab, pivots = lax.optimization_barrier((piece, slab, pivots))
+    with jax.named_scope("fix_half"):
+        fix = half_way_z(z, slab[:, :nb])
+    piece, fix, pivots = lax.optimization_barrier((piece, fix, pivots))
     up1, down1 = ring(piece, piece)
     with jax.named_scope("fix_down"):
-        fix = spread_z(z, slab[:, :nb])
+        fix = rest_of_z(z, fix)
     origin = origin_of(pivots)
     fix, origin, _ = lax.optimization_barrier((fix, origin, up1))
     up2, down2 = ring(up1, down1)
@@ -294,7 +289,7 @@
             out_shape=[small] * 4 + [jax.ShapeDtypeStruct((nb, width), jnp.float32)],
             in_specs=[smem] + [vmem] * 6,
             out_specs=[vmem] * 5,
-            compiler_params=pltpu.CompilerParams(vmem_limit_bytes=24 * 1024 * 1024),
+            compiler_params=pltpu.CompilerParams(vmem_limit_bytes=16 * 1024 * 1024),
             cost_estimate=pl.CostEstimate(
                 flops=3 * 10**9, bytes_accessed=8 * 2**20, transcendentals=0
             ),
@@ -304,16 +299,16 @@
         return pl.pallas_call(
             update_kernel,
             out_shape=jax.ShapeDtypeStruct((rows, width), jnp.float32),
-            in_specs=[smem] + [vmem] * (6 + NZ + 1) + [hbm],
+            in_specs=[smem] + [vmem] * (6 + NZ + 2),
             out_specs=hbm,
-            scratch_shapes=[blocks] * 2 + [pltpu.SemaphoreType.DMA((4,))] * 2,
-            compiler_params=pltpu.CompilerParams(vmem_limit_bytes=24 * 1024 * 1024),
+            scratch_shapes=[blocks, pltpu.SemaphoreType.DMA((4,))],
+            compiler_params=pltpu.CompilerParams(vmem_limit_bytes=16 * 1024 * 1024),
             cost_estimate=pl.CostEstimate(
                 flops=6 * 10**9, bytes_accessed=14 * 2**20, transcendentals=0
             ),
         )(
             ids, origin, *parts, piece, up1, down1, up2, down2, up3, down3, up4, down4,
-            pltpu.with_memory_space_constraint(matrix, pltpu.HBM),
+            matrix,
         )
 
 

time: 134 us -> 128 us (0.955); the launches traced: 133 us -> 125 us
  waiting for transfers between devices: 28.8 us -> 16.6 us
  starting transfers between devices: 75.1 us -> 78.8 us
  other arithmetic: 5.94 us -> 7.51 us
    ppermute x6, waiting for transfers between devices: 8.07 us -> 1.37 us  [gather_y(): lax.ppermute(mine, 'prow', along_y(k))]
    ppermute x4, waiting for transfers between devices: 5.53 us -> 0.01 us  [send_z(): lax.ppermute(value, 'pcol', [(at(a, x), at(b, x)) for a, b in pairs for x...]
    ppermute x4, starting transfers between devices: 5.19 us -> 9.14 us  [send_z(): lax.ppermute(value, 'pcol', [(at(a, x), at(b, x)) for a, b in pairs for x...]
    ppermute x1, starting transfers between devices: 12.9 us -> 10.5 us  [on_device(): top_other = lax.ppermute(top_mine, 'prow', other_core())]
    ppermute x6, starting transfers between devices: 6.12 us -> 8.54 us  [gather_y(): lax.ppermute(mine, 'prow', along_y(k))]
    select_n x4 -> x5, other arithmetic: 1.23 us -> 3.13 us  [pick(): value = jnp.where(index == place, options[place], value)]
    ppermute x4, waiting for transfers between devices: 0.01 us -> 1.81 us  [ring(): lax.ppermute(down, 'pcol', along_z(-1))]
    ppermute x2, waiting for transfers between devices: 3.66 us -> 2.01 us  [across_x(): twice = lax.ppermute(mine, 'pcol', both(2, 3))]
  transfers between devices with their start and end apart: 37 -> 37, of which waited for: 9 -> 11; matrix products, arithmetic and copies ran while one was open for 10% -> 12% of each run, Pallas kernels for 3% -> 3%
where the time goes in v4:
time: 128 us; the launch traced here: 125 us
  starting transfers between devices  78.8 us (62%)
  waiting for transfers between devices  16.6 us (13%)
  Pallas kernels  12.2 us (10%)
  local copies, waits for them, and re-layouts  9.57 us (7%)
  other arithmetic  7.51 us (6%)
    ppermute x7, starting transfers between devices, scatter_z(): arrived.append(lax.ppermute(pieces[k], 'pcol', pairs))  20.4 us
    ppermute x4, starting transfers between devices, ring(): lax.ppermute(down, 'pcol', along_z(-1))  12.4 us
    ppermute x1, starting transfers between devices, on_device(): top_other = lax.ppermute(top_mine, 'prow', other_core())  10.5 us
    ppermute x4, starting transfers between devices, send_z(): lax.ppermute(value, 'pcol', [(at(a, x), at(b, x)) for a, b in pairs for x...  9.14 us
    ppermute x6, starting transfers between devices, gather_y(): lax.ppermute(mine, 'prow', along_y(k))  8.54 us
    pallas_call x1, Pallas kernels, on_device(): pl.pallas_call(update_kernel, out_shape=jax.ShapeDtypeStruct((rows, width...  8.1 us
    ppermute x7, waiting for transfers between devices, scatter_z(): arrived.append(lax.ppermute(pieces[k], 'pcol', pairs))  5.7 us
    ppermute x3, starting transfers between devices, on_device(): got = lax.ppermute(packed, 'prow', along_y(step))  5.23 us
  transfers between devices with their start and end apart: 37, of which 11 were waited for; matrix products, arithmetic and copies ran while one was open for 12% of the time, Pallas kernels for 3%

profile of v4, /device:TPU:1, one launch (start us, length us, event | category | flops | bytes accessed | tf_op | source)
XLA Modules:
  0.0 125.4 jit_solution(7323549258191266787)
XLA Ops:
  0.0 2.4 %fusion.35 = (f32[256,256]{1,0:T(8,128)S(1)}, f32[256,256]{1,0:T(8,128)S(1)}, f32[256,256]{1,0:T(8,128)S(1)}, f32[256,256]{1,0:T(8,128)S(1)}, f32[256,256]{1,0:T...) fusion(f32[2048,512]{1,0:T(8,128)} %rest_9_.1), kind=kLoop, calls=%fused_computation.106 | loop fusion | bytes 3670016 | tf_op jit(solution)/shard_map/panel_scatter/slice | solution.py:204
  2.4 5.1 %collective-permute-start = (f32[256,256]{1,0:T(8,128)}, f32[256,256]{1,0:T(8,128)}, u32[]{:S(2)}, u32[]{:S(2)}) collective-permute-start(f32[256,256]{1,0:T(8,128)} %get-tuple-element.50), channel_id=1, source_target_pairs={{0,4},{1,5},{32,36},{33,37},{64,68},{65,69},{96,100},{97,101},{128... | collective-permute-start | bytes 786440 | tf_op jit(solution)/shard_map/panel_scatter/ppermute | solution.py:54
  7.5 2.7 %collective-permute-start.1 = (f32[256,256]{1,0:T(8,128)}, f32[256,256]{1,0:T(8,128)}, u32[]{:S(2)}, u32[]{:S(2)}) collective-permute-start(f32[256,256]{1,0:T(8,128)} %get-tuple-element.49), channel_id=1, source_target_pairs={{0,8},{1,9},{32,40},{33,41},{64,72},{65,73},{96,104},{97,105},{128... | collective-permute-start | bytes 786440 | tf_op jit(solution)/shard_map/panel_scatter/ppermute | solution.py:54
  10.2 2.7 %collective-permute-start.2 = (f32[256,256]{1,0:T(8,128)S(1)}, f32[256,256]{1,0:T(8,128)}, u32[]{:S(2)}, u32[]{:S(2)}) collective-permute-start(f32[256,256]{1,0:T(8,128)S(1)} %get-tuple-element.48), channel_id=1, source_target_pairs={{0,12},{1,13},{32,44},{33,45},{64,76},{65,77},{96,108},{97,109},{1... | collective-permute-start | bytes 786440 | tf_op jit(solution)/shard_map/panel_scatter/ppermute | solution.py:54
  12.9 3.9 %collective-permute-start.3 = (f32[256,256]{1,0:T(8,128)S(1)}, f32[256,256]{1,0:T(8,128)}, u32[]{:S(2)}, u32[]{:S(2)}) collective-permute-start(f32[256,256]{1,0:T(8,128)S(1)} %get-tuple-element.47), channel_id=1, source_target_pairs={{0,16},{1,17},{32,48},{33,49},{64,80},{65,81},{96,112},{97,113},{1... | collective-permute-start | bytes 786440 | tf_op jit(solution)/shard_map/panel_scatter/ppermute | solution.py:54
  16.9 2.0 %collective-permute-start.4 = (f32[256,256]{1,0:T(8,128)S(1)}, f32[256,256]{1,0:T(8,128)}, u32[]{:S(2)}, u32[]{:S(2)}) collective-permute-start(f32[256,256]{1,0:T(8,128)S(1)} %get-tuple-element.46), channel_id=1, source_target_pairs={{0,20},{1,21},{32,52},{33,53},{64,84},{65,85},{96,116},{97,117},{1... | collective-permute-start | bytes 786440 | tf_op jit(solution)/shard_map/panel_scatter/ppermute | solution.py:54
  19.1 4.2 %gather_fusion = f32[512,512]{1,0:T(8,128)S(1)} fusion(f32[2048,512]{1,0:T(8,128)} %rest_9_.1, s32[1024]{0:T(1024)S(1)} %pad_clamp_fusion), kind=kCustom, calls=%fused_computation | custom fusion | bytes 2099200 | tf_op jit(solution)/shard_map/top_exchange/gather | solution.py:228
  23.5 2.0 %collective-permute-start.5 = (f32[256,256]{1,0:T(8,128)S(1)}, f32[256,256]{1,0:T(8,128)}, u32[]{:S(2)}, u32[]{:S(2)}) collective-permute-start(f32[256,256]{1,0:T(8,128)S(1)} %get-tuple-element.45), channel_id=1, source_target_pairs={{0,24},{1,25},{32,56},{33,57},{64,88},{65,89},{96,120},{97,121},{1... | collective-permute-start | bytes 786440 | tf_op jit(solution)/shard_map/panel_scatter/ppermute | solution.py:54
  25.6 2.0 %collective-permute-start.6 = (f32[256,256]{1,0:T(8,128)S(1)}, f32[256,256]{1,0:T(8,128)}, u32[]{:S(2)}, u32[]{:S(2)}) collective-permute-start(f32[256,256]{1,0:T(8,128)S(1)} %get-tuple-element.44), channel_id=1, source_target_pairs={{0,28},{1,29},{32,60},{33,61},{64,92},{65,93},{96,124},{97,125},{1... | collective-permute-start | bytes 786440 | tf_op jit(solution)/shard_map/panel_scatter/ppermute | solution.py:54
  27.6 1.0 collective-permute-start.7
  28.7 1.1 constant_dynamic-slice_fusion.4
  29.8 5.6 %collective-permute-done.6 = f32[256,256]{1,0:T(8,128)} collective-permute-done((f32[256,256]{1,0:T(8,128)S(1)}, f32[256,256]{1,0:T(8,128)}, u32[]{:S(2)}, u32[]{:S(2)}) %collective-permute-start.6) | collective-permute-done | bytes 262176 | tf_op jit(solution)/shard_map/panel_scatter/ppermute | solution.py:54
  35.4 1.1 select_select_fusion.2
  36.7 1.4 %collective-permute-start.11 = (f32[128,512]{1,0:T(8,128)S(1)}, f32[128,512]{1,0:T(8,128)S(1)}, u32[]{:S(2)}, u32[]{:S(2)}) collective-permute-start(f32[128,512]{1,0:T(8,128)S(1)} %pad_maximum_fusion.4), channel_id=1, source_target_pairs={{0,64},{32,96},{64,128},{96,160},{128,192},{160,224},{192,0},{224,... | collective-permute-start | bytes 786440 | tf_op jit(solution)/shard_map/top_exchange/ppermute | solution.py:243
  38.1 2.7 %collective-permute-start.12 = (f32[128,512]{1,0:T(8,128)S(1)}, f32[128,512]{1,0:T(8,128)S(1)}, u32[]{:S(2)}, u32[]{:S(2)}) collective-permute-start(f32[128,512]{1,0:T(8,128)S(1)} %pad_maximum_fusion.5), channel_id=1, source_target_pairs={{0,128},{32,160},{64,192},{96,224},{128,0},{160,32},{192,64},{224,... | collective-permute-start | bytes 786440 | tf_op jit(solution)/shard_map/top_exchange/ppermute | solution.py:243
  40.8 1.1 collective-permute-start.13
  42.0 1.9 %collective-permute-start.10 = (f32[256,256]{1,0:T(8,128)S(1)}, f32[256,256]{1,0:T(8,128)S(1)}, u32[]{:S(2)}, u32[]{:S(2)}) collective-permute-start(f32[256,256]{1,0:T(8,128)S(1)} %select_select_fusion.2), channel_id=1, source_target_pairs={{0,3},{4,7},{8,11},{12,15},{16,19},{20,23},{24,27},{28,31},{1,0},{... | collective-permute-start | bytes 786440 | tf_op jit(solution)/shard_map/panel_across/ppermute | solution.py:80
  43.9 3.4 %collective-permute-start.8 = (f32[256,256]{1,0:T(8,128)S(1)}, f32[256,256]{1,0:T(8,128)S(1)}, u32[]{:S(2)}, u32[]{:S(2)}) collective-permute-start(f32[256,256]{1,0:T(8,128)S(1)} %select_select_fusion.2), channel_id=1, source_target_pairs={{0,1},{4,5},{8,9},{12,13},{16,17},{20,21},{24,25},{28,29},{1,2},{5... | collective-permute-start | bytes 786440 | tf_op jit(solution)/shard_map/panel_across/ppermute | solution.py:79
  47.3 1.3 %collective-permute-start.9 = (f32[256,256]{1,0:T(8,128)S(1)}, f32[256,256]{1,0:T(8,128)S(1)}, u32[]{:S(2)}, u32[]{:S(2)}) collective-permute-start(f32[256,256]{1,0:T(8,128)S(1)} %select_select_fusion.2), channel_id=1, source_target_pairs={{0,2},{4,6},{8,10},{12,14},{16,18},{20,22},{24,26},{28,30},{1,3},{... | collective-permute-start | bytes 786440 | tf_op jit(solution)/shard_map/panel_across/ppermute | solution.py:81
  48.6 2.5 %collective-permute-done.12 = f32[128,512]{1,0:T(8,128)S(1)} collective-permute-done((f32[128,512]{1,0:T(8,128)S(1)}, f32[128,512]{1,0:T(8,128)S(1)}, u32[]{:S(2)}, u32[]{:S(2)}) %collective-permute-start.12) | collective-permute-done | bytes 262176 | tf_op jit(solution)/shard_map/top_exchange/ppermute | solution.py:243
  51.1 1.0 fusion.16
  52.1 1.7 %collective-permute-start.14 = (f32[128,256]{1,0:T(8,128)S(1)}, f32[128,256]{1,0:T(8,128)S(1)}, u32[]{:S(2)}, u32[]{:S(2)}) collective-permute-start(f32[128,256]{1,0:T(8,128)S(1)} %fusion.14), channel_id=1, source_target_pairs={{0,16},{1,17},{32,48},{33,49},{64,80},{65,81},{96,112},{97,113},{1... | collective-permute-start | bytes 393224 | tf_op jit(solution)/shard_map/fix_half/ppermute | solution.py:59
  53.8 2.0 %collective-permute-done.9 = f32[256,256]{1,0:T(8,128)S(1)} collective-permute-done((f32[256,256]{1,0:T(8,128)S(1)}, f32[256,256]{1,0:T(8,128)S(1)}, u32[]{:S(2)}, u32[]{:S(2)}) %collective-permute-start.9) | collective-permute-done | bytes 262176 | tf_op jit(solution)/shard_map/panel_across/ppermute | solution.py:81
  56.0 1.3 %collective-permute-start.15 = (f32[128,256]{1,0:T(8,128)S(1)}, f32[128,256]{1,0:T(8,128)S(1)}, u32[]{:S(2)}, u32[]{:S(2)}) collective-permute-start(f32[128,256]{1,0:T(8,128)S(1)} %broadcast_select_fusion.1), channel_id=1, source_target_pairs={{0,4},{1,5},{16,12},{17,13},{32,36},{33,37},{48,44},{49,45},{64,68... | collective-permute-start | bytes 393224 | tf_op jit(solution)/shard_map/fix_down/ppermute | solution.py:59
  57.3 1.3 %collective-permute-start.16 = (f32[128,256]{1,0:T(8,128)S(1)}, f32[128,256]{1,0:T(8,128)S(1)}, u32[]{:S(2)}, u32[]{:S(2)}) collective-permute-start(f32[128,256]{1,0:T(8,128)S(1)} %broadcast_select_fusion.1), channel_id=1, source_target_pairs={{0,8},{1,9},{16,24},{17,25},{32,40},{33,41},{48,56},{49,57},{64,72... | collective-permute-start | bytes 393224 | tf_op jit(solution)/shard_map/fix_down/ppermute | solution.py:59
  58.6 4.9 %collective-permute-start.17 = (f32[128,256]{1,0:T(8,128)S(1)}, f32[128,256]{1,0:T(8,128)}, u32[]{:S(2)}, u32[]{:S(2)}) collective-permute-start(f32[128,256]{1,0:T(8,128)S(1)} %broadcast_select_fusion.1), channel_id=1, source_target_pairs={{0,28},{1,29},{16,20},{17,21},{32,60},{33,61},{48,52},{49,53},{64,... | collective-permute-start | bytes 393224 | tf_op jit(solution)/shard_map/fix_down/ppermute | solution.py:59
  63.5 2.7 %collective-permute-start.28 = (f32[256,512]{1,0:T(8,128)S(1)}, f32[256,512]{1,0:T(8,128)S(1)}, u32[]{:S(2)}, u32[]{:S(2)}) collective-permute-start(f32[256,512]{1,0:T(8,128)S(1)} %pad_maximum_fusion.2.rest_0_), channel_id=1, source_target_pairs={{0,28},{1,29},{2,30},{3,31},{4,0},{5,1},{6,2},{7,3},{8,4},{9,5},{1... | collective-permute-start | bytes 1572872 | tf_op jit(solution)/shard_map/panel_ring/ppermute | solution.py:252
  66.4 1.6 %select_reduce_fusion = (s32[2048]{0:T(1024)S(1)}, s32[2048]{0:T(1024)S(1)}) fusion(s32[256]{0:T(256)} %copy-done.3, s32[256]{0:T(256)S(1)} %bitcast.38, s32[2048]{0:T(1024)S(1)} %fusion.26, s32[256]{0:T(256)S(1)} %fusion.33, s32[256]{0:T(256)S(1)} %bitcast.40), kind=kLoop, calls=%fused_computation.2 | loop fusion | flops 3141632 | bytes 28672 | tf_op jit(solution)/shard_map/reduce_sum | solution.py:220
  68.4 1.4 %copy.8 = s32[2048,1]{1,0:T(8,128)} copy(s32[2048,1]{0,1:T(1,128)S(1)} %bitcast.30) | data formatting | bytes 16384 | tf_op jit(solution)/shard_map/reduce_sum | solution.py:219
  70.2 1.1 collective-permute-start.23
  71.3 1.4 %collective-permute-start.24 = (f32[128,512]{1,0:T(8,128)S(1)}, f32[128,512]{1,0:T(8,128)S(1)}, u32[]{:S(2)}, u32[]{:S(2)}) collective-permute-start(f32[128,512]{1,0:T(8,128)S(1)} %get-tuple-element.61), channel_id=1, source_target_pairs={{0,192},{32,224},{64,0},{96,32},{128,64},{160,96},{192,128},{224,1... | collective-permute-start | bytes 786440 | tf_op jit(solution)/shard_map/top_gather/ppermute | solution.py:88
  72.7 1.6 %collective-permute-done.18.rest_1_ = f32[256,512]{1,0:T(8,128)S(1)} collective-permute-done((f32[256,512]{1,0:T(8,128)S(1)}, f32[256,512]{1,0:T(8,128)S(1)}, u32[]{:S(2)}, u32[]{:S(2)}) %collective-permute-start.18) | collective-permute-done | bytes 524320 | tf_op jit(solution)/shard_map/panel_ring/ppermute | solution.py:251
  74.5 1.6 %collective-permute-done.28.rest_2_ = f32[256,512]{1,0:T(8,128)S(1)} collective-permute-done((f32[256,512]{1,0:T(8,128)S(1)}, f32[256,512]{1,0:T(8,128)S(1)}, u32[]{:S(2)}, u32[]{:S(2)}) %collective-permute-start.28) | collective-permute-done | bytes 524320 | tf_op jit(solution)/shard_map/panel_ring/ppermute | solution.py:252
  76.1 3.4 %collective-permute-start.29 = (f32[256,512]{1,0:T(8,128)S(1)}, f32[256,512]{1,0:T(8,128)S(1)}, u32[]{:S(2)}, u32[]{:S(2)}) collective-permute-start(f32[256,512]{1,0:T(8,128)S(1)} %collective-permute-done.28.rest_2_), channel_id=1, source_target_pairs={{0,28},{1,29},{2,30},{3,31},{4,0},{5,1},{6,2},{7,3},{8,4},{9,5},{1... | collective-permute-start | bytes 1572872 | tf_op jit(solution)/shard_map/panel_ring/ppermute | solution.py:252
  79.5 1.6 %fusion.13.origin = s32[2048,1]{1,0:T(8,128)S(1)} fusion(s32[2048,1]{1,0:T(8,128)} %copy.8, s32[2048,1]{1,0:T(8,128)S(1)} %copy.10, s32[]{:T(128)} %axis_index.23), kind=kLoop, calls=%fused_computation.21 | loop fusion | flops 43008 | bytes 24580 | tf_op jit(solution)/shard_map/sub | solution.py:221
  82.1 1.3 %collective-permute-start.19 = (f32[128,256]{1,0:T(8,128)S(1)}, f32[128,256]{1,0:T(8,128)S(1)}, u32[]{:S(2)}, u32[]{:S(2)}) collective-permute-start(f32[128,256]{1,0:T(8,128)S(1)} %select_select_fusion.5), channel_id=1, source_target_pairs={{0,1},{4,5},{8,9},{12,13},{16,17},{20,21},{24,25},{28,29},{1,2},{5... | collective-permute-start | bytes 393224 | tf_op jit(solution)/shard_map/fix_across/ppermute | solution.py:79
  83.4 1.3 %collective-permute-start.20 = (f32[128,256]{1,0:T(8,128)S(1)}, f32[128,256]{1,0:T(8,128)S(1)}, u32[]{:S(2)}, u32[]{:S(2)}) collective-permute-start(f32[128,256]{1,0:T(8,128)S(1)} %select_select_fusion.5), channel_id=1, source_target_pairs={{0,2},{4,6},{8,10},{12,14},{16,18},{20,22},{24,26},{28,30},{1,3},{... | collective-permute-start | bytes 393224 | tf_op jit(solution)/shard_map/fix_across/ppermute | solution.py:81
  84.7 1.9 %collective-permute-start.21 = (f32[128,256]{1,0:T(8,128)S(1)}, f32[128,256]{1,0:T(8,128)S(1)}, u32[]{:S(2)}, u32[]{:S(2)}) collective-permute-start(f32[128,256]{1,0:T(8,128)S(1)} %select_select_fusion.5), channel_id=1, source_target_pairs={{0,3},{4,7},{8,11},{12,15},{16,19},{20,23},{24,27},{28,31},{1,0},{... | collective-permute-start | bytes 393224 | tf_op jit(solution)/shard_map/fix_across/ppermute | solution.py:80
  87.1 3.4 %collective-permute-start.30 = (f32[256,512]{1,0:T(8,128)S(1)}, f32[256,512]{1,0:T(8,128)S(1)}, u32[]{:S(2)}, u32[]{:S(2)}) collective-permute-start(f32[256,512]{1,0:T(8,128)S(1)} %collective-permute-done.29.rest_4_), channel_id=1, source_target_pairs={{0,28},{1,29},{2,30},{3,31},{4,0},{5,1},{6,2},{7,3},{8,4},{9,5},{1... | collective-permute-start | bytes 1572872 | tf_op jit(solution)/shard_map/panel_ring/ppermute | solution.py:252
  90.6 3.2 %collective-permute-start.31 = (f32[128,512]{1,0:T(8,128)S(1)}, f32[128,512]{1,0:T(8,128)S(1)}, u32[]{:S(2)}, u32[]{:S(2)}) collective-permute-start(f32[128,512]{1,0:T(8,128)S(1)} %pad_maximum_fusion.7), channel_id=1, source_target_pairs={{0,64},{32,96},{64,128},{96,160},{128,192},{160,224},{192,0},{224,... | collective-permute-start | bytes 786440 | tf_op jit(solution)/shard_map/fix_gather/ppermute | solution.py:88
  93.8 1.0 collective-permute-start.32
  94.8 1.5 %collective-permute-start.33 = (f32[128,512]{1,0:T(8,128)S(1)}, f32[128,512]{1,0:T(8,128)S(1)}, u32[]{:S(2)}, u32[]{:S(2)}) collective-permute-start(f32[128,512]{1,0:T(8,128)S(1)} %pad_maximum_fusion.7), channel_id=1, source_target_pairs={{0,192},{32,224},{64,0},{96,32},{128,64},{160,96},{192,128},{224,1... | collective-permute-start | bytes 786440 | tf_op jit(solution)/shard_map/fix_gather/ppermute | solution.py:88
  96.3 1.4 %collective-permute-done.31 = f32[128,512]{1,0:T(8,128)S(1)} collective-permute-done((f32[128,512]{1,0:T(8,128)S(1)}, f32[128,512]{1,0:T(8,128)S(1)}, u32[]{:S(2)}, u32[]{:S(2)}) %collective-permute-start.31) | collective-permute-done | bytes 262176 | tf_op jit(solution)/shard_map/fix_gather/ppermute | solution.py:88
  97.6 10.5 %collective-permute-start.26 = (f32[4,128,512]{2,1,0:T(8,128)S(1)}, f32[4,128,512]{2,1,0:T(8,128)S(1)}, u32[]{:S(2)}, u32[]{:S(2)}) collective-permute-start(f32[4,128,512]{2,1,0:T(8,128)S(1)} %pad_maximum_fusion.top_mine), channel_id=1, source_target_pairs={{0,32},{32,0},{64,96},{96,64},{128,160},{160,128},{192,224},{224,1... | collective-permute-start | bytes 3145736 | tf_op jit(solution)/shard_map/core_gather/ppermute | solution.py:277
  108.5 3.0 %collective-permute-start.36 = (f32[128,512]{1,0:T(8,128)S(1)}, f32[128,512]{1,0:T(8,128)S(1)}, u32[]{:S(2)}, u32[]{:S(2)}) collective-permute-start(f32[128,512]{1,0:T(8,128)S(1)} %slice.89), channel_id=1, source_target_pairs={{0,28},{1,29},{2,30},{3,31},{4,0},{5,1},{6,2},{7,3},{8,4},{9,5},{1... | collective-permute-start | bytes 786440 | tf_op jit(solution)/shard_map/panel_ring/ppermute | solution.py:252
  111.9 4.1 %factor.1 = (bf16[512,512]{1,0:T(8,128)(2,1)S(1)}, bf16[512,512]{1,0:T(8,128)(2,1)S(1)}, bf16[512,512]{1,0:T(8,128)(2,1)S(1)}, bf16[512,512]{1,0:T(8,128)(2,1)S(1)}, f32[256,512]{1,0:T(8,128)S(1)}) custom-call(s32[4]{0:T(128)S(1)} %pad_add_fusion.2.ids, f32[4,128,512]{2,1,0:T(8,128)S(1)} %pad_maximum_fusion.top_mine, ...), custom_call_target="tpu_custom_call" | custom-call | flops 3000000000 | bytes 8388608 | tf_op jit(solution)/shard_map/factor/pallas_call | solution.py:287
  116.0 1.1 collective-permute-done.35.rest_7_
  117.1 8.1 %update.1 = f32[2048,512]{1,0:T(8,128)} custom-call(s32[4]{0:T(128)S(1)} %pad_add_fusion.2.ids, s32[2048,1]{1,0:T(8,128)S(1)} %fusion.13.origin, bf16[512,512]{1,0:T(8,128)(2,1)S(1)} %get-tuple-element.32.factor_high, bf16[512,512]{1,0:T(8,128)(2,1)S(1)} %get-tuple-element.33.factor_low, bf16[512,512]{1,0:T(8,128)(2,1)S(1)} %get-tuple-element.34.moved_high, ...), custom_call_target="tpu_custom_call" | custom-call | flops 6000000000 | bytes 14680064 | tf_op jit(solution)/shard_map/update/pallas_call | solution.py:299
  (78 shorter events, 4.3 us)
Async XLA Ops:
  0.0 18.9 %copy-start.4 = (s32[2,256]{1,0:T(2,128)S(1)}, s32[2,256]{1,0:T(2,128)}, u32[]{:S(2)}) copy-start(s32[2,256]{1,0:T(2,128)} %param.5) | copy-start | bytes 6148
  2.4 21.1 %collective-permute-start = (f32[256,256]{1,0:T(8,128)}, f32[256,256]{1,0:T(8,128)}, u32[]{:S(2)}, u32[]{:S(2)}) collective-permute-start(f32[256,256]{1,0:T(8,128)} %get-tuple-element.50), channel_id=1, source_target_pairs={{0,4},{1,5},{32,36},{33,37},{64,68},{65,69},{96,100},{97,101},{128... | collective-permute-start | bytes 786440 | tf_op jit(solution)/shard_map/panel_scatter/ppermute | solution.py:54
  7.5 18.1 %collective-permute-start.1 = (f32[256,256]{1,0:T(8,128)}, f32[256,256]{1,0:T(8,128)}, u32[]{:S(2)}, u32[]{:S(2)}) collective-permute-start(f32[256,256]{1,0:T(8,128)} %get-tuple-element.49), channel_id=1, source_target_pairs={{0,8},{1,9},{32,40},{33,41},{64,72},{65,73},{96,104},{97,105},{128... | collective-permute-start | bytes 786440 | tf_op jit(solution)/shard_map/panel_scatter/ppermute | solution.py:54
  10.2 17.4 %collective-permute-start.2 = (f32[256,256]{1,0:T(8,128)S(1)}, f32[256,256]{1,0:T(8,128)}, u32[]{:S(2)}, u32[]{:S(2)}) collective-permute-start(f32[256,256]{1,0:T(8,128)S(1)} %get-tuple-element.48), channel_id=1, source_target_pairs={{0,12},{1,13},{32,44},{33,45},{64,76},{65,77},{96,108},{97,109},{1... | collective-permute-start | bytes 786440 | tf_op jit(solution)/shard_map/panel_scatter/ppermute | solution.py:54
  12.9 16.8 %collective-permute-start.3 = (f32[256,256]{1,0:T(8,128)S(1)}, f32[256,256]{1,0:T(8,128)}, u32[]{:S(2)}, u32[]{:S(2)}) collective-permute-start(f32[256,256]{1,0:T(8,128)S(1)} %get-tuple-element.47), channel_id=1, source_target_pairs={{0,16},{1,17},{32,48},{33,49},{64,80},{65,81},{96,112},{97,113},{1... | collective-permute-start | bytes 786440 | tf_op jit(solution)/shard_map/panel_scatter/ppermute | solution.py:54
  16.9 12.9 %collective-permute-start.4 = (f32[256,256]{1,0:T(8,128)S(1)}, f32[256,256]{1,0:T(8,128)}, u32[]{:S(2)}, u32[]{:S(2)}) collective-permute-start(f32[256,256]{1,0:T(8,128)S(1)} %get-tuple-element.46), channel_id=1, source_target_pairs={{0,20},{1,21},{32,52},{33,53},{64,84},{65,85},{96,116},{97,117},{1... | collective-permute-start | bytes 786440 | tf_op jit(solution)/shard_map/panel_scatter/ppermute | solution.py:54
  18.9 47.4 %copy-start.3 = (s32[256]{0:T(256)}, s32[256]{0:T(256)S(1)}, u32[]{:S(2)}) copy-start(s32[256]{0:T(256)S(1)} %get-tuple-element.68) | copy-start | bytes 3076
  23.5 6.3 %collective-permute-start.5 = (f32[256,256]{1,0:T(8,128)S(1)}, f32[256,256]{1,0:T(8,128)}, u32[]{:S(2)}, u32[]{:S(2)}) collective-permute-start(f32[256,256]{1,0:T(8,128)S(1)} %get-tuple-element.45), channel_id=1, source_target_pairs={{0,24},{1,25},{32,56},{33,57},{64,88},{65,89},{96,120},{97,121},{1... | collective-permute-start | bytes 786440 | tf_op jit(solution)/shard_map/panel_scatter/ppermute | solution.py:54
  25.6 9.8 %collective-permute-start.6 = (f32[256,256]{1,0:T(8,128)S(1)}, f32[256,256]{1,0:T(8,128)}, u32[]{:S(2)}, u32[]{:S(2)}) collective-permute-start(f32[256,256]{1,0:T(8,128)S(1)} %get-tuple-element.44), channel_id=1, source_target_pairs={{0,28},{1,29},{32,60},{33,61},{64,92},{65,93},{96,124},{97,125},{1... | collective-permute-start | bytes 786440 | tf_op jit(solution)/shard_map/panel_scatter/ppermute | solution.py:54
  27.6 8.9 %collective-permute-start.7 = (f32[256,512]{1,0:T(8,128)S(1)}, f32[256,512]{1,0:T(8,128)S(1)}, u32[]{:S(2)}, u32[]{:S(2)}) collective-permute-start(f32[256,512]{1,0:T(8,128)S(1)} %constant_dynamic-slice_fusion.6), channel_id=1, source_target_pairs={{0,32},{32,0},{64,96},{96,64},{128,160},{160,128},{192,224},{224,1... | collective-permute-start | bytes 1572872 | tf_op jit(solution)/shard_map/top_exchange/ppermute | solution.py:231
  36.7 10.6 %collective-permute-start.11 = (f32[128,512]{1,0:T(8,128)S(1)}, f32[128,512]{1,0:T(8,128)S(1)}, u32[]{:S(2)}, u32[]{:S(2)}) collective-permute-start(f32[128,512]{1,0:T(8,128)S(1)} %pad_maximum_fusion.4), channel_id=1, source_target_pairs={{0,64},{32,96},{64,128},{96,160},{128,192},{160,224},{192,0},{224,... | collective-permute-start | bytes 786440 | tf_op jit(solution)/shard_map/top_exchange/ppermute | solution.py:243
  38.1 13.0 %collective-permute-start.12 = (f32[128,512]{1,0:T(8,128)S(1)}, f32[128,512]{1,0:T(8,128)S(1)}, u32[]{:S(2)}, u32[]{:S(2)}) collective-permute-start(f32[128,512]{1,0:T(8,128)S(1)} %pad_maximum_fusion.5), channel_id=1, source_target_pairs={{0,128},{32,160},{64,192},{96,224},{128,0},{160,32},{192,64},{224,... | collective-permute-start | bytes 786440 | tf_op jit(solution)/shard_map/top_exchange/ppermute | solution.py:243
  40.8 10.3 %collective-permute-start.13 = (f32[128,512]{1,0:T(8,128)S(1)}, f32[128,512]{1,0:T(8,128)S(1)}, u32[]{:S(2)}, u32[]{:S(2)}) collective-permute-start(f32[128,512]{1,0:T(8,128)S(1)} %pad_maximum_fusion.6), channel_id=1, source_target_pairs={{0,192},{32,224},{64,0},{96,32},{128,64},{160,96},{192,128},{224,1... | collective-permute-start | bytes 786440 | tf_op jit(solution)/shard_map/top_exchange/ppermute | solution.py:243
  42.0 11.8 %collective-permute-start.10 = (f32[256,256]{1,0:T(8,128)S(1)}, f32[256,256]{1,0:T(8,128)S(1)}, u32[]{:S(2)}, u32[]{:S(2)}) collective-permute-start(f32[256,256]{1,0:T(8,128)S(1)} %select_select_fusion.2), channel_id=1, source_target_pairs={{0,3},{4,7},{8,11},{12,15},{16,19},{20,23},{24,27},{28,31},{1,0},{... | collective-permute-start | bytes 786440 | tf_op jit(solution)/shard_map/panel_across/ppermute | solution.py:80
  43.9 9.9 %collective-permute-start.8 = (f32[256,256]{1,0:T(8,128)S(1)}, f32[256,256]{1,0:T(8,128)S(1)}, u32[]{:S(2)}, u32[]{:S(2)}) collective-permute-start(f32[256,256]{1,0:T(8,128)S(1)} %select_select_fusion.2), channel_id=1, source_target_pairs={{0,1},{4,5},{8,9},{12,13},{16,17},{20,21},{24,25},{28,29},{1,2},{5... | collective-permute-start | bytes 786440 | tf_op jit(solution)/shard_map/panel_across/ppermute | solution.py:79
  47.3 8.5 %collective-permute-start.9 = (f32[256,256]{1,0:T(8,128)S(1)}, f32[256,256]{1,0:T(8,128)S(1)}, u32[]{:S(2)}, u32[]{:S(2)}) collective-permute-start(f32[256,256]{1,0:T(8,128)S(1)} %select_select_fusion.2), channel_id=1, source_target_pairs={{0,2},{4,6},{8,10},{12,14},{16,18},{20,22},{24,26},{28,30},{1,3},{... | collective-permute-start | bytes 786440 | tf_op jit(solution)/shard_map/panel_across/ppermute | solution.py:81
  52.1 3.9 %collective-permute-start.14 = (f32[128,256]{1,0:T(8,128)S(1)}, f32[128,256]{1,0:T(8,128)S(1)}, u32[]{:S(2)}, u32[]{:S(2)}) collective-permute-start(f32[128,256]{1,0:T(8,128)S(1)} %fusion.14), channel_id=1, source_target_pairs={{0,16},{1,17},{32,48},{33,49},{64,80},{65,81},{96,112},{97,113},{1... | collective-permute-start | bytes 393224 | tf_op jit(solution)/shard_map/fix_half/ppermute | solution.py:59
  56.0 13.7 %collective-permute-start.15 = (f32[128,256]{1,0:T(8,128)S(1)}, f32[128,256]{1,0:T(8,128)S(1)}, u32[]{:S(2)}, u32[]{:S(2)}) collective-permute-start(f32[128,256]{1,0:T(8,128)S(1)} %broadcast_select_fusion.1), channel_id=1, source_target_pairs={{0,4},{1,5},{16,12},{17,13},{32,36},{33,37},{48,44},{49,45},{64,68... | collective-permute-start | bytes 393224 | tf_op jit(solution)/shard_map/fix_down/ppermute | solution.py:59
  57.3 12.8 %collective-permute-start.16 = (f32[128,256]{1,0:T(8,128)S(1)}, f32[128,256]{1,0:T(8,128)S(1)}, u32[]{:S(2)}, u32[]{:S(2)}) collective-permute-start(f32[128,256]{1,0:T(8,128)S(1)} %broadcast_select_fusion.1), channel_id=1, source_target_pairs={{0,8},{1,9},{16,24},{17,25},{32,40},{33,41},{48,56},{49,57},{64,72... | collective-permute-start | bytes 393224 | tf_op jit(solution)/shard_map/fix_down/ppermute | solution.py:59
  58.6 12.7 %collective-permute-start.17 = (f32[128,256]{1,0:T(8,128)S(1)}, f32[128,256]{1,0:T(8,128)}, u32[]{:S(2)}, u32[]{:S(2)}) collective-permute-start(f32[128,256]{1,0:T(8,128)S(1)} %broadcast_select_fusion.1), channel_id=1, source_target_pairs={{0,28},{1,29},{16,20},{17,21},{32,60},{33,61},{48,52},{49,53},{64,... | collective-permute-start | bytes 393224 | tf_op jit(solution)/shard_map/fix_down/ppermute | solution.py:59
  63.5 10.8 %collective-permute-start.18 = (f32[256,512]{1,0:T(8,128)S(1)}, f32[256,512]{1,0:T(8,128)S(1)}, u32[]{:S(2)}, u32[]{:S(2)}) collective-permute-start(f32[256,512]{1,0:T(8,128)S(1)} %pad_maximum_fusion.2.rest_0_), channel_id=1, source_target_pairs={{0,4},{1,5},{2,6},{3,7},{4,8},{5,9},{6,10},{7,11},{8,12},{9,13},{1... | collective-permute-start | bytes 1572872 | tf_op jit(solution)/shard_map/panel_ring/ppermute | solution.py:251
  63.5 12.6 %collective-permute-start.28 = (f32[256,512]{1,0:T(8,128)S(1)}, f32[256,512]{1,0:T(8,128)S(1)}, u32[]{:S(2)}, u32[]{:S(2)}) collective-permute-start(f32[256,512]{1,0:T(8,128)S(1)} %pad_maximum_fusion.2.rest_0_), channel_id=1, source_target_pairs={{0,28},{1,29},{2,30},{3,31},{4,0},{5,1},{6,2},{7,3},{8,4},{9,5},{1... | collective-permute-start | bytes 1572872 | tf_op jit(solution)/shard_map/panel_ring/ppermute | solution.py:252
  69.8 12.3 %collective-permute-start.22 = (f32[128,512]{1,0:T(8,128)S(1)}, f32[128,512]{1,0:T(8,128)S(1)}, u32[]{:S(2)}, u32[]{:S(2)}) collective-permute-start(f32[128,512]{1,0:T(8,128)S(1)} %get-tuple-element.61), channel_id=1, source_target_pairs={{0,64},{32,96},{64,128},{96,160},{128,192},{160,224},{192,0},{224,... | collective-permute-start | bytes 786440 | tf_op jit(solution)/shard_map/top_gather/ppermute | solution.py:88
  70.2 13.2 %collective-permute-start.23 = (f32[128,512]{1,0:T(8,128)S(1)}, f32[128,512]{1,0:T(8,128)S(1)}, u32[]{:S(2)}, u32[]{:S(2)}) collective-permute-start(f32[128,512]{1,0:T(8,128)S(1)} %get-tuple-element.61), channel_id=1, source_target_pairs={{0,128},{32,160},{64,192},{96,224},{128,0},{160,32},{192,64},{224,... | collective-permute-start | bytes 786440 | tf_op jit(solution)/shard_map/top_gather/ppermute | solution.py:88
  71.3 13.4 %collective-permute-start.24 = (f32[128,512]{1,0:T(8,128)S(1)}, f32[128,512]{1,0:T(8,128)S(1)}, u32[]{:S(2)}, u32[]{:S(2)}) collective-permute-start(f32[128,512]{1,0:T(8,128)S(1)} %get-tuple-element.61), channel_id=1, source_target_pairs={{0,192},{32,224},{64,0},{96,32},{128,64},{160,96},{192,128},{224,1... | collective-permute-start | bytes 786440 | tf_op jit(solution)/shard_map/top_gather/ppermute | solution.py:88
  74.3 12.5 %collective-permute-start.25 = (f32[256,512]{1,0:T(8,128)S(1)}, f32[256,512]{1,0:T(8,128)S(1)}, u32[]{:S(2)}, u32[]{:S(2)}) collective-permute-start(f32[256,512]{1,0:T(8,128)S(1)} %collective-permute-done.18.rest_1_), channel_id=1, source_target_pairs={{0,4},{1,5},{2,6},{3,7},{4,8},{5,9},{6,10},{7,11},{8,12},{9,13},{1... | collective-permute-start | bytes 1572872 | tf_op jit(solution)/shard_map/panel_ring/ppermute | solution.py:251
  76.1 11.0 %collective-permute-start.29 = (f32[256,512]{1,0:T(8,128)S(1)}, f32[256,512]{1,0:T(8,128)S(1)}, u32[]{:S(2)}, u32[]{:S(2)}) collective-permute-start(f32[256,512]{1,0:T(8,128)S(1)} %collective-permute-done.28.rest_2_), channel_id=1, source_target_pairs={{0,28},{1,29},{2,30},{3,31},{4,0},{5,1},{6,2},{7,3},{8,4},{9,5},{1... | collective-permute-start | bytes 1572872 | tf_op jit(solution)/shard_map/panel_ring/ppermute | solution.py:252
  82.1 8.4 %collective-permute-start.19 = (f32[128,256]{1,0:T(8,128)S(1)}, f32[128,256]{1,0:T(8,128)S(1)}, u32[]{:S(2)}, u32[]{:S(2)}) collective-permute-start(f32[128,256]{1,0:T(8,128)S(1)} %select_select_fusion.5), channel_id=1, source_target_pairs={{0,1},{4,5},{8,9},{12,13},{16,17},{20,21},{24,25},{28,29},{1,2},{5... | collective-permute-start | bytes 393224 | tf_op jit(solution)/shard_map/fix_across/ppermute | solution.py:79
  83.4 7.1 %collective-permute-start.20 = (f32[128,256]{1,0:T(8,128)S(1)}, f32[128,256]{1,0:T(8,128)S(1)}, u32[]{:S(2)}, u32[]{:S(2)}) collective-permute-start(f32[128,256]{1,0:T(8,128)S(1)} %select_select_fusion.5), channel_id=1, source_target_pairs={{0,2},{4,6},{8,10},{12,14},{16,18},{20,22},{24,26},{28,30},{1,3},{... | collective-permute-start | bytes 393224 | tf_op jit(solution)/shard_map/fix_across/ppermute | solution.py:81
  84.7 5.8 %collective-permute-start.21 = (f32[128,256]{1,0:T(8,128)S(1)}, f32[128,256]{1,0:T(8,128)S(1)}, u32[]{:S(2)}, u32[]{:S(2)}) collective-permute-start(f32[128,256]{1,0:T(8,128)S(1)} %select_select_fusion.5), channel_id=1, source_target_pairs={{0,3},{4,7},{8,11},{12,15},{16,19},{20,23},{24,27},{28,31},{1,0},{... | collective-permute-start | bytes 393224 | tf_op jit(solution)/shard_map/fix_across/ppermute | solution.py:80
  86.7 25.2 %copy-start.1 = (f32[2,256,256]{2,1,0:T(8,128)S(1)}, f32[2,256,256]{2,1,0:T(8,128)}, u32[]{:S(2)}) copy-start(f32[2,256,256]{2,1,0:T(8,128)} %lower_inverse.1) | copy-start | bytes 1572868
  86.7 25.1 %copy-start.2 = (f32[2,256,256]{2,1,0:T(8,128)S(1)}, f32[2,256,256]{2,1,0:T(8,128)}, u32[]{:S(2)}) copy-start(f32[2,256,256]{2,1,0:T(8,128)} %upper_inverse.1) | copy-start | bytes 1572868
  86.8 21.4 %collective-permute-start.27 = (f32[256,512]{1,0:T(8,128)S(1)}, f32[256,512]{1,0:T(8,128)S(1)}, u32[]{:S(2)}, u32[]{:S(2)}) collective-permute-start(f32[256,512]{1,0:T(8,128)S(1)} %collective-permute-done.25.rest_3_), channel_id=1, source_target_pairs={{0,4},{1,5},{2,6},{3,7},{4,8},{5,9},{6,10},{7,11},{8,12},{9,13},{1... | collective-permute-start | bytes 1572872 | tf_op jit(solution)/shard_map/panel_ring/ppermute | solution.py:251
  87.1 21.1 %collective-permute-start.30 = (f32[256,512]{1,0:T(8,128)S(1)}, f32[256,512]{1,0:T(8,128)S(1)}, u32[]{:S(2)}, u32[]{:S(2)}) collective-permute-start(f32[256,512]{1,0:T(8,128)S(1)} %collective-permute-done.29.rest_4_), channel_id=1, source_target_pairs={{0,28},{1,29},{2,30},{3,31},{4,0},{5,1},{6,2},{7,3},{8,4},{9,5},{1... | collective-permute-start | bytes 1572872 | tf_op jit(solution)/shard_map/panel_ring/ppermute | solution.py:252
  90.6 7.0 %collective-permute-start.31 = (f32[128,512]{1,0:T(8,128)S(1)}, f32[128,512]{1,0:T(8,128)S(1)}, u32[]{:S(2)}, u32[]{:S(2)}) collective-permute-start(f32[128,512]{1,0:T(8,128)S(1)} %pad_maximum_fusion.7), channel_id=1, source_target_pairs={{0,64},{32,96},{64,128},{96,160},{128,192},{160,224},{192,0},{224,... | collective-permute-start | bytes 786440 | tf_op jit(solution)/shard_map/fix_gather/ppermute | solution.py:88
  93.8 14.3 %collective-permute-start.32 = (f32[128,512]{1,0:T(8,128)S(1)}, f32[128,512]{1,0:T(8,128)S(1)}, u32[]{:S(2)}, u32[]{:S(2)}) collective-permute-start(f32[128,512]{1,0:T(8,128)S(1)} %pad_maximum_fusion.7), channel_id=1, source_target_pairs={{0,128},{32,160},{64,192},{96,224},{128,0},{160,32},{192,64},{224,... | collective-permute-start | bytes 786440 | tf_op jit(solution)/shard_map/fix_gather/ppermute | solution.py:88
  94.8 13.3 %collective-permute-start.33 = (f32[128,512]{1,0:T(8,128)S(1)}, f32[128,512]{1,0:T(8,128)S(1)}, u32[]{:S(2)}, u32[]{:S(2)}) collective-permute-start(f32[128,512]{1,0:T(8,128)S(1)} %pad_maximum_fusion.7), channel_id=1, source_target_pairs={{0,192},{32,224},{64,0},{96,32},{128,64},{160,96},{192,128},{224,1... | collective-permute-start | bytes 786440 | tf_op jit(solution)/shard_map/fix_gather/ppermute | solution.py:88
  97.6 13.9 %collective-permute-start.26 = (f32[4,128,512]{2,1,0:T(8,128)S(1)}, f32[4,128,512]{2,1,0:T(8,128)S(1)}, u32[]{:S(2)}, u32[]{:S(2)}) collective-permute-start(f32[4,128,512]{2,1,0:T(8,128)S(1)} %pad_maximum_fusion.top_mine), channel_id=1, source_target_pairs={{0,32},{32,0},{64,96},{96,64},{128,160},{160,128},{192,224},{224,1... | collective-permute-start | bytes 3145736 | tf_op jit(solution)/shard_map/core_gather/ppermute | solution.py:277
  108.2 3.7 %collective-permute-start.34 = (f32[4,128,512]{2,1,0:T(8,128)S(1)}, f32[4,128,512]{2,1,0:T(8,128)S(1)}, u32[]{:S(2)}, u32[]{:S(2)}) collective-permute-start(f32[4,128,512]{2,1,0:T(8,128)S(1)} %pad_maximum_fusion.1.fix_mine), channel_id=1, source_target_pairs={{0,32},{32,0},{64,96},{96,64},{128,160},{160,128},{192,224},{224,1... | collective-permute-start | bytes 3145736 | tf_op jit(solution)/shard_map/core_gather/ppermute | solution.py:278
  108.4 8.7 %collective-permute-start.35 = (f32[128,512]{1,0:T(8,128)S(1)}, f32[128,512]{1,0:T(8,128)S(1)}, u32[]{:S(2)}, u32[]{:S(2)}) collective-permute-start(f32[128,512]{1,0:T(8,128)S(1)} %slice.88), channel_id=1, source_target_pairs={{0,4},{1,5},{2,6},{3,7},{4,8},{5,9},{6,10},{7,11},{8,12},{9,13},{1... | collective-permute-start | bytes 786440 | tf_op jit(solution)/shard_map/panel_ring/ppermute | solution.py:251
  108.5 8.6 %copy-start = (f32[2048,512]{1,0:T(8,128)S(1)}, f32[2048,512]{1,0:T(8,128)}, u32[]{:S(2)}) copy-start(f32[2048,512]{1,0:T(8,128)} %rest_9_.1) | copy-start | bytes 12582916
  108.5 8.5 %collective-permute-start.36 = (f32[128,512]{1,0:T(8,128)S(1)}, f32[128,512]{1,0:T(8,128)S(1)}, u32[]{:S(2)}, u32[]{:S(2)}) collective-permute-start(f32[128,512]{1,0:T(8,128)S(1)} %slice.89), channel_id=1, source_target_pairs={{0,28},{1,29},{2,30},{3,31},{4,0},{5,1},{6,2},{7,3},{8,4},{9,5},{1... | collective-permute-start | bytes 786440 | tf_op jit(solution)/shard_map/panel_ring/ppermute | solution.py:252

commit v5 on v4

--- a/solution.py
+++ b/solution.py
@@ -161,10 +161,10 @@
         return pl.ds(pl.multiple_of(owners[i] * nb, nb), nb)
 
     def part(i):
-        return pl.ds(i % 4 * nb, nb)
+        return pl.ds(i * nb, nb)
 
     def out_copy(i):
-        return pltpu.make_async_copy(out_block.at[part(i)], out.at[place(i)], out_sem.at[i % 4])
+        return pltpu.make_async_copy(out_block.at[part(i)], out.at[place(i)], out_sem.at[i])
 
     for i in range(0, NZ, 2):
         held = [pieces[i][...], pieces[i + 1][...]]
@@ -180,14 +180,12 @@
         moved = one(chosen, moved_high[...]) + one(chosen, moved_low[...])
         for j in (i, i + 1):
             here = slice((j - i) * nb, (j - i + 1) * nb)
-            if j >= 4:
-                out_copy(j - 4).wait()
             kept = jnp.where(drop, 0.0, matrix[place(j), :]) - product[here]
             value = jnp.where(source[here] >= 0, moved[here], kept)
             is_head = jnp.logical_and(owners[j] == 0, p < 2)
             out_block[part(j)] = jnp.where(is_head, head[...], value)
             out_copy(j).start()
-    for i in range(NZ - 4, NZ):
+    for i in range(NZ):
         out_copy(i).wait()
 
 
@@ -289,20 +287,20 @@
             out_shape=[small] * 4 + [jax.ShapeDtypeStruct((nb, width), jnp.float32)],
             in_specs=[smem] + [vmem] * 6,
             out_specs=[vmem] * 5,
-            compiler_params=pltpu.CompilerParams(vmem_limit_bytes=16 * 1024 * 1024),
+            compiler_params=pltpu.CompilerParams(vmem_limit_bytes=20 * 1024 * 1024),
             cost_estimate=pl.CostEstimate(
                 flops=3 * 10**9, bytes_accessed=8 * 2**20, transcendentals=0
             ),
         )(ids, top_mine, top_other, fix_mine, fix_other, lower_inverse, upper_inverse)
-    blocks = pltpu.VMEM((4 * nb, width), jnp.float32)
+    blocks = pltpu.VMEM((NZ * nb, width), jnp.float32)
     with jax.named_scope("update"):
         return pl.pallas_call(
             update_kernel,
             out_shape=jax.ShapeDtypeStruct((rows, width), jnp.float32),
             in_specs=[smem] + [vmem] * (6 + NZ + 2),
             out_specs=hbm,
-            scratch_shapes=[blocks, pltpu.SemaphoreType.DMA((4,))],
-            compiler_params=pltpu.CompilerParams(vmem_limit_bytes=16 * 1024 * 1024),
+            scratch_shapes=[blocks, pltpu.SemaphoreType.DMA((NZ,))],
+            compiler_params=pltpu.CompilerParams(vmem_limit_bytes=20 * 1024 * 1024),
             cost_estimate=pl.CostEstimate(
                 flops=6 * 10**9, bytes_accessed=14 * 2**20, transcendentals=0
             ),

time: 128 us -> 127 us (level)
  no operation moved by 1% of the time
where the time goes in v5:
time: 127 us; the launch traced here: 125 us
  starting transfers between devices  78.8 us (62%)
  waiting for transfers between devices  16.6 us (13%)
  Pallas kernels  11.6 us (9%)
  local copies, waits for them, and re-layouts  9.57 us (8%)
  other arithmetic  7.51 us (6%)
    ppermute x7, starting transfers between devices, scatter_z(): arrived.append(lax.ppermute(pieces[k], 'pcol', pairs))  20.4 us
    ppermute x4, starting transfers between devices, ring(): lax.ppermute(down, 'pcol', along_z(-1))  12.4 us
    ppermute x1, starting transfers between devices, on_device(): top_other = lax.ppermute(top_mine, 'prow', other_core())  10.5 us
    ppermute x4, starting transfers between devices, send_z(): lax.ppermute(value, 'pcol', [(at(a, x), at(b, x)) for a, b in pairs for x...  9.14 us
    ppermute x6, starting transfers between devices, gather_y(): lax.ppermute(mine, 'prow', along_y(k))  8.54 us
    pallas_call x1, Pallas kernels, on_device(): pl.pallas_call(update_kernel, out_shape=jax.ShapeDtypeStruct((rows, width...  7.57 us
    ppermute x7, waiting for transfers between devices, scatter_z(): arrived.append(lax.ppermute(pieces[k], 'pcol', pairs))  5.7 us
    ppermute x3, starting transfers between devices, on_device(): got = lax.ppermute(packed, 'prow', along_y(step))  5.23 us
  transfers between devices with their start and end apart: 37, of which 11 were waited for; matrix products, arithmetic and copies ran while one was open for 12% of the time, Pallas kernels for 3%

profile of v5, /device:TPU:1, one launch (start us, length us, event | category | flops | bytes accessed | tf_op | source)
XLA Modules:
  0.0 124.8 jit_solution(8507658636393060598)
XLA Ops:
  0.0 2.4 %fusion.35 = (f32[256,256]{1,0:T(8,128)S(1)}, f32[256,256]{1,0:T(8,128)S(1)}, f32[256,256]{1,0:T(8,128)S(1)}, f32[256,256]{1,0:T(8,128)S(1)}, f32[256,256]{1,0:T...) fusion(f32[2048,512]{1,0:T(8,128)} %rest_9_.1), kind=kLoop, calls=%fused_computation.106 | loop fusion | bytes 3670016 | tf_op jit(solution)/shard_map/panel_scatter/slice | solution.py:202
  2.4 5.1 %collective-permute-start = (f32[256,256]{1,0:T(8,128)}, f32[256,256]{1,0:T(8,128)}, u32[]{:S(2)}, u32[]{:S(2)}) collective-permute-start(f32[256,256]{1,0:T(8,128)} %get-tuple-element.50), channel_id=1, source_target_pairs={{0,4},{1,5},{32,36},{33,37},{64,68},{65,69},{96,100},{97,101},{128... | collective-permute-start | bytes 786440 | tf_op jit(solution)/shard_map/panel_scatter/ppermute | solution.py:54
  7.5 2.7 %collective-permute-start.1 = (f32[256,256]{1,0:T(8,128)}, f32[256,256]{1,0:T(8,128)}, u32[]{:S(2)}, u32[]{:S(2)}) collective-permute-start(f32[256,256]{1,0:T(8,128)} %get-tuple-element.49), channel_id=1, source_target_pairs={{0,8},{1,9},{32,40},{33,41},{64,72},{65,73},{96,104},{97,105},{128... | collective-permute-start | bytes 786440 | tf_op jit(solution)/shard_map/panel_scatter/ppermute | solution.py:54
  10.2 2.7 %collective-permute-start.2 = (f32[256,256]{1,0:T(8,128)S(1)}, f32[256,256]{1,0:T(8,128)}, u32[]{:S(2)}, u32[]{:S(2)}) collective-permute-start(f32[256,256]{1,0:T(8,128)S(1)} %get-tuple-element.48), channel_id=1, source_target_pairs={{0,12},{1,13},{32,44},{33,45},{64,76},{65,77},{96,108},{97,109},{1... | collective-permute-start | bytes 786440 | tf_op jit(solution)/shard_map/panel_scatter/ppermute | solution.py:54
  12.9 3.9 %collective-permute-start.3 = (f32[256,256]{1,0:T(8,128)S(1)}, f32[256,256]{1,0:T(8,128)}, u32[]{:S(2)}, u32[]{:S(2)}) collective-permute-start(f32[256,256]{1,0:T(8,128)S(1)} %get-tuple-element.47), channel_id=1, source_target_pairs={{0,16},{1,17},{32,48},{33,49},{64,80},{65,81},{96,112},{97,113},{1... | collective-permute-start | bytes 786440 | tf_op jit(solution)/shard_map/panel_scatter/ppermute | solution.py:54
  16.9 2.0 %collective-permute-start.4 = (f32[256,256]{1,0:T(8,128)S(1)}, f32[256,256]{1,0:T(8,128)}, u32[]{:S(2)}, u32[]{:S(2)}) collective-permute-start(f32[256,256]{1,0:T(8,128)S(1)} %get-tuple-element.46), channel_id=1, source_target_pairs={{0,20},{1,21},{32,52},{33,53},{64,84},{65,85},{96,116},{97,117},{1... | collective-permute-start | bytes 786440 | tf_op jit(solution)/shard_map/panel_scatter/ppermute | solution.py:54
  19.1 4.2 %gather_fusion = f32[512,512]{1,0:T(8,128)S(1)} fusion(f32[2048,512]{1,0:T(8,128)} %rest_9_.1, s32[1024]{0:T(1024)S(1)} %pad_clamp_fusion), kind=kCustom, calls=%fused_computation | custom fusion | bytes 2099200 | tf_op jit(solution)/shard_map/top_exchange/gather | solution.py:226
  23.5 2.0 %collective-permute-start.5 = (f32[256,256]{1,0:T(8,128)S(1)}, f32[256,256]{1,0:T(8,128)}, u32[]{:S(2)}, u32[]{:S(2)}) collective-permute-start(f32[256,256]{1,0:T(8,128)S(1)} %get-tuple-element.45), channel_id=1, source_target_pairs={{0,24},{1,25},{32,56},{33,57},{64,88},{65,89},{96,120},{97,121},{1... | collective-permute-start | bytes 786440 | tf_op jit(solution)/shard_map/panel_scatter/ppermute | solution.py:54
  25.6 2.0 %collective-permute-start.6 = (f32[256,256]{1,0:T(8,128)S(1)}, f32[256,256]{1,0:T(8,128)}, u32[]{:S(2)}, u32[]{:S(2)}) collective-permute-start(f32[256,256]{1,0:T(8,128)S(1)} %get-tuple-element.44), channel_id=1, source_target_pairs={{0,28},{1,29},{32,60},{33,61},{64,92},{65,93},{96,124},{97,125},{1... | collective-permute-start | bytes 786440 | tf_op jit(solution)/shard_map/panel_scatter/ppermute | solution.py:54
  27.6 1.0 collective-permute-start.7
  28.7 1.1 constant_dynamic-slice_fusion.4
  29.8 5.6 %collective-permute-done.6 = f32[256,256]{1,0:T(8,128)} collective-permute-done((f32[256,256]{1,0:T(8,128)S(1)}, f32[256,256]{1,0:T(8,128)}, u32[]{:S(2)}, u32[]{:S(2)}) %collective-permute-start.6) | collective-permute-done | bytes 262176 | tf_op jit(solution)/shard_map/panel_scatter/ppermute | solution.py:54
  35.4 1.1 select_select_fusion.2
  36.7 1.4 %collective-permute-start.11 = (f32[128,512]{1,0:T(8,128)S(1)}, f32[128,512]{1,0:T(8,128)S(1)}, u32[]{:S(2)}, u32[]{:S(2)}) collective-permute-start(f32[128,512]{1,0:T(8,128)S(1)} %pad_maximum_fusion.4), channel_id=1, source_target_pairs={{0,64},{32,96},{64,128},{96,160},{128,192},{160,224},{192,0},{224,... | collective-permute-start | bytes 786440 | tf_op jit(solution)/shard_map/top_exchange/ppermute | solution.py:241
  38.1 2.7 %collective-permute-start.12 = (f32[128,512]{1,0:T(8,128)S(1)}, f32[128,512]{1,0:T(8,128)S(1)}, u32[]{:S(2)}, u32[]{:S(2)}) collective-permute-start(f32[128,512]{1,0:T(8,128)S(1)} %pad_maximum_fusion.5), channel_id=1, source_target_pairs={{0,128},{32,160},{64,192},{96,224},{128,0},{160,32},{192,64},{224,... | collective-permute-start | bytes 786440 | tf_op jit(solution)/shard_map/top_exchange/ppermute | solution.py:241
  40.8 1.1 collective-permute-start.13
  42.0 1.9 %collective-permute-start.10 = (f32[256,256]{1,0:T(8,128)S(1)}, f32[256,256]{1,0:T(8,128)S(1)}, u32[]{:S(2)}, u32[]{:S(2)}) collective-permute-start(f32[256,256]{1,0:T(8,128)S(1)} %select_select_fusion.2), channel_id=1, source_target_pairs={{0,3},{4,7},{8,11},{12,15},{16,19},{20,23},{24,27},{28,31},{1,0},{... | collective-permute-start | bytes 786440 | tf_op jit(solution)/shard_map/panel_across/ppermute | solution.py:80
  43.9 3.4 %collective-permute-start.8 = (f32[256,256]{1,0:T(8,128)S(1)}, f32[256,256]{1,0:T(8,128)S(1)}, u32[]{:S(2)}, u32[]{:S(2)}) collective-permute-start(f32[256,256]{1,0:T(8,128)S(1)} %select_select_fusion.2), channel_id=1, source_target_pairs={{0,1},{4,5},{8,9},{12,13},{16,17},{20,21},{24,25},{28,29},{1,2},{5... | collective-permute-start | bytes 786440 | tf_op jit(solution)/shard_map/panel_across/ppermute | solution.py:79
  47.3 1.3 %collective-permute-start.9 = (f32[256,256]{1,0:T(8,128)S(1)}, f32[256,256]{1,0:T(8,128)S(1)}, u32[]{:S(2)}, u32[]{:S(2)}) collective-permute-start(f32[256,256]{1,0:T(8,128)S(1)} %select_select_fusion.2), channel_id=1, source_target_pairs={{0,2},{4,6},{8,10},{12,14},{16,18},{20,22},{24,26},{28,30},{1,3},{... | collective-permute-start | bytes 786440 | tf_op jit(solution)/shard_map/panel_across/ppermute | solution.py:81
  48.6 2.5 %collective-permute-done.12 = f32[128,512]{1,0:T(8,128)S(1)} collective-permute-done((f32[128,512]{1,0:T(8,128)S(1)}, f32[128,512]{1,0:T(8,128)S(1)}, u32[]{:S(2)}, u32[]{:S(2)}) %collective-permute-start.12) | collective-permute-done | bytes 262176 | tf_op jit(solution)/shard_map/top_exchange/ppermute | solution.py:241
  51.1 1.0 fusion.16
  52.1 1.7 %collective-permute-start.14 = (f32[128,256]{1,0:T(8,128)S(1)}, f32[128,256]{1,0:T(8,128)S(1)}, u32[]{:S(2)}, u32[]{:S(2)}) collective-permute-start(f32[128,256]{1,0:T(8,128)S(1)} %fusion.14), channel_id=1, source_target_pairs={{0,16},{1,17},{32,48},{33,49},{64,80},{65,81},{96,112},{97,113},{1... | collective-permute-start | bytes 393224 | tf_op jit(solution)/shard_map/fix_half/ppermute | solution.py:59
  53.8 2.0 %collective-permute-done.9 = f32[256,256]{1,0:T(8,128)S(1)} collective-permute-done((f32[256,256]{1,0:T(8,128)S(1)}, f32[256,256]{1,0:T(8,128)S(1)}, u32[]{:S(2)}, u32[]{:S(2)}) %collective-permute-start.9) | collective-permute-done | bytes 262176 | tf_op jit(solution)/shard_map/panel_across/ppermute | solution.py:81
  56.0 1.3 %collective-permute-start.15 = (f32[128,256]{1,0:T(8,128)S(1)}, f32[128,256]{1,0:T(8,128)S(1)}, u32[]{:S(2)}, u32[]{:S(2)}) collective-permute-start(f32[128,256]{1,0:T(8,128)S(1)} %broadcast_select_fusion.1), channel_id=1, source_target_pairs={{0,4},{1,5},{16,12},{17,13},{32,36},{33,37},{48,44},{49,45},{64,68... | collective-permute-start | bytes 393224 | tf_op jit(solution)/shard_map/fix_down/ppermute | solution.py:59
  57.3 1.3 %collective-permute-start.16 = (f32[128,256]{1,0:T(8,128)S(1)}, f32[128,256]{1,0:T(8,128)S(1)}, u32[]{:S(2)}, u32[]{:S(2)}) collective-permute-start(f32[128,256]{1,0:T(8,128)S(1)} %broadcast_select_fusion.1), channel_id=1, source_target_pairs={{0,8},{1,9},{16,24},{17,25},{32,40},{33,41},{48,56},{49,57},{64,72... | collective-permute-start | bytes 393224 | tf_op jit(solution)/shard_map/fix_down/ppermute | solution.py:59
  58.6 4.9 %collective-permute-start.17 = (f32[128,256]{1,0:T(8,128)S(1)}, f32[128,256]{1,0:T(8,128)}, u32[]{:S(2)}, u32[]{:S(2)}) collective-permute-start(f32[128,256]{1,0:T(8,128)S(1)} %broadcast_select_fusion.1), channel_id=1, source_target_pairs={{0,28},{1,29},{16,20},{17,21},{32,60},{33,61},{48,52},{49,53},{64,... | collective-permute-start | bytes 393224 | tf_op jit(solution)/shard_map/fix_down/ppermute | solution.py:59
  63.5 2.7 %collective-permute-start.28 = (f32[256,512]{1,0:T(8,128)S(1)}, f32[256,512]{1,0:T(8,128)S(1)}, u32[]{:S(2)}, u32[]{:S(2)}) collective-permute-start(f32[256,512]{1,0:T(8,128)S(1)} %pad_maximum_fusion.2.rest_0_), channel_id=1, source_target_pairs={{0,28},{1,29},{2,30},{3,31},{4,0},{5,1},{6,2},{7,3},{8,4},{9,5},{1... | collective-permute-start | bytes 1572872 | tf_op jit(solution)/shard_map/panel_ring/ppermute | solution.py:250
  66.4 1.6 %select_reduce_fusion = (s32[2048]{0:T(1024)S(1)}, s32[2048]{0:T(1024)S(1)}) fusion(s32[256]{0:T(256)} %copy-done.3, s32[256]{0:T(256)S(1)} %bitcast.38, s32[2048]{0:T(1024)S(1)} %fusion.26, s32[256]{0:T(256)S(1)} %fusion.33, s32[256]{0:T(256)S(1)} %bitcast.40), kind=kLoop, calls=%fused_computation.2 | loop fusion | flops 3141632 | bytes 28672 | tf_op jit(solution)/shard_map/reduce_sum | solution.py:218
  68.4 1.4 %copy.8 = s32[2048,1]{1,0:T(8,128)} copy(s32[2048,1]{0,1:T(1,128)S(1)} %bitcast.30) | data formatting | bytes 16384 | tf_op jit(solution)/shard_map/reduce_sum | solution.py:217
  70.2 1.1 collective-permute-start.23
  71.3 1.4 %collective-permute-start.24 = (f32[128,512]{1,0:T(8,128)S(1)}, f32[128,512]{1,0:T(8,128)S(1)}, u32[]{:S(2)}, u32[]{:S(2)}) collective-permute-start(f32[128,512]{1,0:T(8,128)S(1)} %get-tuple-element.61), channel_id=1, source_target_pairs={{0,192},{32,224},{64,0},{96,32},{128,64},{160,96},{192,128},{224,1... | collective-permute-start | bytes 786440 | tf_op jit(solution)/shard_map/top_gather/ppermute | solution.py:88
  72.7 1.6 %collective-permute-done.18.rest_1_ = f32[256,512]{1,0:T(8,128)S(1)} collective-permute-done((f32[256,512]{1,0:T(8,128)S(1)}, f32[256,512]{1,0:T(8,128)S(1)}, u32[]{:S(2)}, u32[]{:S(2)}) %collective-permute-start.18) | collective-permute-done | bytes 524320 | tf_op jit(solution)/shard_map/panel_ring/ppermute | solution.py:249
  74.5 1.6 %collective-permute-done.28.rest_2_ = f32[256,512]{1,0:T(8,128)S(1)} collective-permute-done((f32[256,512]{1,0:T(8,128)S(1)}, f32[256,512]{1,0:T(8,128)S(1)}, u32[]{:S(2)}, u32[]{:S(2)}) %collective-permute-start.28) | collective-permute-done | bytes 524320 | tf_op jit(solution)/shard_map/panel_ring/ppermute | solution.py:250
  76.1 3.4 %collective-permute-start.29 = (f32[256,512]{1,0:T(8,128)S(1)}, f32[256,512]{1,0:T(8,128)S(1)}, u32[]{:S(2)}, u32[]{:S(2)}) collective-permute-start(f32[256,512]{1,0:T(8,128)S(1)} %collective-permute-done.28.rest_2_), channel_id=1, source_target_pairs={{0,28},{1,29},{2,30},{3,31},{4,0},{5,1},{6,2},{7,3},{8,4},{9,5},{1... | collective-permute-start | bytes 1572872 | tf_op jit(solution)/shard_map/panel_ring/ppermute | solution.py:250
  79.5 1.6 %fusion.13.origin = s32[2048,1]{1,0:T(8,128)S(1)} fusion(s32[2048,1]{1,0:T(8,128)} %copy.8, s32[2048,1]{1,0:T(8,128)S(1)} %copy.10, s32[]{:T(128)} %axis_index.23), kind=kLoop, calls=%fused_computation.21 | loop fusion | flops 43008 | bytes 24580 | tf_op jit(solution)/shard_map/sub | solution.py:219
  82.1 1.3 %collective-permute-start.19 = (f32[128,256]{1,0:T(8,128)S(1)}, f32[128,256]{1,0:T(8,128)S(1)}, u32[]{:S(2)}, u32[]{:S(2)}) collective-permute-start(f32[128,256]{1,0:T(8,128)S(1)} %select_select_fusion.5), channel_id=1, source_target_pairs={{0,1},{4,5},{8,9},{12,13},{16,17},{20,21},{24,25},{28,29},{1,2},{5... | collective-permute-start | bytes 393224 | tf_op jit(solution)/shard_map/fix_across/ppermute | solution.py:79
  83.4 1.3 %collective-permute-start.20 = (f32[128,256]{1,0:T(8,128)S(1)}, f32[128,256]{1,0:T(8,128)S(1)}, u32[]{:S(2)}, u32[]{:S(2)}) collective-permute-start(f32[128,256]{1,0:T(8,128)S(1)} %select_select_fusion.5), channel_id=1, source_target_pairs={{0,2},{4,6},{8,10},{12,14},{16,18},{20,22},{24,26},{28,30},{1,3},{... | collective-permute-start | bytes 393224 | tf_op jit(solution)/shard_map/fix_across/ppermute | solution.py:81
  84.7 1.9 %collective-permute-start.21 = (f32[128,256]{1,0:T(8,128)S(1)}, f32[128,256]{1,0:T(8,128)S(1)}, u32[]{:S(2)}, u32[]{:S(2)}) collective-permute-start(f32[128,256]{1,0:T(8,128)S(1)} %select_select_fusion.5), channel_id=1, source_target_pairs={{0,3},{4,7},{8,11},{12,15},{16,19},{20,23},{24,27},{28,31},{1,0},{... | collective-permute-start | bytes 393224 | tf_op jit(solution)/shard_map/fix_across/ppermute | solution.py:80
  87.1 3.4 %collective-permute-start.30 = (f32[256,512]{1,0:T(8,128)S(1)}, f32[256,512]{1,0:T(8,128)S(1)}, u32[]{:S(2)}, u32[]{:S(2)}) collective-permute-start(f32[256,512]{1,0:T(8,128)S(1)} %collective-permute-done.29.rest_4_), channel_id=1, source_target_pairs={{0,28},{1,29},{2,30},{3,31},{4,0},{5,1},{6,2},{7,3},{8,4},{9,5},{1... | collective-permute-start | bytes 1572872 | tf_op jit(solution)/shard_map/panel_ring/ppermute | solution.py:250
  90.6 3.2 %collective-permute-start.31 = (f32[128,512]{1,0:T(8,128)S(1)}, f32[128,512]{1,0:T(8,128)S(1)}, u32[]{:S(2)}, u32[]{:S(2)}) collective-permute-start(f32[128,512]{1,0:T(8,128)S(1)} %pad_maximum_fusion.7), channel_id=1, source_target_pairs={{0,64},{32,96},{64,128},{96,160},{128,192},{160,224},{192,0},{224,... | collective-permute-start | bytes 786440 | tf_op jit(solution)/shard_map/fix_gather/ppermute | solution.py:88
  93.8 1.0 collective-permute-start.32
  94.8 1.5 %collective-permute-start.33 = (f32[128,512]{1,0:T(8,128)S(1)}, f32[128,512]{1,0:T(8,128)S(1)}, u32[]{:S(2)}, u32[]{:S(2)}) collective-permute-start(f32[128,512]{1,0:T(8,128)S(1)} %pad_maximum_fusion.7), channel_id=1, source_target_pairs={{0,192},{32,224},{64,0},{96,32},{128,64},{160,96},{192,128},{224,1... | collective-permute-start | bytes 786440 | tf_op jit(solution)/shard_map/fix_gather/ppermute | solution.py:88
  96.3 1.4 %collective-permute-done.31 = f32[128,512]{1,0:T(8,128)S(1)} collective-permute-done((f32[128,512]{1,0:T(8,128)S(1)}, f32[128,512]{1,0:T(8,128)S(1)}, u32[]{:S(2)}, u32[]{:S(2)}) %collective-permute-start.31) | collective-permute-done | bytes 262176 | tf_op jit(solution)/shard_map/fix_gather/ppermute | solution.py:88
  97.6 10.5 %collective-permute-start.26 = (f32[4,128,512]{2,1,0:T(8,128)S(1)}, f32[4,128,512]{2,1,0:T(8,128)S(1)}, u32[]{:S(2)}, u32[]{:S(2)}) collective-permute-start(f32[4,128,512]{2,1,0:T(8,128)S(1)} %pad_maximum_fusion.top_mine), channel_id=1, source_target_pairs={{0,32},{32,0},{64,96},{96,64},{128,160},{160,128},{192,224},{224,1... | collective-permute-start | bytes 3145736 | tf_op jit(solution)/shard_map/core_gather/ppermute | solution.py:275
  108.5 3.0 %collective-permute-start.36 = (f32[128,512]{1,0:T(8,128)S(1)}, f32[128,512]{1,0:T(8,128)S(1)}, u32[]{:S(2)}, u32[]{:S(2)}) collective-permute-start(f32[128,512]{1,0:T(8,128)S(1)} %slice.89), channel_id=1, source_target_pairs={{0,28},{1,29},{2,30},{3,31},{4,0},{5,1},{6,2},{7,3},{8,4},{9,5},{1... | collective-permute-start | bytes 786440 | tf_op jit(solution)/shard_map/panel_ring/ppermute | solution.py:250
  111.9 4.1 %factor.1 = (bf16[512,512]{1,0:T(8,128)(2,1)S(1)}, bf16[512,512]{1,0:T(8,128)(2,1)S(1)}, bf16[512,512]{1,0:T(8,128)(2,1)S(1)}, bf16[512,512]{1,0:T(8,128)(2,1)S(1)}, f32[256,512]{1,0:T(8,128)S(1)}) custom-call(s32[4]{0:T(128)S(1)} %pad_add_fusion.2.ids, f32[4,128,512]{2,1,0:T(8,128)S(1)} %pad_maximum_fusion.top_mine, ...), custom_call_target="tpu_custom_call" | custom-call | flops 3000000000 | bytes 8388608 | tf_op jit(solution)/shard_map/factor/pallas_call | solution.py:285
  116.0 1.1 collective-permute-done.35.rest_7_
  117.1 7.6 %update.1 = f32[2048,512]{1,0:T(8,128)} custom-call(s32[4]{0:T(128)S(1)} %pad_add_fusion.2.ids, s32[2048,1]{1,0:T(8,128)S(1)} %fusion.13.origin, bf16[512,512]{1,0:T(8,128)(2,1)S(1)} %get-tuple-element.32.factor_high, bf16[512,512]{1,0:T(8,128)(2,1)S(1)} %get-tuple-element.33.factor_low, bf16[512,512]{1,0:T(8,128)(2,1)S(1)} %get-tuple-element.34.moved_high, ...), custom_call_target="tpu_custom_call" | custom-call | flops 6000000000 | bytes 14680064 | tf_op jit(solution)/shard_map/update/pallas_call | solution.py:297
  (78 shorter events, 4.3 us)
Async XLA Ops:
  0.0 18.9 %copy-start.4 = (s32[2,256]{1,0:T(2,128)S(1)}, s32[2,256]{1,0:T(2,128)}, u32[]{:S(2)}) copy-start(s32[2,256]{1,0:T(2,128)} %param.5) | copy-start | bytes 6148
  2.4 21.1 %collective-permute-start = (f32[256,256]{1,0:T(8,128)}, f32[256,256]{1,0:T(8,128)}, u32[]{:S(2)}, u32[]{:S(2)}) collective-permute-start(f32[256,256]{1,0:T(8,128)} %get-tuple-element.50), channel_id=1, source_target_pairs={{0,4},{1,5},{32,36},{33,37},{64,68},{65,69},{96,100},{97,101},{128... | collective-permute-start | bytes 786440 | tf_op jit(solution)/shard_map/panel_scatter/ppermute | solution.py:54
  7.5 18.1 %collective-permute-start.1 = (f32[256,256]{1,0:T(8,128)}, f32[256,256]{1,0:T(8,128)}, u32[]{:S(2)}, u32[]{:S(2)}) collective-permute-start(f32[256,256]{1,0:T(8,128)} %get-tuple-element.49), channel_id=1, source_target_pairs={{0,8},{1,9},{32,40},{33,41},{64,72},{65,73},{96,104},{97,105},{128... | collective-permute-start | bytes 786440 | tf_op jit(solution)/shard_map/panel_scatter/ppermute | solution.py:54
  10.2 17.4 %collective-permute-start.2 = (f32[256,256]{1,0:T(8,128)S(1)}, f32[256,256]{1,0:T(8,128)}, u32[]{:S(2)}, u32[]{:S(2)}) collective-permute-start(f32[256,256]{1,0:T(8,128)S(1)} %get-tuple-element.48), channel_id=1, source_target_pairs={{0,12},{1,13},{32,44},{33,45},{64,76},{65,77},{96,108},{97,109},{1... | collective-permute-start | bytes 786440 | tf_op jit(solution)/shard_map/panel_scatter/ppermute | solution.py:54
  12.9 16.8 %collective-permute-start.3 = (f32[256,256]{1,0:T(8,128)S(1)}, f32[256,256]{1,0:T(8,128)}, u32[]{:S(2)}, u32[]{:S(2)}) collective-permute-start(f32[256,256]{1,0:T(8,128)S(1)} %get-tuple-element.47), channel_id=1, source_target_pairs={{0,16},{1,17},{32,48},{33,49},{64,80},{65,81},{96,112},{97,113},{1... | collective-permute-start | bytes 786440 | tf_op jit(solution)/shard_map/panel_scatter/ppermute | solution.py:54
  16.9 12.9 %collective-permute-start.4 = (f32[256,256]{1,0:T(8,128)S(1)}, f32[256,256]{1,0:T(8,128)}, u32[]{:S(2)}, u32[]{:S(2)}) collective-permute-start(f32[256,256]{1,0:T(8,128)S(1)} %get-tuple-element.46), channel_id=1, source_target_pairs={{0,20},{1,21},{32,52},{33,53},{64,84},{65,85},{96,116},{97,117},{1... | collective-permute-start | bytes 786440 | tf_op jit(solution)/shard_map/panel_scatter/ppermute | solution.py:54
  18.9 47.4 %copy-start.3 = (s32[256]{0:T(256)}, s32[256]{0:T(256)S(1)}, u32[]{:S(2)}) copy-start(s32[256]{0:T(256)S(1)} %get-tuple-element.68) | copy-start | bytes 3076
  23.5 6.3 %collective-permute-start.5 = (f32[256,256]{1,0:T(8,128)S(1)}, f32[256,256]{1,0:T(8,128)}, u32[]{:S(2)}, u32[]{:S(2)}) collective-permute-start(f32[256,256]{1,0:T(8,128)S(1)} %get-tuple-element.45), channel_id=1, source_target_pairs={{0,24},{1,25},{32,56},{33,57},{64,88},{65,89},{96,120},{97,121},{1... | collective-permute-start | bytes 786440 | tf_op jit(solution)/shard_map/panel_scatter/ppermute | solution.py:54
  25.6 9.8 %collective-permute-start.6 = (f32[256,256]{1,0:T(8,128)S(1)}, f32[256,256]{1,0:T(8,128)}, u32[]{:S(2)}, u32[]{:S(2)}) collective-permute-start(f32[256,256]{1,0:T(8,128)S(1)} %get-tuple-element.44), channel_id=1, source_target_pairs={{0,28},{1,29},{32,60},{33,61},{64,92},{65,93},{96,124},{97,125},{1... | collective-permute-start | bytes 786440 | tf_op jit(solution)/shard_map/panel_scatter/ppermute | solution.py:54
  27.6 8.9 %collective-permute-start.7 = (f32[256,512]{1,0:T(8,128)S(1)}, f32[256,512]{1,0:T(8,128)S(1)}, u32[]{:S(2)}, u32[]{:S(2)}) collective-permute-start(f32[256,512]{1,0:T(8,128)S(1)} %constant_dynamic-slice_fusion.6), channel_id=1, source_target_pairs={{0,32},{32,0},{64,96},{96,64},{128,160},{160,128},{192,224},{224,1... | collective-permute-start | bytes 1572872 | tf_op jit(solution)/shard_map/top_exchange/ppermute | solution.py:229
  36.7 10.6 %collective-permute-start.11 = (f32[128,512]{1,0:T(8,128)S(1)}, f32[128,512]{1,0:T(8,128)S(1)}, u32[]{:S(2)}, u32[]{:S(2)}) collective-permute-start(f32[128,512]{1,0:T(8,128)S(1)} %pad_maximum_fusion.4), channel_id=1, source_target_pairs={{0,64},{32,96},{64,128},{96,160},{128,192},{160,224},{192,0},{224,... | collective-permute-start | bytes 786440 | tf_op jit(solution)/shard_map/top_exchange/ppermute | solution.py:241
  38.1 13.0 %collective-permute-start.12 = (f32[128,512]{1,0:T(8,128)S(1)}, f32[128,512]{1,0:T(8,128)S(1)}, u32[]{:S(2)}, u32[]{:S(2)}) collective-permute-start(f32[128,512]{1,0:T(8,128)S(1)} %pad_maximum_fusion.5), channel_id=1, source_target_pairs={{0,128},{32,160},{64,192},{96,224},{128,0},{160,32},{192,64},{224,... | collective-permute-start | bytes 786440 | tf_op jit(solution)/shard_map/top_exchange/ppermute | solution.py:241
  40.8 10.3 %collective-permute-start.13 = (f32[128,512]{1,0:T(8,128)S(1)}, f32[128,512]{1,0:T(8,128)S(1)}, u32[]{:S(2)}, u32[]{:S(2)}) collective-permute-start(f32[128,512]{1,0:T(8,128)S(1)} %pad_maximum_fusion.6), channel_id=1, source_target_pairs={{0,192},{32,224},{64,0},{96,32},{128,64},{160,96},{192,128},{224,1... | collective-permute-start | bytes 786440 | tf_op jit(solution)/shard_map/top_exchange/ppermute | solution.py:241
  42.0 11.8 %collective-permute-start.10 = (f32[256,256]{1,0:T(8,128)S(1)}, f32[256,256]{1,0:T(8,128)S(1)}, u32[]{:S(2)}, u32[]{:S(2)}) collective-permute-start(f32[256,256]{1,0:T(8,128)S(1)} %select_select_fusion.2), channel_id=1, source_target_pairs={{0,3},{4,7},{8,11},{12,15},{16,19},{20,23},{24,27},{28,31},{1,0},{... | collective-permute-start | bytes 786440 | tf_op jit(solution)/shard_map/panel_across/ppermute | solution.py:80
  43.9 9.9 %collective-permute-start.8 = (f32[256,256]{1,0:T(8,128)S(1)}, f32[256,256]{1,0:T(8,128)S(1)}, u32[]{:S(2)}, u32[]{:S(2)}) collective-permute-start(f32[256,256]{1,0:T(8,128)S(1)} %select_select_fusion.2), channel_id=1, source_target_pairs={{0,1},{4,5},{8,9},{12,13},{16,17},{20,21},{24,25},{28,29},{1,2},{5... | collective-permute-start | bytes 786440 | tf_op jit(solution)/shard_map/panel_across/ppermute | solution.py:79
  47.3 8.5 %collective-permute-start.9 = (f32[256,256]{1,0:T(8,128)S(1)}, f32[256,256]{1,0:T(8,128)S(1)}, u32[]{:S(2)}, u32[]{:S(2)}) collective-permute-start(f32[256,256]{1,0:T(8,128)S(1)} %select_select_fusion.2), channel_id=1, source_target_pairs={{0,2},{4,6},{8,10},{12,14},{16,18},{20,22},{24,26},{28,30},{1,3},{... | collective-permute-start | bytes 786440 | tf_op jit(solution)/shard_map/panel_across/ppermute | solution.py:81
  52.1 3.9 %collective-permute-start.14 = (f32[128,256]{1,0:T(8,128)S(1)}, f32[128,256]{1,0:T(8,128)S(1)}, u32[]{:S(2)}, u32[]{:S(2)}) collective-permute-start(f32[128,256]{1,0:T(8,128)S(1)} %fusion.14), channel_id=1, source_target_pairs={{0,16},{1,17},{32,48},{33,49},{64,80},{65,81},{96,112},{97,113},{1... | collective-permute-start | bytes 393224 | tf_op jit(solution)/shard_map/fix_half/ppermute | solution.py:59
  56.0 13.7 %collective-permute-start.15 = (f32[128,256]{1,0:T(8,128)S(1)}, f32[128,256]{1,0:T(8,128)S(1)}, u32[]{:S(2)}, u32[]{:S(2)}) collective-permute-start(f32[128,256]{1,0:T(8,128)S(1)} %broadcast_select_fusion.1), channel_id=1, source_target_pairs={{0,4},{1,5},{16,12},{17,13},{32,36},{33,37},{48,44},{49,45},{64,68... | collective-permute-start | bytes 393224 | tf_op jit(solution)/shard_map/fix_down/ppermute | solution.py:59
  57.3 12.8 %collective-permute-start.16 = (f32[128,256]{1,0:T(8,128)S(1)}, f32[128,256]{1,0:T(8,128)S(1)}, u32[]{:S(2)}, u32[]{:S(2)}) collective-permute-start(f32[128,256]{1,0:T(8,128)S(1)} %broadcast_select_fusion.1), channel_id=1, source_target_pairs={{0,8},{1,9},{16,24},{17,25},{32,40},{33,41},{48,56},{49,57},{64,72... | collective-permute-start | bytes 393224 | tf_op jit(solution)/shard_map/fix_down/ppermute | solution.py:59
  58.6 12.7 %collective-permute-start.17 = (f32[128,256]{1,0:T(8,128)S(1)}, f32[128,256]{1,0:T(8,128)}, u32[]{:S(2)}, u32[]{:S(2)}) collective-permute-start(f32[128,256]{1,0:T(8,128)S(1)} %broadcast_select_fusion.1), channel_id=1, source_target_pairs={{0,28},{1,29},{16,20},{17,21},{32,60},{33,61},{48,52},{49,53},{64,... | collective-permute-start | bytes 393224 | tf_op jit(solution)/shard_map/fix_down/ppermute | solution.py:59
  63.5 10.8 %collective-permute-start.18 = (f32[256,512]{1,0:T(8,128)S(1)}, f32[256,512]{1,0:T(8,128)S(1)}, u32[]{:S(2)}, u32[]{:S(2)}) collective-permute-start(f32[256,512]{1,0:T(8,128)S(1)} %pad_maximum_fusion.2.rest_0_), channel_id=1, source_target_pairs={{0,4},{1,5},{2,6},{3,7},{4,8},{5,9},{6,10},{7,11},{8,12},{9,13},{1... | collective-permute-start | bytes 1572872 | tf_op jit(solution)/shard_map/panel_ring/ppermute | solution.py:249
  63.5 12.6 %collective-permute-start.28 = (f32[256,512]{1,0:T(8,128)S(1)}, f32[256,512]{1,0:T(8,128)S(1)}, u32[]{:S(2)}, u32[]{:S(2)}) collective-permute-start(f32[256,512]{1,0:T(8,128)S(1)} %pad_maximum_fusion.2.rest_0_), channel_id=1, source_target_pairs={{0,28},{1,29},{2,30},{3,31},{4,0},{5,1},{6,2},{7,3},{8,4},{9,5},{1... | collective-permute-start | bytes 1572872 | tf_op jit(solution)/shard_map/panel_ring/ppermute | solution.py:250
  69.8 12.3 %collective-permute-start.22 = (f32[128,512]{1,0:T(8,128)S(1)}, f32[128,512]{1,0:T(8,128)S(1)}, u32[]{:S(2)}, u32[]{:S(2)}) collective-permute-start(f32[128,512]{1,0:T(8,128)S(1)} %get-tuple-element.61), channel_id=1, source_target_pairs={{0,64},{32,96},{64,128},{96,160},{128,192},{160,224},{192,0},{224,... | collective-permute-start | bytes 786440 | tf_op jit(solution)/shard_map/top_gather/ppermute | solution.py:88
  70.2 13.2 %collective-permute-start.23 = (f32[128,512]{1,0:T(8,128)S(1)}, f32[128,512]{1,0:T(8,128)S(1)}, u32[]{:S(2)}, u32[]{:S(2)}) collective-permute-start(f32[128,512]{1,0:T(8,128)S(1)} %get-tuple-element.61), channel_id=1, source_target_pairs={{0,128},{32,160},{64,192},{96,224},{128,0},{160,32},{192,64},{224,... | collective-permute-start | bytes 786440 | tf_op jit(solution)/shard_map/top_gather/ppermute | solution.py:88
  71.3 13.4 %collective-permute-start.24 = (f32[128,512]{1,0:T(8,128)S(1)}, f32[128,512]{1,0:T(8,128)S(1)}, u32[]{:S(2)}, u32[]{:S(2)}) collective-permute-start(f32[128,512]{1,0:T(8,128)S(1)} %get-tuple-element.61), channel_id=1, source_target_pairs={{0,192},{32,224},{64,0},{96,32},{128,64},{160,96},{192,128},{224,1... | collective-permute-start | bytes 786440 | tf_op jit(solution)/shard_map/top_gather/ppermute | solution.py:88
  74.3 12.5 %collective-permute-start.25 = (f32[256,512]{1,0:T(8,128)S(1)}, f32[256,512]{1,0:T(8,128)S(1)}, u32[]{:S(2)}, u32[]{:S(2)}) collective-permute-start(f32[256,512]{1,0:T(8,128)S(1)} %collective-permute-done.18.rest_1_), channel_id=1, source_target_pairs={{0,4},{1,5},{2,6},{3,7},{4,8},{5,9},{6,10},{7,11},{8,12},{9,13},{1... | collective-permute-start | bytes 1572872 | tf_op jit(solution)/shard_map/panel_ring/ppermute | solution.py:249
  76.1 11.0 %collective-permute-start.29 = (f32[256,512]{1,0:T(8,128)S(1)}, f32[256,512]{1,0:T(8,128)S(1)}, u32[]{:S(2)}, u32[]{:S(2)}) collective-permute-start(f32[256,512]{1,0:T(8,128)S(1)} %collective-permute-done.28.rest_2_), channel_id=1, source_target_pairs={{0,28},{1,29},{2,30},{3,31},{4,0},{5,1},{6,2},{7,3},{8,4},{9,5},{1... | collective-permute-start | bytes 1572872 | tf_op jit(solution)/shard_map/panel_ring/ppermute | solution.py:250
  82.1 8.4 %collective-permute-start.19 = (f32[128,256]{1,0:T(8,128)S(1)}, f32[128,256]{1,0:T(8,128)S(1)}, u32[]{:S(2)}, u32[]{:S(2)}) collective-permute-start(f32[128,256]{1,0:T(8,128)S(1)} %select_select_fusion.5), channel_id=1, source_target_pairs={{0,1},{4,5},{8,9},{12,13},{16,17},{20,21},{24,25},{28,29},{1,2},{5... | collective-permute-start | bytes 393224 | tf_op jit(solution)/shard_map/fix_across/ppermute | solution.py:79
  83.4 7.1 %collective-permute-start.20 = (f32[128,256]{1,0:T(8,128)S(1)}, f32[128,256]{1,0:T(8,128)S(1)}, u32[]{:S(2)}, u32[]{:S(2)}) collective-permute-start(f32[128,256]{1,0:T(8,128)S(1)} %select_select_fusion.5), channel_id=1, source_target_pairs={{0,2},{4,6},{8,10},{12,14},{16,18},{20,22},{24,26},{28,30},{1,3},{... | collective-permute-start | bytes 393224 | tf_op jit(solution)/shard_map/fix_across/ppermute | solution.py:81
  84.7 5.8 %collective-permute-start.21 = (f32[128,256]{1,0:T(8,128)S(1)}, f32[128,256]{1,0:T(8,128)S(1)}, u32[]{:S(2)}, u32[]{:S(2)}) collective-permute-start(f32[128,256]{1,0:T(8,128)S(1)} %select_select_fusion.5), channel_id=1, source_target_pairs={{0,3},{4,7},{8,11},{12,15},{16,19},{20,23},{24,27},{28,31},{1,0},{... | collective-permute-start | bytes 393224 | tf_op jit(solution)/shard_map/fix_across/ppermute | solution.py:80
  86.7 25.1 %copy-start.1 = (f32[2,256,256]{2,1,0:T(8,128)S(1)}, f32[2,256,256]{2,1,0:T(8,128)}, u32[]{:S(2)}) copy-start(f32[2,256,256]{2,1,0:T(8,128)} %lower_inverse.1) | copy-start | bytes 1572868
  86.8 25.1 %copy-start.2 = (f32[2,256,256]{2,1,0:T(8,128)S(1)}, f32[2,256,256]{2,1,0:T(8,128)}, u32[]{:S(2)}) copy-start(f32[2,256,256]{2,1,0:T(8,128)} %upper_inverse.1) | copy-start | bytes 1572868
  86.8 21.4 %collective-permute-start.27 = (f32[256,512]{1,0:T(8,128)S(1)}, f32[256,512]{1,0:T(8,128)S(1)}, u32[]{:S(2)}, u32[]{:S(2)}) collective-permute-start(f32[256,512]{1,0:T(8,128)S(1)} %collective-permute-done.25.rest_3_), channel_id=1, source_target_pairs={{0,4},{1,5},{2,6},{3,7},{4,8},{5,9},{6,10},{7,11},{8,12},{9,13},{1... | collective-permute-start | bytes 1572872 | tf_op jit(solution)/shard_map/panel_ring/ppermute | solution.py:249
  87.1 21.1 %collective-permute-start.30 = (f32[256,512]{1,0:T(8,128)S(1)}, f32[256,512]{1,0:T(8,128)S(1)}, u32[]{:S(2)}, u32[]{:S(2)}) collective-permute-start(f32[256,512]{1,0:T(8,128)S(1)} %collective-permute-done.29.rest_4_), channel_id=1, source_target_pairs={{0,28},{1,29},{2,30},{3,31},{4,0},{5,1},{6,2},{7,3},{8,4},{9,5},{1... | collective-permute-start | bytes 1572872 | tf_op jit(solution)/shard_map/panel_ring/ppermute | solution.py:250
  90.6 7.0 %collective-permute-start.31 = (f32[128,512]{1,0:T(8,128)S(1)}, f32[128,512]{1,0:T(8,128)S(1)}, u32[]{:S(2)}, u32[]{:S(2)}) collective-permute-start(f32[128,512]{1,0:T(8,128)S(1)} %pad_maximum_fusion.7), channel_id=1, source_target_pairs={{0,64},{32,96},{64,128},{96,160},{128,192},{160,224},{192,0},{224,... | collective-permute-start | bytes 786440 | tf_op jit(solution)/shard_map/fix_gather/ppermute | solution.py:88
  93.8 14.3 %collective-permute-start.32 = (f32[128,512]{1,0:T(8,128)S(1)}, f32[128,512]{1,0:T(8,128)S(1)}, u32[]{:S(2)}, u32[]{:S(2)}) collective-permute-start(f32[128,512]{1,0:T(8,128)S(1)} %pad_maximum_fusion.7), channel_id=1, source_target_pairs={{0,128},{32,160},{64,192},{96,224},{128,0},{160,32},{192,64},{224,... | collective-permute-start | bytes 786440 | tf_op jit(solution)/shard_map/fix_gather/ppermute | solution.py:88
  94.8 13.3 %collective-permute-start.33 = (f32[128,512]{1,0:T(8,128)S(1)}, f32[128,512]{1,0:T(8,128)S(1)}, u32[]{:S(2)}, u32[]{:S(2)}) collective-permute-start(f32[128,512]{1,0:T(8,128)S(1)} %pad_maximum_fusion.7), channel_id=1, source_target_pairs={{0,192},{32,224},{64,0},{96,32},{128,64},{160,96},{192,128},{224,1... | collective-permute-start | bytes 786440 | tf_op jit(solution)/shard_map/fix_gather/ppermute | solution.py:88
  97.6 13.9 %collective-permute-start.26 = (f32[4,128,512]{2,1,0:T(8,128)S(1)}, f32[4,128,512]{2,1,0:T(8,128)S(1)}, u32[]{:S(2)}, u32[]{:S(2)}) collective-permute-start(f32[4,128,512]{2,1,0:T(8,128)S(1)} %pad_maximum_fusion.top_mine), channel_id=1, source_target_pairs={{0,32},{32,0},{64,96},{96,64},{128,160},{160,128},{192,224},{224,1... | collective-permute-start | bytes 3145736 | tf_op jit(solution)/shard_map/core_gather/ppermute | solution.py:275
  108.2 3.7 %collective-permute-start.34 = (f32[4,128,512]{2,1,0:T(8,128)S(1)}, f32[4,128,512]{2,1,0:T(8,128)S(1)}, u32[]{:S(2)}, u32[]{:S(2)}) collective-permute-start(f32[4,128,512]{2,1,0:T(8,128)S(1)} %pad_maximum_fusion.1.fix_mine), channel_id=1, source_target_pairs={{0,32},{32,0},{64,96},{96,64},{128,160},{160,128},{192,224},{224,1... | collective-permute-start | bytes 3145736 | tf_op jit(solution)/shard_map/core_gather/ppermute | solution.py:276
  108.4 8.7 %collective-permute-start.35 = (f32[128,512]{1,0:T(8,128)S(1)}, f32[128,512]{1,0:T(8,128)S(1)}, u32[]{:S(2)}, u32[]{:S(2)}) collective-permute-start(f32[128,512]{1,0:T(8,128)S(1)} %slice.88), channel_id=1, source_target_pairs={{0,4},{1,5},{2,6},{3,7},{4,8},{5,9},{6,10},{7,11},{8,12},{9,13},{1... | collective-permute-start | bytes 786440 | tf_op jit(solution)/shard_map/panel_ring/ppermute | solution.py:249
  108.5 8.6 %copy-start = (f32[2048,512]{1,0:T(8,128)S(1)}, f32[2048,512]{1,0:T(8,128)}, u32[]{:S(2)}) copy-start(f32[2048,512]{1,0:T(8,128)} %rest_9_.1) | copy-start | bytes 12582916
  108.5 8.5 %collective-permute-start.36 = (f32[128,512]{1,0:T(8,128)S(1)}, f32[128,512]{1,0:T(8,128)S(1)}, u32[]{:S(2)}, u32[]{:S(2)}) collective-permute-start(f32[128,512]{1,0:T(8,128)S(1)} %slice.89), channel_id=1, source_target_pairs={{0,28},{1,29},{2,30},{3,31},{4,0},{5,1},{6,2},{7,3},{8,4},{9,5},{1... | collective-permute-start | bytes 786440 | tf_op jit(solution)/shard_map/panel_ring/ppermute | solution.py:250
